TPU v7x, 32 devices: a whole 2x2x4 slice. The times are simulated.
32 devices in a mesh: dp: 4 (over y, x), fsdp: 8 (over z, core).
Axes of the slice: x: 2, y: 2, z: 4, core: 2. Of those that a mesh axis runs over, the one named last changes fastest.
Arguments:
- signal: bfloat16 [2048, 1024], P(('dp', 'fsdp')), may hold values from -6 to 6
- grad_gated: bfloat16 [2048, 512], P(('dp', 'fsdp')), may hold values from -6 to 6
- conv_weight: bfloat16 [1024, 3072], P('fsdp'), may hold values from -0.109375 to 0.109375
- source_seg: int32 [32, 8], P(('dp', 'fsdp')), may hold values from -1 to 63, as said below
Outputs:
- gated_out: bfloat16 [2048, 512], P(('dp', 'fsdp'))
- grad_in: bfloat16 [2048, 1024], P(('dp', 'fsdp'))
- grad_weight: float32 [1024, 3072], P('fsdp')
Inputs may be any that keep to these rules, and one draw needn't show every extreme that they name: `source_seg`: -1 where a stream begins. The preceding segment holds the same position on its device as g on its own, no two segments of one device take their left context from the same device, and every segment precedes at most one segment.
All inputs are finite; a program needn't handle non-finite values.
Results may differ from a plain program's by a relative error of at most 0.0049.
Values may be sent and summed in bfloat16 or wider, within the bound.
No kernel may reach another device: no remote copies, remote signals or barrier semaphores. Data moves between devices by JAX's collectives and lax.ppermute only.
A program may use at most 64 MiB of HBM per device.

v0:
```python
import math

import jax
import jax.numpy as jnp
from jax import lax
from jax.sharding import PartitionSpec as P

C = 1024
H = 512
DILATION_SIZE = 4


def tap_starts(context_row_block):
    return [context_row_block - (2 - selected_index) * DILATION_SIZE for selected_index in range(3)]


def per_device(signal, grad_gated, conv_weight, source_seg):
    peer_count = lax.axis_size("fsdp")
    seg_count = source_seg.shape[1]
    row_count = signal.shape[0]
    seg_rows = row_count // seg_count
    context_row_block = 2 * DILATION_SIZE
    starts = tap_starts(context_row_block)
    segments = signal.reshape(seg_count, seg_rows, C)
    sources = source_seg[0]
    source_dev = jnp.where(sources >= 0, sources // seg_count, -1)
    peers = jnp.arange(peer_count, dtype=jnp.int32)
    request_mask = (source_dev[None, :] == peers[:, None]).astype(jnp.int32)
    asked = lax.all_to_all(request_mask, "fsdp", split_axis=0, concat_axis=0, tiled=True)
    send_table = asked.astype(jnp.bfloat16)
    recv_table = (source_dev[:, None] == peers[None, :]).astype(jnp.bfloat16)
    outgoing = jnp.einsum(
        "ns,slc->nlc", send_table, segments, preferred_element_type=jnp.float32
    ).astype(jnp.bfloat16)
    incoming = lax.all_to_all(outgoing, "fsdp", split_axis=0, concat_axis=0, tiled=True)
    carries = jnp.einsum(
        "sn,nlc->slc", recv_table, incoming, preferred_element_type=jnp.float32
    ).astype(jnp.bfloat16)
    extended = jnp.concatenate([carries, segments], axis=1)
    full_weight = lax.all_gather(conv_weight, "fsdp", axis=0, tiled=True)
    contract_final_axis = (((1,), (1,)), ((), ()))
    contract_first = (((0,), (0,)), ((), ()))
    windows = [extended[:, start : start + seg_rows, :].reshape(row_count, C) for start in starts]
    preact = sum(
        (
            lax.dot_general(
                windows[selected_index],
                full_weight[:, selected_index * C : (selected_index + 1) * C],
                contract_final_axis,
                preferred_element_type=jnp.float32,
            )
            for selected_index in range(3)
        )
    )
    filter_act = jnp.tanh(preact[:, :H])
    gate_act = jax.nn.sigmoid(preact[:, H:])
    gated_out = (filter_act * gate_act).astype(jnp.bfloat16)
    upstream_wide = grad_gated.astype(jnp.float32)
    grad_pre = jnp.concatenate(
        [
            upstream_wide * gate_act * (1.0 - filter_act * filter_act),
            upstream_wide * filter_act * gate_act * (1.0 - gate_act),
        ],
        axis=1,
    ).astype(jnp.bfloat16)
    partial_value = jnp.concatenate(
        [
            lax.dot_general(
                grad_pre,
                windows[selected_index],
                contract_first,
                preferred_element_type=jnp.float32,
            ).astype(jnp.bfloat16)
            for selected_index in range(3)
        ],
        axis=1,
    )
    arrived = lax.all_to_all(partial_value, "fsdp", split_axis=0, concat_axis=0, tiled=True)
    shard_sum = jnp.sum(arrived.reshape(peer_count, -1, 3 * C), axis=0, dtype=jnp.float32)
    group_total = lax.psum(shard_sum, "dp")
    total_token_count = row_count * peer_count * lax.axis_size("dp")
    grad_weight = group_total * (1.0 / math.sqrt(total_token_count))
    back_proj = jnp.dot(grad_pre, full_weight, preferred_element_type=jnp.float32)
    back_proj = back_proj.reshape(seg_count, seg_rows, 3 * C)
    grad_ext = jnp.zeros((seg_count, context_row_block + seg_rows, C), jnp.float32)
    for selected_index, start in enumerate(starts):
        grad_ext = grad_ext.at[:, start : start + seg_rows, :].add(
            back_proj[:, :, selected_index * C : (selected_index + 1) * C]
        )
    outgoing_grad = jnp.einsum(
        "sn,slc->nlc",
        recv_table.astype(jnp.float32),
        grad_ext[:, :context_row_block, :],
        precision=lax.Precision.HIGHEST,
    )
    incoming_grad = lax.all_to_all(outgoing_grad, "fsdp", split_axis=0, concat_axis=0, tiled=True)
    tail_grad = jnp.einsum(
        "ns,nlc->slc",
        send_table.astype(jnp.float32),
        incoming_grad,
        precision=lax.Precision.HIGHEST,
    )
    grad_in = (
        grad_ext[:, context_row_block:, :].at[:, seg_rows - context_row_block :, :].add(tail_grad)
    )
    grad_in = grad_in.reshape(row_count, C).astype(jnp.bfloat16)
    return (gated_out, grad_in, grad_weight)


def solution(mesh):
    placed = (
        P(("dp", "fsdp"), None),
        P(("dp", "fsdp"), None),
        P("fsdp", None),
        P(("dp", "fsdp"), None),
    )
    return jax.shard_map(
        per_device,
        mesh=mesh,
        in_specs=placed,
        out_specs=(P(("dp", "fsdp"), None), P(("dp", "fsdp"), None), P("fsdp", None)),
        check_vma=False,
    )
```

profile of v0, /device:TPU:0, one launch (start us, length us, event | category | flops | bytes accessed | tf_op | source)
XLA Modules:
  0.0 307.9 jit_solution(13101673594312532258)
XLA Ops:
  7.2 0.0 all-gather.2.cloned.1.call-start
  7.2 0.7 all-gather.2.cloned.1.call-update
  7.9 0.7 fusion.43
  8.6 11.7 %all_to_all.25 = s32[8,1,8]{2,1,0:T(1,128)S(1)} all-to-all(s32[8,1,8]{2,1,0:T(1,128)S(1)} %compare_convert_fusion), channel_id=1, replica_groups=mesh['dp'=4,'fsdp'=8] {'fsdp'}, dimensions={0} | all-to-all | bytes 512 | tf_op jit(solution)/shard_map/all_to_all | solution.py:29
  20.3 1.1 convolution_convert_fusion.3
  21.4 0.7 copy.21
  22.1 3.4 %all-to-all-start.1 = ((bf16[8,8,1024]{2,1,0:T(8,128)(2,1)}), bf16[8,8,1024]{2,1,0:T(8,128)(2,1)S(1)}, u32[]{:S(2)}, u32[]{:S(2)}) async-start(bf16[8,8,1024]{2,1,0:T(8,128)(2,1)} %copy.21), calls=%async_computation.1 | async-start | bytes 262144 | tf_op jit(solution)/shard_map/all_to_all | solution.py:35
  25.5 0.0 all-reduce.3.cloned.1.call-start
  25.5 1.0 copy.20
  26.5 0.7 compare_select_fusion.1
  27.2 8.6 %all-to-all-done.1 = bf16[8,8,1024]{2,1,0:T(8,128)(2,1)S(1)} async-done(((bf16[8,8,1024]{2,1,0:T(8,128)(2,1)}), bf16[8,8,1024]{2,1,0:T(8,128)(2,1)S(1)}, u32[]{:S(2)}, u32[]{:S(2)}) %all-to-all-start.1) | async-done | bytes 131104 | tf_op jit(solution)/shard_map/all_to_all | solution.py:35
  35.8 0.2 convolution_convert_fusion.4
  36.0 0.0 copy-start.1
  36.0 43.8 %all-gather.2.cloned.1.call-done = bf16[1024,3072]{1,0:T(8,128)(2,1)} async-done(((bf16[128,3072]{1,0:T(8,128)(2,1)}), bf16[1024,3072]{1,0:T(8,128)(2,1)}) %all-gather.2.cloned.1.call-update) | async-done | bytes 6291472 | tf_op jit(solution)/shard_map/all_gather | solution.py:40
  79.9 2.4 fusion
  82.3 2.4 fusion.2
  84.6 0.0 copy-start
  84.6 2.4 fusion.9
  87.0 0.0 copy-done.1
  87.0 0.7 fusion.18
  87.8 0.8 convolution_convert_fusion.2
  88.5 0.8 convolution_convert_fusion.1
  89.3 0.0 copy-done
  89.3 0.8 convolution_convert_fusion
  90.1 4.4 %copy_bitcast_fusion = bf16[8,128,3072]{1,2,0:T(8,128)(2,1)S(1)} fusion(bf16[1024,1024]{0,1:T(8,128)(2,1)S(1)} %convolution_convert_fusion, bf16[1024,1024]{0,1:T(8,128)(2,1)S(1)} %convolution_convert_fusion.1, bf16[1024,1024]{0,1:T(8,128)(2,1)S(1)} %convolution_convert_fusion.2), kind=kLoop, calls=%fused_computation.1 | loop fusion | flops 18874368 | bytes 12582912 | tf_op jit(solution)/shard_map/all_to_all | solution.py:78
  94.5 141.6 %all_to_all.26 = bf16[8,128,3072]{1,2,0:T(8,128)(2,1)S(1)} all-to-all(bf16[8,128,3072]{1,2,0:T(8,128)(2,1)S(1)} %copy_bitcast_fusion), channel_id=1, replica_groups=mesh['dp'=4,'fsdp'=8] {'fsdp'}, dimensions={0} | all-to-all | bytes 12582912 | tf_op jit(solution)/shard_map/all_to_all | solution.py:78
  236.1 2.1 convert_reduce_fusion
  238.2 0.0 all-reduce.3.cloned.1.call-update
  238.2 4.0 %convolution_bitcast_fusion = f32[8,8,3072]{2,1,0:T(8,128)S(1)} fusion(bf16[1024,3072]{1,0:T(8,128)(2,1)} %all-gather.2.cloned.1.call-done, bf16[64,512]{1,0:T(8,128)(2,1)S(1)} %get-tuple-element.66, bf16[64,512]{1,0:T(8,128)(2,1)S(1)} %get-tuple-element.65), kind=kOutput, calls=%fused_computation.3 | convolution fusion | flops 402915328 | bytes 7208960 | tf_op jit(solution)/shard_map/dot_general | solution.py:83
  242.2 0.1 fusion.45
  242.3 0.2 copy.42
  242.5 0.2 fusion.15
  242.7 0.2 fusion.13
  243.0 0.2 copy.30
  243.1 12.1 %all_to_all.27 = f32[8,8,1024]{2,1,0:T(8,128)S(1)} all-to-all(f32[8,8,1024]{2,1,0:T(8,128)S(1)} %copy.30), channel_id=1, replica_groups=mesh['dp'=4,'fsdp'=8] {'fsdp'}, dimensions={0} | all-to-all | bytes 524288 | tf_op jit(solution)/shard_map/all_to_all | solution.py:96
  255.3 0.5 fusion.12
  255.8 0.7 copy.74
  256.5 41.4 %all-reduce.3.cloned.1.call-done = f32[128,3072]{0,1:T(8,128)} async-done(((f32[128,3072]{0,1:T(8,128)}), f32[128,3072]{0,1:T(8,128)}) %all-reduce.3.cloned.1.call-update) | async-done | bytes 1572880 | tf_op jit(solution)/shard_map/psum | solution.py:80
  297.9 1.5 broadcast_multiply_fusion
  299.5 1.6 copy.36
  (3 shorter events, 0.1 us)
Async XLA Ops:
  7.2 72.7 %all-gather.2.cloned.1.call-start = ((), (), s32[]{:S(2)}) async-start(), calls=%async_computation.4 | async-start | bytes 7077888 | tf_op jit(solution)/shard_map/all_gather | solution.py:40
  22.1 13.7 %all-to-all-start.1 = ((bf16[8,8,1024]{2,1,0:T(8,128)(2,1)}), bf16[8,8,1024]{2,1,0:T(8,128)(2,1)S(1)}, u32[]{:S(2)}, u32[]{:S(2)}) async-start(bf16[8,8,1024]{2,1,0:T(8,128)(2,1)} %copy.21), calls=%async_computation.1 | async-start | bytes 262144 | tf_op jit(solution)/shard_map/all_to_all | solution.py:35
  25.5 272.4 %all-reduce.3.cloned.1.call-start = ((), (), s32[]{:S(2)}) async-start(), calls=%async_computation.5 | async-start | bytes 3145728 | tf_op jit(solution)/shard_map/psum | solution.py:80
  36.0 51.0 %copy-start.1 = (bf16[64,512]{1,0:T(8,128)(2,1)S(1)}, bf16[64,512]{1,0:T(8,128)(2,1)}, u32[]{:S(2)}) copy-start(bf16[64,512]{1,0:T(8,128)(2,1)} %param.15) | copy-start | bytes 196612
  84.6 4.7 %copy-start = (bf16[64,1024]{1,0:T(8,128)(2,1)S(1)}, bf16[64,1024]{1,0:T(8,128)(2,1)}, u32[]{:S(2)}) copy-start(bf16[64,1024]{1,0:T(8,128)(2,1)} %param.14) | copy-start | bytes 393220
Sparse Core Ops, SparseCore 0:
  9.6 70.1 all-gather.1
  238.3 59.5 all-reduce.2
where the time goes:
time: 308 us
  blocking collectives  165 us (54%)
  waiting for transfers between devices  94.5 us (31%)
  matrix products  15.5 us (5%)
  between operations  14.2 us (5%)
  other arithmetic  10.4 us (3%)
  local copies, waits for them, and re-layouts  4.48 us (1%)
  starting transfers between devices  3.45 us (1%)
    all_to_all x1, blocking collectives, per_device(): lax.all_to_all(partial_value, 'fsdp', split_axis=0, concat_axis=0, tiled=...  142 us
    all_gather x1, waiting for transfers between devices, per_device(): full_weight = lax.all_gather(conv_weight, 'fsdp', axis=0, tiled=True)  43.8 us
    psum x1, waiting for transfers between devices, per_device(): group_total = lax.psum(shard_sum, 'dp')  41.4 us
    all_to_all x1, blocking collectives, per_device(): lax.all_to_all(outgoing_grad, 'fsdp', split_axis=0, concat_axis=0, tiled=...  12.1 us
    all_to_all x1, blocking collectives, per_device(): lax.all_to_all(request_mask, 'fsdp', split_axis=0, concat_axis=0, tiled=T...  11.7 us
    all_to_all x1, waiting for transfers between devices, per_device(): lax.all_to_all(outgoing, 'fsdp', split_axis=0, concat_axis=0, tiled=True)  8.59 us
    dot_general x3, matrix products, per_device(): lax.dot_general(windows[selected_index], full_weight[:, selected_index *...  7.17 us
  transfers between devices with their start and end apart: 3, of which 3 were waited for; matrix products, arithmetic and copies ran while one was open for 3% of the time, Pallas kernels for 0%

commit v1 on v0

--- a/solution.py
+++ b/solution.py
@@ -1,20 +1,313 @@
+import functools
 import math
 
 import jax
 import jax.numpy as jnp
 from jax import lax
+from jax.experimental import pallas as pl
+from jax.experimental.pallas import tpu as pltpu
 from jax.sharding import PartitionSpec as P
 
 C = 1024
 H = 512
 DILATION_SIZE = 4
+SEG = 8
+BF16 = jnp.bfloat16
+F32 = jnp.float32
+VMEM = pl.BlockSpec(memory_space=pltpu.VMEM)
+SMEM = pl.BlockSpec(memory_space=pltpu.SMEM)
+
+
+def swap(value, axis, distance):
+    count = lax.axis_size(axis)
+    return lax.ppermute(value, axis, [(i, i ^ distance) for i in range(count)])
+
+
+def call(body, out_shapes, in_specs, scratch=(), out_specs=None, flops=0, moved=0):
+    return pl.pallas_call(
+        body,
+        out_shape=out_shapes,
+        in_specs=in_specs,
+        out_specs=out_specs if out_specs is not None else [VMEM] * len(out_shapes),
+        scratch_shapes=list(scratch),
+        compiler_params=pltpu.CompilerParams(vmem_limit_bytes=24 * 1024 * 1024),
+        cost_estimate=pl.CostEstimate(flops=flops, bytes_accessed=moved, transcendentals=0),
+    )
+
+
+def shaped(shape, dtype):
+    return jax.ShapeDtypeStruct(shape, dtype)
+
+
+def roll_half(first, second):
+    row = lax.broadcasted_iota(jnp.int32, first.shape, 0)
+    return pltpu.roll(jnp.where(row >= 4, first, second), 4, 0)
+
+
+def pick_columns(me_ref, grad_ref, *outs):
+    width = outs[0].shape[1] // 2
+    q = lax.rem(me_ref[0], grad_ref.shape[1] // width)
+    for pair, out in enumerate(outs):
+        for half in range(2):
+            start = pl.multiple_of((q ^ (2 * pair + half)) * width, width)
+            out[:, half * width : (half + 1) * width] = grad_ref[:, pl.ds(start, width)]
+
+
+def stack_weight(own_ref, other_ref, out_ref):
+    width = own_ref.shape[0]
+    for tap in range(3):
+        for part, ref in enumerate((own_ref, other_ref)):
+            start = (2 * tap + part) * width
+            out_ref[start : start + width, :] = ref[:, tap * C : (tap + 1) * C]
+
+
+def routes(seg_count, chips, rows, me_ref, *refs):
+    tables, source_ref, follow_ref = refs[:-2], refs[-2], refs[-1]
+    slots = 2 * chips
+    missing = slots * rows
+    me = me_ref[0]
+    for i in range(follow_ref.shape[0]):
+        follow_ref[i] = missing
+    for group in range(len(tables) // 2):
+        for slot in range(slots):
+            table = tables[2 * group + slot // chips]
+            for position in range(seg_count):
+                source = table[slot % chips, position]
+                safe = jnp.maximum(source, 0)
+                apart = (safe // seg_count) ^ me
+                segment = ((apart & 1) * chips + (apart >> 1)) * seg_count + lax.rem(safe, seg_count)
+                at = slot * seg_count + position
+                source_ref[group * slots * seg_count + at] = jnp.where(source >= 0, segment * SEG, missing)
+
+                @pl.when(source >= 0)
+                def _():
+                    follow_ref[group * slots * seg_count + segment] = at * SEG
+
+
+def forward(own_class, me_ref, source_ref, weight_ref, *refs):
+    blocks, (act_ref, sent_ref, rows_ref, early_ref) = refs[:-4], refs[-4:]
+    count = blocks[0].shape[0]
+    for i, block in enumerate(blocks):
+        rows_ref[i * count : (i + 1) * count, :] = block[...]
+    total = len(blocks) * count
+    wide = weight_ref.shape[0] // 3
+    nt = (((1,), (1,)), ((), ()))
+    early_ref[:total, :] = lax.dot_general(
+        rows_ref[...], weight_ref[: 2 * wide, :], nt, preferred_element_type=F32
+    )
+    early_ref[total:, :] = jnp.zeros((SEG, 2 * wide), F32)
+    act_ref[...] = lax.dot_general(
+        rows_ref[:own_class, :], weight_ref[2 * wide :, :], nt, preferred_element_type=F32
+    )
+    is_filter = me_ref[0] < me_ref[1]
+    for segment in range(own_class // SEG):
+        at = segment * SEG
+        source = pl.multiple_of(source_ref[segment], SEG)
+        carried = early_ref[pl.ds(source, SEG), :]
+        preact = (
+            act_ref[at : at + SEG, :]
+            + carried[:, :wide]
+            + roll_half(carried[:, wide:], early_ref[at : at + SEG, wide:])
+        )
+        act_ref[at : at + SEG, :] = jnp.where(is_filter, jnp.tanh(preact), jax.nn.sigmoid(preact))
+    sent_ref[...] = act_ref[...].astype(BF16)
+
+
+def gate(me_ref, act_ref, other_ref, *refs):
+    grads, outs, pre_ref = refs[: len(refs) // 3 * 2], refs[len(refs) // 3 * 2 : -1], refs[-1]
+    count = grads[0].shape[0]
+    is_filter = me_ref[0] < me_ref[1]
+    slots = len(grads)
+    for slot, grad in enumerate(grads):
+        at = slot * count
+        there = (slot ^ (slots // 2)) * count
+        mine = act_ref[at : at + count, :]
+        theirs = other_ref[there : there + count, :].astype(F32)
+        upstream = grad[...].astype(F32)
+        if slot < len(outs):
+            outs[slot][...] = (mine * theirs).astype(BF16)
+        for_filter = upstream * theirs * (1.0 - mine * mine)
+        for_gate = upstream * theirs * mine * (1.0 - mine)
+        pre_ref[at : at + count, :] = jnp.where(is_filter, for_filter, for_gate).astype(BF16)
+
+
+def input_grad(follow_ref, own_ref, other_ref, weight_ref, *refs):
+    kept_ref, sends, sent_pre_ref, pre_ref, routed_ref = refs[0], refs[1:-3], refs[-3], refs[-2], refs[-1]
+    total, wide = own_ref.shape
+    width = wide // 2
+    sent_pre_ref[:total, :] = own_ref[:, :width]
+    sent_pre_ref[total:, :] = other_ref[:, width:]
+    pre_ref[:total, :] = own_ref[...].astype(F32)
+    pre_ref[total : 2 * total, :width] = other_ref[:, width:].astype(F32)
+    pre_ref[total : 2 * total, width:] = other_ref[:, :width].astype(F32)
+    pre_ref[2 * total :, :] = jnp.zeros((SEG, wide), F32)
+    for segment in range(total // SEG):
+        at = segment * SEG
+        follow = pl.multiple_of(follow_ref[segment], SEG)
+        carried = pre_ref[pl.ds(follow, SEG), :]
+        local = pre_ref[at : at + SEG, :]
+        routed_ref[at : at + SEG, :wide] = carried
+        routed_ref[at : at + SEG, wide : 2 * wide] = roll_half(local, carried)
+        routed_ref[at : at + SEG, 2 * wide :] = local
+    part = jnp.dot(routed_ref[...].astype(BF16), weight_ref[...], preferred_element_type=F32)
+    count = kept_ref.shape[0]
+    kept_ref[...] = part[:count, :]
+    for slot, out in enumerate(sends):
+        out[...] = part[(slot + 1) * count : (slot + 2) * count, :].astype(BF16)
+
+
+def weight_grad(groups, scale, follow_ref, *refs):
+    per_group = (len(refs) - 4) // groups
+    first_ref, out_ref, pre_ref, routed_ref, rows_ref = (None,) + refs[-4:]
+    if (len(refs) - 4) % groups:
+        first_ref, refs = refs[0], refs[1:]
+        per_group = (len(refs) - 4) // groups
+    total = pre_ref.shape[0] - SEG
+    width = pre_ref.shape[1]
+    pre_ref[total:, :] = jnp.zeros((SEG, width), F32)
+    for group in range(groups):
+        inputs = refs[group * per_group : (group + 1) * per_group]
+        pre_ref[:total, :] = inputs[0][...].astype(F32)
+        base = group * total
+        at = base
+        for block in inputs[1:]:
+            rows_ref[at : at + block.shape[0], :] = block[...]
+            at += block.shape[0]
+        for segment in range(total // SEG):
+            at = segment * SEG
+            follow = pl.multiple_of(follow_ref[group * (total // SEG) + segment], SEG)
+            carried = pre_ref[pl.ds(follow, SEG), :]
+            local = pre_ref[at : at + SEG, :]
+            at += base
+            routed_ref[at : at + SEG, :width] = carried
+            routed_ref[at : at + SEG, width : 2 * width] = roll_half(local, carried)
+            routed_ref[at : at + SEG, 2 * width :] = local
+    product = lax.dot_general(
+        routed_ref[...].astype(BF16), rows_ref[...], (((0,), (0,)), ((), ())), preferred_element_type=F32
+    )
+    for tap in range(3):
+        here = slice(tap * C, (tap + 1) * C)
+        value = product[tap * width : (tap + 1) * width, :]
+        if first_ref is not None:
+            value = (value + first_ref[:, here]) * scale
+        out_ref[:, here] = value
+
+
+def place_gated(me_ref, *refs):
+    pieces, out_ref = refs[:-1], refs[-1]
+    width = pieces[0].shape[1] // 2
+    q = lax.rem(me_ref[0], out_ref.shape[1] // width)
+    for pair, piece in enumerate(pieces):
+        for half in range(2):
+            start = pl.multiple_of((q ^ (2 * pair + half)) * width, width)
+            out_ref[:, pl.ds(start, width)] = piece[:, half * width : (half + 1) * width]
+
+
+def add_parts(kept_ref, *refs):
+    total = kept_ref[...]
+    for part in refs[:-1]:
+        total = total + part[...].astype(F32)
+    refs[-1][...] = total.astype(BF16)
+
+
+def by_channels(signal, grad_gated, conv_weight, source_seg):
+    peers, groups = lax.axis_size("fsdp"), lax.axis_size("dp")
+    chips = peers // 2
+    seg_count = source_seg.shape[1]
+    rows, width = signal.shape[0], conv_weight.shape[0]
+    own_class, all_rows = chips * rows, peers * rows
+    wide = 2 * width
+    half_chips = chips // 2
+    me = lax.axis_index("fsdp").astype(jnp.int32)
+    who = jnp.stack([me, jnp.int32(peers // 2)])
+
+    own_rows = [signal] + [swap(signal, "fsdp", 2 * k) for k in range(1, chips)]
+    other_weight = swap(conv_weight, "fsdp", 1)
+    tables = [jnp.concatenate([source_seg] + [swap(source_seg, "fsdp", 2 * k) for k in range(1, chips)], 0)]
+    tables.append(swap(tables[0], "fsdp", 1))
+    picked = call(
+        pick_columns, [shaped((rows, wide), BF16)] * half_chips, [SMEM, VMEM]
+    )(who, grad_gated)
+    grads = [picked[0]] + [swap(picked[k % half_chips], "fsdp", 2 * k) for k in range(1, chips)]
+    weight = call(stack_weight, [shaped((3 * wide, C), BF16)], [VMEM, VMEM])(conv_weight, other_weight)[0]
+    other_rows = [swap(block, "fsdp", 1) for block in own_rows]
+
+    def find_routes(*found):
+        count = len(found) // 2 * peers * seg_count
+        return call(
+            functools.partial(routes, seg_count, chips, rows),
+            [shaped((count,), jnp.int32)] * 2,
+            [SMEM] * (1 + len(found)),
+            out_specs=[SMEM] * 2,
+        )(who, *found)
+
+    sources, follows = find_routes(*tables)
+
+    act, sent = call(
+        functools.partial(forward, own_class),
+        [shaped((own_class, wide), F32), shaped((own_class, wide), BF16)],
+        [SMEM, SMEM] + [VMEM] * (1 + peers),
+        [pltpu.VMEM((all_rows, C), BF16), pltpu.VMEM((all_rows + SEG, 2 * wide), F32)],
+        flops=2 * all_rows * C * 3 * wide,
+        moved=2 * all_rows * C,
+    )(who, sources, weight, *own_rows, *other_rows)
+    partner = swap(sent, "fsdp", peers // 2)
+
+    far = []
+    own_stack = jnp.concatenate(own_rows, 0)
+    for d in range(1, groups):
+        there = swap(own_stack, "dp", d)
+        far.append([there, swap(there, "fsdp", 1)])
+    far_tables = []
+    for d in range(1, groups):
+        far_tables += [swap(table, "dp", d) for table in tables]
+    far_follows = find_routes(*far_tables)[1]
+
+    *gated, pre = call(
+        gate,
+        [shaped((rows, wide), BF16)] * half_chips + [shaped((own_class, wide), BF16)],
+        [SMEM] + [VMEM] * (2 + chips),
+    )(who, act, partner, *grads)
+    other_pre = swap(pre, "fsdp", 1)
+    kept, *sends, sent_pre = call(
+        input_grad,
+        [shaped((rows, C), F32)] + [shaped((rows, C), BF16)] * (chips - 1) + [shaped((all_rows, width), BF16)],
+        [SMEM, VMEM, VMEM, VMEM],
+        [pltpu.VMEM((all_rows + SEG, wide), F32), pltpu.VMEM((own_class, 3 * wide), F32)],
+        flops=2 * own_class * C * 3 * wide,
+    )(follows, pre, other_pre, weight)
+    parts = [swap(part, "fsdp", 2 * (k + 1)) for k, part in enumerate(sends)]
+    far_pre = [swap(sent_pre, "dp", d) for d in range(1, groups)]
+    gated = [gated[0]] + [swap(piece, "fsdp", 2 * (k + 1)) for k, piece in enumerate(gated[1:])]
+    gated_out = call(place_gated, [shaped((rows, H), BF16)], [SMEM] + [VMEM] * len(gated))(who, *gated)[0]
+
+    def grads_of(count, inputs, table, first):
+        return call(
+            functools.partial(weight_grad, count, 1.0 / math.sqrt(all_rows * groups)),
+            [shaped((width, 3 * C), F32)],
+            [SMEM] + [VMEM] * (len(inputs) + len(first)),
+            [
+                pltpu.VMEM((all_rows + SEG, width), F32),
+                pltpu.VMEM((count * all_rows, 3 * width), F32),
+                pltpu.VMEM((count * all_rows, C), BF16),
+            ],
+            flops=2 * count * all_rows * C * 3 * width,
+        )(table, *first, *inputs)[0]
+
+    near = grads_of(1, [sent_pre, *own_rows, *other_rows], follows, [])
+    far_inputs = []
+    for d in range(groups - 1):
+        far_inputs += [far_pre[d], *far[d]]
+    grad_weight = grads_of(groups - 1, far_inputs, far_follows, [near])
+    grad_in = call(add_parts, [shaped((rows, C), BF16)], [VMEM] * chips)(kept, *parts)[0]
+    return gated_out, grad_in, grad_weight
 
 
 def tap_starts(context_row_block):
     return [context_row_block - (2 - selected_index) * DILATION_SIZE for selected_index in range(3)]
 
 
-def per_device(signal, grad_gated, conv_weight, source_seg):
+def by_rows(signal, grad_gated, conv_weight, source_seg):
     peer_count = lax.axis_size("fsdp")
     seg_count = source_seg.shape[1]
     row_count = signal.shape[0]
@@ -107,6 +400,22 @@
     return (gated_out, grad_in, grad_weight)
 
 
+def per_device(signal, grad_gated, conv_weight, source_seg):
+    peers, groups = lax.axis_size("fsdp"), lax.axis_size("dp")
+    rows, seg_count = signal.shape[0], source_seg.shape[1]
+    fits = (
+        rows == SEG * seg_count
+        and conv_weight.shape[0] % 128 == 0
+        and peers & (peers - 1) == 0
+        and groups & (groups - 1) == 0
+        and peers >= 4
+        and groups >= 2
+        and groups * peers * rows <= 2048
+    )
+    plan = by_channels if fits else by_rows
+    return plan(signal, grad_gated, conv_weight, source_seg)
+
+
 def solution(mesh):
     placed = (
         P(("dp", "fsdp"), None),

time: 308 us -> 110 us (0.36)
  blocking collectives: 165 us -> 0 us
  waiting for transfers between devices: 94.5 us -> 47.7 us
  starting transfers between devices: 3.45 us -> 38.3 us
  Pallas kernels: 0 us -> 16.3 us
  matrix products: 15.5 us -> 0 us
  between operations: 14.2 us -> 0.84 us
  other arithmetic: 10.4 us -> 0.74 us
    all_to_all x3 -> x0, blocking collectives: 165 us -> none  [the longest x1 142 us: per_device(): lax.all_to_all(partial_value, 'fsdp', split_axis=0, concat_axis=0, tiled=...]
    ppermute x0 -> x36, waiting for transfers between devices: none -> 47.7 us  [swap(): return lax.ppermute(value, axis, [(i, i ^ distance) for i in range(count)])]
    all_gather x1 -> x0, waiting for transfers between devices: 43.8 us -> none  [per_device(): full_weight = lax.all_gather(conv_weight, 'fsdp', axis=0, tiled=True)]
    psum x1 -> x0, waiting for transfers between devices: 41.4 us -> none  [per_device(): group_total = lax.psum(shard_sum, 'dp')]
    ppermute x0 -> x36, starting transfers between devices: none -> 38.3 us  [swap(): return lax.ppermute(value, axis, [(i, i ^ distance) for i in range(count)])]
    pallas_call x0 -> x11, Pallas kernels: none -> 16.3 us  [the longest x2 5.27 us: grads_of(): call(functools.partial(weight_grad, count, 1.0 / math.sqrt(all_rows * gro...]
    dot_general x11 -> x0, matrix products: 15.5 us -> none  [the longest x3 7.17 us: per_device(): lax.dot_general(windows[selected_index], full_weight[:, selected_index *...]
    all_to_all x1 -> x0, waiting for transfers between devices: 8.59 us -> none  [per_device(): lax.all_to_all(outgoing, 'fsdp', split_axis=0, concat_axis=0, tiled=True)]
  transfers between devices with their start and end apart: 3 -> 36, of which waited for: 3 -> 18; matrix products, arithmetic and copies ran while one was open for 3% -> 4% of each run, Pallas kernels for 0% -> 11%
where the time goes in v1:
time: 110 us
  waiting for transfers between devices  47.7 us (43%)
  starting transfers between devices  38.3 us (35%)
  Pallas kernels  16.3 us (15%)
  local copies, waits for them, and re-layouts  5.77 us (5%)
    ppermute x36, waiting for transfers between devices, swap(): return lax.ppermute(value, axis, [(i, i ^ distance) for i in range(count)])  47.7 us
    ppermute x36, starting transfers between devices, swap(): return lax.ppermute(value, axis, [(i, i ^ distance) for i in range(count)])  38.3 us
    pallas_call x2, Pallas kernels, grads_of(): call(functools.partial(weight_grad, count, 1.0 / math.sqrt(all_rows * gro...  5.27 us
    unnamed x17, local copies, waits for them, and re-layouts  5.11 us
    pallas_call x2, Pallas kernels, find_routes(): call(functools.partial(routes, seg_count, chips, rows), [shaped((count,),...  4.67 us
  transfers between devices with their start and end apart: 36, of which 18 were waited for; matrix products, arithmetic and copies ran while one was open for 4% of the time, Pallas kernels for 11%

profile of v1, /device:TPU:0, one launch (start us, length us, event | category | flops | bytes accessed | tf_op | source)
XLA Modules:
  0.0 109.7 jit_solution(16781512949067866390)
XLA Ops:
  0.6 3.1 %collective-permute-start.5 = (bf16[64,1024]{1,0:T(8,128)(2,1)}, bf16[64,1024]{1,0:T(8,128)(2,1)S(1)}, u32[]{:S(2)}, u32[]{:S(2)}) collective-permute-start(bf16[64,1024]{1,0:T(8,128)(2,1)} %refs_1_.1), channel_id=1, source_target_pairs={{0,2},{1,3},{2,0},{3,1},{4,6},{5,7},{6,4},{7,5},{8,10},{9,11},{10,... | collective-permute-start | bytes 393224 | tf_op jit(solution)/shard_map/ppermute | solution.py:23
  3.7 2.5 %collective-permute-start.7 = (bf16[64,1024]{1,0:T(8,128)(2,1)}, bf16[64,1024]{1,0:T(8,128)(2,1)S(1)}, u32[]{:S(2)}, u32[]{:S(2)}) collective-permute-start(bf16[64,1024]{1,0:T(8,128)(2,1)} %refs_1_.1), channel_id=1, source_target_pairs={{0,6},{1,7},{2,4},{3,5},{4,2},{5,3},{6,0},{7,1},{8,14},{9,15},{10,... | collective-permute-start | bytes 393224 | tf_op jit(solution)/shard_map/ppermute | solution.py:23
  6.2 0.1 collective-permute-start.6
  6.3 1.6 %constant_dynamic-update-slice_fusion.3 = bf16[256,1024]{1,0:T(8,128)(2,1)} fusion(bf16[64,1024]{1,0:T(8,128)(2,1)} %refs_1_.1), kind=kLoop, calls=%fused_computation.3 | loop fusion | bytes 262144
  7.9 0.7 constant_dynamic-update-slice_fusion.2
  8.6 9.6 %collective-permute-done.6.refs_2_.refs_3_ = bf16[64,1024]{1,0:T(8,128)(2,1)S(1)} collective-permute-done((bf16[64,1024]{1,0:T(8,128)(2,1)}, bf16[64,1024]{1,0:T(8,128)(2,1)S(1)}, u32[]{:S(2)}, u32[]{:S(2)}) %collective-permute-start.6) | collective-permute-done | bytes 131104 | tf_op jit(solution)/shard_map/ppermute | solution.py:23
  18.2 0.7 constant_dynamic-update-slice_fusion.1
  18.9 0.7 constant_dynamic-update-slice_fusion
  19.5 2.4 %collective-permute-start.34 = (bf16[256,1024]{1,0:T(8,128)(2,1)}, bf16[256,1024]{1,0:T(8,128)(2,1)S(1)}, u32[]{:S(2)}, u32[]{:S(2)}) collective-permute-start(bf16[256,1024]{1,0:T(8,128)(2,1)} %constant_dynamic-update-slice_fusion), channel_id=1, source_target_pairs={{0,24},{8,16},{16,8},{24,0},{1,25},{9,17},{17,9},{25,1},{2,26},{10... | collective-permute-start | bytes 1572872 | tf_op jit(solution)/shard_map/ppermute | solution.py:23
  22.0 3.2 %collective-permute-start = (s32[1,8]{1,0:T(1,128)}, s32[1,8]{1,0:T(1,128)S(1)}, u32[]{:S(2)}, u32[]{:S(2)}) collective-permute-start(s32[1,8]{1,0:T(1,128)} %param.7), channel_id=1, source_target_pairs={{0,2},{1,3},{2,0},{3,1},{4,6},{5,7},{6,4},{7,5},{8,10},{9,11},{10,... | collective-permute-start | bytes 104 | tf_op jit(solution)/shard_map/ppermute | solution.py:23
  25.2 1.2 %collective-permute-start.2 = (s32[1,8]{1,0:T(1,128)}, s32[1,8]{1,0:T(1,128)S(1)}, u32[]{:S(2)}, u32[]{:S(2)}) collective-permute-start(s32[1,8]{1,0:T(1,128)} %param.7), channel_id=1, source_target_pairs={{0,6},{1,7},{2,4},{3,5},{4,2},{5,3},{6,0},{7,1},{8,14},{9,15},{10,... | collective-permute-start | bytes 104 | tf_op jit(solution)/shard_map/ppermute | solution.py:23
  26.4 0.2 collective-permute-done.1
  26.6 0.5 collective-permute-start.31
  27.1 0.5 collective-permute-start.28
  27.6 3.0 %collective-permute-done.2 = s32[1,8]{1,0:T(1,128)S(1)} collective-permute-done((s32[1,8]{1,0:T(1,128)}, s32[1,8]{1,0:T(1,128)S(1)}, u32[]{:S(2)}, u32[]{:S(2)}) %collective-permute-start.2) | collective-permute-done | bytes 64 | tf_op jit(solution)/shard_map/ppermute | solution.py:23
  30.6 0.7 pad_add_fusion.refs_0_
  31.3 1.1 %collective-permute-done.3.refs_1_ = s32[4,8]{1,0:T(4,128)S(1)} collective-permute-done((s32[4,8]{1,0:T(4,128)S(1)}, s32[4,8]{1,0:T(4,128)S(1)}, u32[]{:S(2)}, u32[]{:S(2)}) %collective-permute-start.3) | collective-permute-done | bytes 160 | tf_op jit(solution)/shard_map/ppermute | solution.py:23
  32.5 0.2 collective-permute-start.8
  32.6 1.4 %collective-permute-done.8.refs_4_.refs_5_ = bf16[64,1024]{1,0:T(8,128)(2,1)S(1)} collective-permute-done((bf16[64,1024]{1,0:T(8,128)(2,1)}, bf16[64,1024]{1,0:T(8,128)(2,1)S(1)}, u32[]{:S(2)}, u32[]{:S(2)}) %collective-permute-start.8) | collective-permute-done | bytes 131104 | tf_op jit(solution)/shard_map/ppermute | solution.py:23
  34.0 0.7 copy-done.2
  34.7 0.2 collective-permute-start.11
  34.8 0.7 collective-permute-done.34.refs_8_
  35.6 0.5 collective-permute-done.11.refs_7_.refs_8_
  36.0 0.6 copy-done.4
  36.7 0.2 collective-permute-start.10
  36.8 0.3 collective-permute-start.9
  37.2 0.1 pad_add_fusion.1.me_ref
  37.3 1.7 %shard_map.67 = (s32[64]{0:T(128)S(1)}, s32[64]{0:T(128)S(1)}) custom-call(s32[2]{0:T(128)S(1)} %pad_add_fusion.1.me_ref, s32[4,8]{1,0:T(4,128)S(1)} %pad_add_fusion.refs_0_, s32[4,8]{1,0:T(4,128)S(1)} %collective-permute-done.3.refs_1_), custom_call_target="tpu_custom_call" | custom-call | tf_op jit(solution)/shard_map/pallas_call | solution.py:237
  39.0 0.1 shard_map.68.weight_ref
  39.1 0.7 copy-done.1
  40.0 2.0 %shard_map.69 = (f32[256,256]{1,0:T(8,128)S(1)}, bf16[256,256]{1,0:T(8,128)(2,1)S(1)}) custom-call(s32[2]{0:T(128)S(1)} %pad_add_fusion.1.me_ref, s32[64]{0:T(128)S(1)} %get-tuple-element.18.source_ref, bf16[768,1024]{1,0:T(8,128)(2,1)S(1)} %shard_map.68.weight_ref, bf16[64,1024]{1,0:T(8,128)(2,1)S(1)} %copy-done.1, ...), custom_call_target="tpu_custom_call" | custom-call | flops 805306368 | bytes 1048576 | tf_op jit(solution)/shard_map/pallas_call | solution.py:246
  42.0 0.6 shard_map.70
  42.6 3.0 %collective-permute-start.14 = (bf16[64,256]{1,0:T(8,128)(2,1)S(1)}, bf16[64,256]{1,0:T(8,128)(2,1)S(1)}, u32[]{:S(2)}, u32[]{:S(2)}) collective-permute-start(bf16[64,256]{1,0:T(8,128)(2,1)S(1)} %get-tuple-element.21.refs_0_), channel_id=1, source_target_pairs={{0,4},{1,5},{2,6},{3,7},{4,0},{5,1},{6,2},{7,3},{8,12},{9,13},{10,... | collective-permute-start | bytes 98312 | tf_op jit(solution)/shard_map/ppermute | solution.py:23
  45.6 0.5 collective-permute-start.29
  46.1 6.4 %collective-permute-done.14.refs_2_ = bf16[64,256]{1,0:T(8,128)(2,1)S(1)} collective-permute-done((bf16[64,256]{1,0:T(8,128)(2,1)S(1)}, bf16[64,256]{1,0:T(8,128)(2,1)S(1)}, u32[]{:S(2)}, u32[]{:S(2)}) %collective-permute-start.14) | collective-permute-done | bytes 32800 | tf_op jit(solution)/shard_map/ppermute | solution.py:23
  52.5 1.3 %collective-permute-start.15 = (bf16[64,256]{1,0:T(8,128)(2,1)S(1)}, bf16[64,256]{1,0:T(8,128)(2,1)S(1)}, u32[]{:S(2)}, u32[]{:S(2)}) collective-permute-start(bf16[64,256]{1,0:T(8,128)(2,1)S(1)} %get-tuple-element.22), channel_id=1, source_target_pairs={{0,6},{1,7},{2,4},{3,5},{4,2},{5,3},{6,0},{7,1},{8,14},{9,15},{10,... | collective-permute-start | bytes 98312 | tf_op jit(solution)/shard_map/ppermute | solution.py:23
  53.9 4.4 %collective-permute-done.15.refs_3_ = bf16[64,256]{1,0:T(8,128)(2,1)S(1)} collective-permute-done((bf16[64,256]{1,0:T(8,128)(2,1)S(1)}, bf16[64,256]{1,0:T(8,128)(2,1)S(1)}, u32[]{:S(2)}, u32[]{:S(2)}) %collective-permute-start.15) | collective-permute-done | bytes 32800 | tf_op jit(solution)/shard_map/ppermute | solution.py:23
  58.3 3.9 %collective-permute-done.13.refs_1_ = bf16[64,256]{1,0:T(8,128)(2,1)S(1)} collective-permute-done((bf16[64,256]{1,0:T(8,128)(2,1)S(1)}, bf16[64,256]{1,0:T(8,128)(2,1)S(1)}, u32[]{:S(2)}, u32[]{:S(2)}) %collective-permute-start.13) | collective-permute-done | bytes 32800 | tf_op jit(solution)/shard_map/ppermute | solution.py:23
  62.2 0.6 shard_map.71
  62.9 2.5 %collective-permute-start.25 = (s32[4,8]{1,0:T(4,128)S(1)}, s32[4,8]{1,0:T(4,128)S(1)}, u32[]{:S(2)}, u32[]{:S(2)}) collective-permute-start(s32[4,8]{1,0:T(4,128)S(1)} %pad_add_fusion.refs_0_), channel_id=1, source_target_pairs={{0,24},{8,16},{16,8},{24,0},{1,25},{9,17},{17,9},{25,1},{2,26},{10... | collective-permute-start | bytes 392 | tf_op jit(solution)/shard_map/ppermute | solution.py:23
  65.4 2.0 %collective-permute-done.25.refs_4_ = s32[4,8]{1,0:T(4,128)S(1)} collective-permute-done((s32[4,8]{1,0:T(4,128)S(1)}, s32[4,8]{1,0:T(4,128)S(1)}, u32[]{:S(2)}, u32[]{:S(2)}) %collective-permute-start.25) | collective-permute-done | bytes 160 | tf_op jit(solution)/shard_map/ppermute | solution.py:23
  67.4 1.5 %collective-permute-start.23 = (s32[4,8]{1,0:T(4,128)S(1)}, s32[4,8]{1,0:T(4,128)S(1)}, u32[]{:S(2)}, u32[]{:S(2)}) collective-permute-start(s32[4,8]{1,0:T(4,128)S(1)} %pad_add_fusion.refs_0_), channel_id=1, source_target_pairs={{0,16},{8,24},{16,0},{24,8},{1,17},{9,25},{17,1},{25,9},{2,18},{10... | collective-permute-start | bytes 392 | tf_op jit(solution)/shard_map/ppermute | solution.py:23
  69.0 2.1 %collective-permute-done.23.refs_2_ = s32[4,8]{1,0:T(4,128)S(1)} collective-permute-done((s32[4,8]{1,0:T(4,128)S(1)}, s32[4,8]{1,0:T(4,128)S(1)}, u32[]{:S(2)}, u32[]{:S(2)}) %collective-permute-start.23) | collective-permute-done | bytes 160 | tf_op jit(solution)/shard_map/ppermute | solution.py:23
  71.0 1.5 %collective-permute-start.21 = (s32[4,8]{1,0:T(4,128)S(1)}, s32[4,8]{1,0:T(4,128)S(1)}, u32[]{:S(2)}, u32[]{:S(2)}) collective-permute-start(s32[4,8]{1,0:T(4,128)S(1)} %pad_add_fusion.refs_0_), channel_id=1, source_target_pairs={{0,8},{8,0},{16,24},{24,16},{1,9},{9,1},{17,25},{25,17},{2,10},{10... | collective-permute-start | bytes 392 | tf_op jit(solution)/shard_map/ppermute | solution.py:23
  72.5 2.1 %collective-permute-done.21.refs_0_ = s32[4,8]{1,0:T(4,128)S(1)} collective-permute-done((s32[4,8]{1,0:T(4,128)S(1)}, s32[4,8]{1,0:T(4,128)S(1)}, u32[]{:S(2)}, u32[]{:S(2)}) %collective-permute-start.21) | collective-permute-done | bytes 160 | tf_op jit(solution)/shard_map/ppermute | solution.py:23
  74.6 2.4 %collective-permute-start.26 = (s32[4,8]{1,0:T(4,128)S(1)}, s32[4,8]{1,0:T(4,128)S(1)}, u32[]{:S(2)}, u32[]{:S(2)}) collective-permute-start(s32[4,8]{1,0:T(4,128)S(1)} %collective-permute-done.3.refs_1_), channel_id=1, source_target_pairs={{0,24},{8,16},{16,8},{24,0},{1,25},{9,17},{17,9},{25,1},{2,26},{10... | collective-permute-start | bytes 392 | tf_op jit(solution)/shard_map/ppermute | solution.py:23
  77.1 2.0 %collective-permute-done.26.refs_5_ = s32[4,8]{1,0:T(4,128)S(1)} collective-permute-done((s32[4,8]{1,0:T(4,128)S(1)}, s32[4,8]{1,0:T(4,128)S(1)}, u32[]{:S(2)}, u32[]{:S(2)}) %collective-permute-start.26) | collective-permute-done | bytes 160 | tf_op jit(solution)/shard_map/ppermute | solution.py:23
  79.1 1.5 %collective-permute-start.24 = (s32[4,8]{1,0:T(4,128)S(1)}, s32[4,8]{1,0:T(4,128)S(1)}, u32[]{:S(2)}, u32[]{:S(2)}) collective-permute-start(s32[4,8]{1,0:T(4,128)S(1)} %collective-permute-done.3.refs_1_), channel_id=1, source_target_pairs={{0,16},{8,24},{16,0},{24,8},{1,17},{9,25},{17,1},{25,9},{2,18},{10... | collective-permute-start | bytes 392 | tf_op jit(solution)/shard_map/ppermute | solution.py:23
  80.6 2.1 %collective-permute-done.24.refs_3_ = s32[4,8]{1,0:T(4,128)S(1)} collective-permute-done((s32[4,8]{1,0:T(4,128)S(1)}, s32[4,8]{1,0:T(4,128)S(1)}, u32[]{:S(2)}, u32[]{:S(2)}) %collective-permute-start.24) | collective-permute-done | bytes 160 | tf_op jit(solution)/shard_map/ppermute | solution.py:23
  82.7 1.5 %collective-permute-start.22 = (s32[4,8]{1,0:T(4,128)S(1)}, s32[4,8]{1,0:T(4,128)S(1)}, u32[]{:S(2)}, u32[]{:S(2)}) collective-permute-start(s32[4,8]{1,0:T(4,128)S(1)} %collective-permute-done.3.refs_1_), channel_id=1, source_target_pairs={{0,8},{8,0},{16,24},{24,16},{1,9},{9,1},{17,25},{25,17},{2,10},{10... | collective-permute-start | bytes 392 | tf_op jit(solution)/shard_map/ppermute | solution.py:23
  84.2 1.2 %shard_map.73 = (f32[64,1024]{1,0:T(8,128)S(1)}, bf16[64,1024]{1,0:T(8,128)(2,1)S(1)}, bf16[64,1024]{1,0:T(8,128)(2,1)S(1)}, bf16[64,1024]{1,0:T(8,128)(2,1)S(1)}, bf16[512,128]{1,0:T(8,128)(2,1)S(1)}) custom-call(s32[64]{0:T(128)S(1)} %get-tuple-element.25.follow_ref, bf16[256,256]{1,0:T(8,128)(2,1)S(1)} %get-tuple-element.26.own_ref, ...), custom_call_target="tpu_custom_call" | custom-call | flops 402653184 | tf_op jit(solution)/shard_map/pallas_call | solution.py:272
  85.3 0.9 collective-permute-done.22.refs_1_
  86.3 1.2 %collective-permute-start.18 = (bf16[64,1024]{1,0:T(8,128)(2,1)S(1)}, bf16[64,1024]{1,0:T(8,128)(2,1)S(1)}, u32[]{:S(2)}, u32[]{:S(2)}) collective-permute-start(bf16[64,1024]{1,0:T(8,128)(2,1)S(1)} %get-tuple-element.28), channel_id=1, source_target_pairs={{0,2},{1,3},{2,0},{3,1},{4,6},{5,7},{6,4},{7,5},{8,10},{9,11},{10,... | collective-permute-start | bytes 393224 | tf_op jit(solution)/shard_map/ppermute | solution.py:23
  87.4 1.9 %collective-permute-done.16.refs_1_ = bf16[64,256]{1,0:T(8,128)(2,1)S(1)} collective-permute-done((bf16[64,256]{1,0:T(8,128)(2,1)S(1)}, bf16[64,256]{1,0:T(8,128)(2,1)S(1)}, u32[]{:S(2)}, u32[]{:S(2)}) %collective-permute-start.16) | collective-permute-done | bytes 32800 | tf_op jit(solution)/shard_map/ppermute | solution.py:23
  89.3 1.9 %collective-permute-start.20 = (bf16[64,1024]{1,0:T(8,128)(2,1)S(1)}, bf16[64,1024]{1,0:T(8,128)(2,1)S(1)}, u32[]{:S(2)}, u32[]{:S(2)}) collective-permute-start(bf16[64,1024]{1,0:T(8,128)(2,1)S(1)} %get-tuple-element.30), channel_id=1, source_target_pairs={{0,6},{1,7},{2,4},{3,5},{4,2},{5,3},{6,0},{7,1},{8,14},{9,15},{10,... | collective-permute-start | bytes 393224 | tf_op jit(solution)/shard_map/ppermute | solution.py:23
  91.3 2.4 %collective-permute-start.33 = (bf16[512,128]{1,0:T(8,128)(2,1)S(1)}, bf16[512,128]{1,0:T(8,128)(2,1)S(1)}, u32[]{:S(2)}, u32[]{:S(2)}) collective-permute-start(bf16[512,128]{1,0:T(8,128)(2,1)S(1)} %get-tuple-element.32.refs_0_), channel_id=1, source_target_pairs={{0,24},{8,16},{16,8},{24,0},{1,25},{9,17},{17,9},{25,1},{2,26},{10... | collective-permute-start | bytes 393224 | tf_op jit(solution)/shard_map/ppermute | solution.py:23
  93.7 3.3 %collective-permute-done.19.refs_1_ = bf16[64,1024]{1,0:T(8,128)(2,1)S(1)} collective-permute-done((bf16[64,1024]{1,0:T(8,128)(2,1)S(1)}, bf16[64,1024]{1,0:T(8,128)(2,1)S(1)}, u32[]{:S(2)}, u32[]{:S(2)}) %collective-permute-start.19) | collective-permute-done | bytes 131104 | tf_op jit(solution)/shard_map/ppermute | solution.py:23
  97.0 1.5 %collective-permute-start.30 = (bf16[512,128]{1,0:T(8,128)(2,1)S(1)}, bf16[512,128]{1,0:T(8,128)(2,1)S(1)}, u32[]{:S(2)}, u32[]{:S(2)}) collective-permute-start(bf16[512,128]{1,0:T(8,128)(2,1)S(1)} %get-tuple-element.32.refs_0_), channel_id=1, source_target_pairs={{0,16},{8,24},{16,0},{24,8},{1,17},{9,25},{17,1},{25,9},{2,18},{10... | collective-permute-start | bytes 393224 | tf_op jit(solution)/shard_map/ppermute | solution.py:23
  98.5 0.9 collective-permute-start.27
  99.5 3.0 %shard_map.75 = (s32[192]{0:T(256)}, s32[192]{0:T(256)S(1)}) custom-call(s32[2]{0:T(128)S(1)} %pad_add_fusion.1.me_ref, s32[4,8]{1,0:T(4,128)S(1)} %collective-permute-done.21.refs_0_, s32[4,8]{1,0:T(4,128)S(1)} %collective-permute-done.22.refs_1_, s32[4,8]{1,0:T(4,128)S(1)} %collective-permute-done.23.refs_2_, s32[4,8]{1,0:T(4,128)S(1)} %collective-permute-done.24.refs_3_, ...), custom_call_target="tpu_custom_call" | custom-call | tf_op jit(solution)/shard_map/pallas_call | solution.py:237
  102.5 1.2 %shard_map.72 = bf16[64,512]{1,0:T(8,128)(2,1)} custom-call(s32[2]{0:T(128)S(1)} %pad_add_fusion.1.me_ref, bf16[64,256]{1,0:T(8,128)(2,1)S(1)} %get-tuple-element.23.refs_0_, bf16[64,256]{1,0:T(8,128)(2,1)S(1)} %collective-permute-done.16.refs_1_), custom_call_target="tpu_custom_call" | custom-call | tf_op jit(solution)/shard_map/pallas_call | solution.py:282
  103.6 1.6 %shard_map.76.refs_0_ = f32[128,3072]{1,0:T(8,128)S(1)} custom-call(s32[64]{0:T(128)S(1)} %get-tuple-element.25.follow_ref, bf16[512,128]{1,0:T(8,128)(2,1)S(1)} %get-tuple-element.32.refs_0_, bf16[64,1024]{1,0:T(8,128)(2,1)S(1)} %copy-done.1, bf16[64,1024]{1,0:T(8,128)(2,1)S(1)} %collective-permute-done.5.refs_1_.refs_2_, ...), custom_call_target="tpu_custom_call" | custom-call | flops 402653184 | tf_op jit(solution)/shard_map/pallas_call | solution.py:285
  105.3 0.7 shard_map.74
  106.0 3.7 %shard_map.77 = f32[128,3072]{1,0:T(8,128)} custom-call(s32[192]{0:T(256)S(1)} %get-tuple-element.31.follow_ref, f32[128,3072]{1,0:T(8,128)S(1)} %shard_map.76.refs_0_, bf16[512,128]{1,0:T(8,128)(2,1)S(1)} %collective-permute-done.27.refs_1_, bf16[256,1024]{1,0:T(8,128)(2,1)S(1)} %collective-permute-done.28.refs_2_, ...), custom_call_target="tpu_custom_call" | custom-call | flops 1207959552 | tf_op jit(solution)/shard_map/pallas_call | solution.py:285
  (39 shorter events, 0.4 us)
Async XLA Ops:
  0.6 38.3 %copy-start = (bf16[128,3072]{1,0:T(8,128)(2,1)S(1)}, bf16[128,3072]{1,0:T(8,128)(2,1)}, u32[]{:S(2)}) copy-start(bf16[128,3072]{1,0:T(8,128)(2,1)} %own_ref.1) | copy-start | bytes 2359300
  0.6 7.3 %collective-permute-start.5 = (bf16[64,1024]{1,0:T(8,128)(2,1)}, bf16[64,1024]{1,0:T(8,128)(2,1)S(1)}, u32[]{:S(2)}, u32[]{:S(2)}) collective-permute-start(bf16[64,1024]{1,0:T(8,128)(2,1)} %refs_1_.1), channel_id=1, source_target_pairs={{0,2},{1,3},{2,0},{3,1},{4,6},{5,7},{6,4},{7,5},{8,10},{9,11},{10,... | collective-permute-start | bytes 393224 | tf_op jit(solution)/shard_map/ppermute | solution.py:23
  3.7 15.1 %collective-permute-start.7 = (bf16[64,1024]{1,0:T(8,128)(2,1)}, bf16[64,1024]{1,0:T(8,128)(2,1)S(1)}, u32[]{:S(2)}, u32[]{:S(2)}) collective-permute-start(bf16[64,1024]{1,0:T(8,128)(2,1)} %refs_1_.1), channel_id=1, source_target_pairs={{0,6},{1,7},{2,4},{3,5},{4,2},{5,3},{6,0},{7,1},{8,14},{9,15},{10,... | collective-permute-start | bytes 393224 | tf_op jit(solution)/shard_map/ppermute | solution.py:23
  6.2 12.0 %collective-permute-start.6 = (bf16[64,1024]{1,0:T(8,128)(2,1)}, bf16[64,1024]{1,0:T(8,128)(2,1)S(1)}, u32[]{:S(2)}, u32[]{:S(2)}) collective-permute-start(bf16[64,1024]{1,0:T(8,128)(2,1)} %refs_1_.1), channel_id=1, source_target_pairs={{0,4},{1,5},{2,6},{3,7},{4,0},{5,1},{6,2},{7,3},{8,12},{9,13},{10,... | collective-permute-start | bytes 393224 | tf_op jit(solution)/shard_map/ppermute | solution.py:23
  6.3 30.5 %collective-permute-start.4 = (bf16[128,3072]{1,0:T(8,128)(2,1)}, bf16[128,3072]{1,0:T(8,128)(2,1)S(1)}, u32[]{:S(2)}, u32[]{:S(2)}) collective-permute-start(bf16[128,3072]{1,0:T(8,128)(2,1)} %own_ref.1), channel_id=1, source_target_pairs={{0,1},{1,0},{2,3},{3,2},{4,5},{5,4},{6,7},{7,6},{8,9},{9,8},{10,11... | collective-permute-start | bytes 2359304 | tf_op jit(solution)/shard_map/ppermute | solution.py:23
  19.5 16.0 %collective-permute-start.34 = (bf16[256,1024]{1,0:T(8,128)(2,1)}, bf16[256,1024]{1,0:T(8,128)(2,1)S(1)}, u32[]{:S(2)}, u32[]{:S(2)}) collective-permute-start(bf16[256,1024]{1,0:T(8,128)(2,1)} %constant_dynamic-update-slice_fusion), channel_id=1, source_target_pairs={{0,24},{8,16},{16,8},{24,0},{1,25},{9,17},{17,9},{25,1},{2,26},{10... | collective-permute-start | bytes 1572872 | tf_op jit(solution)/shard_map/ppermute | solution.py:23
  22.0 4.6 %collective-permute-start.1 = (s32[1,8]{1,0:T(1,128)}, s32[1,8]{1,0:T(1,128)S(1)}, u32[]{:S(2)}, u32[]{:S(2)}) collective-permute-start(s32[1,8]{1,0:T(1,128)} %param.7), channel_id=1, source_target_pairs={{0,4},{1,5},{2,6},{3,7},{4,0},{5,1},{6,2},{7,3},{8,12},{9,13},{10,... | collective-permute-start | bytes 104 | tf_op jit(solution)/shard_map/ppermute | solution.py:23
  22.0 5.1 %collective-permute-start = (s32[1,8]{1,0:T(1,128)}, s32[1,8]{1,0:T(1,128)S(1)}, u32[]{:S(2)}, u32[]{:S(2)}) collective-permute-start(s32[1,8]{1,0:T(1,128)} %param.7), channel_id=1, source_target_pairs={{0,2},{1,3},{2,0},{3,1},{4,6},{5,7},{6,4},{7,5},{8,10},{9,11},{10,... | collective-permute-start | bytes 104 | tf_op jit(solution)/shard_map/ppermute | solution.py:23
  25.2 5.5 %collective-permute-start.2 = (s32[1,8]{1,0:T(1,128)}, s32[1,8]{1,0:T(1,128)S(1)}, u32[]{:S(2)}, u32[]{:S(2)}) collective-permute-start(s32[1,8]{1,0:T(1,128)} %param.7), channel_id=1, source_target_pairs={{0,6},{1,7},{2,4},{3,5},{4,2},{5,3},{6,0},{7,1},{8,14},{9,15},{10,... | collective-permute-start | bytes 104 | tf_op jit(solution)/shard_map/ppermute | solution.py:23
  26.6 19.0 %collective-permute-start.31 = (bf16[256,1024]{1,0:T(8,128)(2,1)}, bf16[256,1024]{1,0:T(8,128)(2,1)S(1)}, u32[]{:S(2)}, u32[]{:S(2)}) collective-permute-start(bf16[256,1024]{1,0:T(8,128)(2,1)} %constant_dynamic-update-slice_fusion), channel_id=1, source_target_pairs={{0,16},{8,24},{16,0},{24,8},{1,17},{9,25},{17,1},{25,9},{2,18},{10... | collective-permute-start | bytes 1572872 | tf_op jit(solution)/shard_map/ppermute | solution.py:23
  27.1 18.5 %collective-permute-start.28 = (bf16[256,1024]{1,0:T(8,128)(2,1)}, bf16[256,1024]{1,0:T(8,128)(2,1)S(1)}, u32[]{:S(2)}, u32[]{:S(2)}) collective-permute-start(bf16[256,1024]{1,0:T(8,128)(2,1)} %constant_dynamic-update-slice_fusion), channel_id=1, source_target_pairs={{0,8},{8,0},{16,24},{24,16},{1,9},{9,1},{17,25},{25,17},{2,10},{10... | collective-permute-start | bytes 1572872 | tf_op jit(solution)/shard_map/ppermute | solution.py:23
  31.3 1.2 %collective-permute-start.3 = (s32[4,8]{1,0:T(4,128)S(1)}, s32[4,8]{1,0:T(4,128)S(1)}, u32[]{:S(2)}, u32[]{:S(2)}) collective-permute-start(s32[4,8]{1,0:T(4,128)S(1)} %pad_add_fusion.refs_0_), channel_id=1, source_target_pairs={{0,1},{1,0},{2,3},{3,2},{4,5},{5,4},{6,7},{7,6},{8,9},{9,8},{10,11... | collective-permute-start | bytes 392 | tf_op jit(solution)/shard_map/ppermute | solution.py:23
  32.5 1.6 %collective-permute-start.8 = (bf16[64,1024]{1,0:T(8,128)(2,1)}, bf16[64,1024]{1,0:T(8,128)(2,1)S(1)}, u32[]{:S(2)}, u32[]{:S(2)}) collective-permute-start(bf16[64,1024]{1,0:T(8,128)(2,1)} %refs_1_.1), channel_id=1, source_target_pairs={{0,1},{1,0},{2,3},{3,2},{4,5},{5,4},{6,7},{7,6},{8,9},{9,8},{10,11... | collective-permute-start | bytes 393224 | tf_op jit(solution)/shard_map/ppermute | solution.py:23
  34.0 0.7 copy-start.2
  34.7 1.3 %collective-permute-start.11 = (bf16[64,1024]{1,0:T(8,128)(2,1)S(1)}, bf16[64,1024]{1,0:T(8,128)(2,1)S(1)}, u32[]{:S(2)}, u32[]{:S(2)}) collective-permute-start(bf16[64,1024]{1,0:T(8,128)(2,1)S(1)} %collective-permute-done.7.refs_3_.refs_4_), channel_id=1, source_target_pairs={{0,1},{1,0},{2,3},{3,2},{4,5},{5,4},{6,7},{7,6},{8,9},{9,8},{10,11... | collective-permute-start | bytes 393224 | tf_op jit(solution)/shard_map/ppermute | solution.py:23
  35.5 53.8 %collective-permute-start.35 = (bf16[256,1024]{1,0:T(8,128)(2,1)S(1)}, bf16[256,1024]{1,0:T(8,128)(2,1)}, u32[]{:S(2)}, u32[]{:S(2)}) collective-permute-start(bf16[256,1024]{1,0:T(8,128)(2,1)S(1)} %collective-permute-done.34.refs_8_), channel_id=1, source_target_pairs={{0,1},{1,0},{2,3},{3,2},{4,5},{5,4},{6,7},{7,6},{8,9},{9,8},{10,11... | collective-permute-start | bytes 1572872 | tf_op jit(solution)/shard_map/ppermute | solution.py:23
  36.0 0.6 copy-start.4
  36.7 2.4 %collective-permute-start.10 = (bf16[64,1024]{1,0:T(8,128)(2,1)S(1)}, bf16[64,1024]{1,0:T(8,128)(2,1)}, u32[]{:S(2)}, u32[]{:S(2)}) collective-permute-start(bf16[64,1024]{1,0:T(8,128)(2,1)S(1)} %collective-permute-done.6.refs_2_.refs_3_), channel_id=1, source_target_pairs={{0,1},{1,0},{2,3},{3,2},{4,5},{5,4},{6,7},{7,6},{8,9},{9,8},{10,11... | collective-permute-start | bytes 393224 | tf_op jit(solution)/shard_map/ppermute | solution.py:23
  36.8 2.3 %collective-permute-start.9 = (bf16[64,1024]{1,0:T(8,128)(2,1)S(1)}, bf16[64,1024]{1,0:T(8,128)(2,1)}, u32[]{:S(2)}, u32[]{:S(2)}) collective-permute-start(bf16[64,1024]{1,0:T(8,128)(2,1)S(1)} %collective-permute-done.5.refs_1_.refs_2_), channel_id=1, source_target_pairs={{0,1},{1,0},{2,3},{3,2},{4,5},{5,4},{6,7},{7,6},{8,9},{9,8},{10,11... | collective-permute-start | bytes 393224 | tf_op jit(solution)/shard_map/ppermute | solution.py:23
  38.9 0.9 copy-start.1
  39.0 1.0 copy-start.3
  39.0 1.0 copy-start.5
  39.1 2.9 %copy-start.6 = (bf16[64,512]{1,0:T(8,128)(2,1)S(1)}, bf16[64,512]{1,0:T(8,128)(2,1)}, u32[]{:S(2)}) copy-start(bf16[64,512]{1,0:T(8,128)(2,1)} %grad_ref.1) | copy-start | bytes 196612
  41.9 20.2 %collective-permute-start.12 = (bf16[256,256]{1,0:T(8,128)(2,1)S(1)}, bf16[256,256]{1,0:T(8,128)(2,1)S(1)}, u32[]{:S(2)}, u32[]{:S(2)}) collective-permute-start(bf16[256,256]{1,0:T(8,128)(2,1)S(1)} %get-tuple-element.20), channel_id=1, source_target_pairs={{0,4},{1,5},{2,6},{3,7},{4,0},{5,1},{6,2},{7,3},{8,12},{9,13},{10,... | collective-permute-start | bytes 393224 | tf_op jit(solution)/shard_map/ppermute | solution.py:23
  42.6 9.9 %collective-permute-start.14 = (bf16[64,256]{1,0:T(8,128)(2,1)S(1)}, bf16[64,256]{1,0:T(8,128)(2,1)S(1)}, u32[]{:S(2)}, u32[]{:S(2)}) collective-permute-start(bf16[64,256]{1,0:T(8,128)(2,1)S(1)} %get-tuple-element.21.refs_0_), channel_id=1, source_target_pairs={{0,4},{1,5},{2,6},{3,7},{4,0},{5,1},{6,2},{7,3},{8,12},{9,13},{10,... | collective-permute-start | bytes 98312 | tf_op jit(solution)/shard_map/ppermute | solution.py:23
  45.6 60.4 %collective-permute-start.32 = (bf16[256,1024]{1,0:T(8,128)(2,1)S(1)}, bf16[256,1024]{1,0:T(8,128)(2,1)S(1)}, u32[]{:S(2)}, u32[]{:S(2)}) collective-permute-start(bf16[256,1024]{1,0:T(8,128)(2,1)S(1)} %collective-permute-done.31.refs_5_), channel_id=1, source_target_pairs={{0,1},{1,0},{2,3},{3,2},{4,5},{5,4},{6,7},{7,6},{8,9},{9,8},{10,11... | collective-permute-start | bytes 1572872 | tf_op jit(solution)/shard_map/ppermute | solution.py:23
  45.6 60.4 %collective-permute-start.29 = (bf16[256,1024]{1,0:T(8,128)(2,1)S(1)}, bf16[256,1024]{1,0:T(8,128)(2,1)S(1)}, u32[]{:S(2)}, u32[]{:S(2)}) collective-permute-start(bf16[256,1024]{1,0:T(8,128)(2,1)S(1)} %collective-permute-done.28.refs_2_), channel_id=1, source_target_pairs={{0,1},{1,0},{2,3},{3,2},{4,5},{5,4},{6,7},{7,6},{8,9},{9,8},{10,11... | collective-permute-start | bytes 1572872 | tf_op jit(solution)/shard_map/ppermute | solution.py:23
  52.5 5.7 %collective-permute-start.15 = (bf16[64,256]{1,0:T(8,128)(2,1)S(1)}, bf16[64,256]{1,0:T(8,128)(2,1)S(1)}, u32[]{:S(2)}, u32[]{:S(2)}) collective-permute-start(bf16[64,256]{1,0:T(8,128)(2,1)S(1)} %get-tuple-element.22), channel_id=1, source_target_pairs={{0,6},{1,7},{2,4},{3,5},{4,2},{5,3},{6,0},{7,1},{8,14},{9,15},{10,... | collective-permute-start | bytes 98312 | tf_op jit(solution)/shard_map/ppermute | solution.py:23
  58.3 3.9 %collective-permute-start.13 = (bf16[64,256]{1,0:T(8,128)(2,1)S(1)}, bf16[64,256]{1,0:T(8,128)(2,1)S(1)}, u32[]{:S(2)}, u32[]{:S(2)}) collective-permute-start(bf16[64,256]{1,0:T(8,128)(2,1)S(1)} %get-tuple-element.22), channel_id=1, source_target_pairs={{0,2},{1,3},{2,0},{3,1},{4,6},{5,7},{6,4},{7,5},{8,10},{9,11},{10,... | collective-permute-start | bytes 98312 | tf_op jit(solution)/shard_map/ppermute | solution.py:23
  62.8 21.4 %collective-permute-start.17 = (bf16[256,256]{1,0:T(8,128)(2,1)S(1)}, bf16[256,256]{1,0:T(8,128)(2,1)S(1)}, u32[]{:S(2)}, u32[]{:S(2)}) collective-permute-start(bf16[256,256]{1,0:T(8,128)(2,1)S(1)} %get-tuple-element.26.own_ref), channel_id=1, source_target_pairs={{0,1},{1,0},{2,3},{3,2},{4,5},{5,4},{6,7},{7,6},{8,9},{9,8},{10,11... | collective-permute-start | bytes 393224 | tf_op jit(solution)/shard_map/ppermute | solution.py:23
  62.9 4.5 %collective-permute-start.25 = (s32[4,8]{1,0:T(4,128)S(1)}, s32[4,8]{1,0:T(4,128)S(1)}, u32[]{:S(2)}, u32[]{:S(2)}) collective-permute-start(s32[4,8]{1,0:T(4,128)S(1)} %pad_add_fusion.refs_0_), channel_id=1, source_target_pairs={{0,24},{8,16},{16,8},{24,0},{1,25},{9,17},{17,9},{25,1},{2,26},{10... | collective-permute-start | bytes 392 | tf_op jit(solution)/shard_map/ppermute | solution.py:23
  67.4 3.6 %collective-permute-start.23 = (s32[4,8]{1,0:T(4,128)S(1)}, s32[4,8]{1,0:T(4,128)S(1)}, u32[]{:S(2)}, u32[]{:S(2)}) collective-permute-start(s32[4,8]{1,0:T(4,128)S(1)} %pad_add_fusion.refs_0_), channel_id=1, source_target_pairs={{0,16},{8,24},{16,0},{24,8},{1,17},{9,25},{17,1},{25,9},{2,18},{10... | collective-permute-start | bytes 392 | tf_op jit(solution)/shard_map/ppermute | solution.py:23
  71.0 3.6 %collective-permute-start.21 = (s32[4,8]{1,0:T(4,128)S(1)}, s32[4,8]{1,0:T(4,128)S(1)}, u32[]{:S(2)}, u32[]{:S(2)}) collective-permute-start(s32[4,8]{1,0:T(4,128)S(1)} %pad_add_fusion.refs_0_), channel_id=1, source_target_pairs={{0,8},{8,0},{16,24},{24,16},{1,9},{9,1},{17,25},{25,17},{2,10},{10... | collective-permute-start | bytes 392 | tf_op jit(solution)/shard_map/ppermute | solution.py:23
  74.6 4.5 %collective-permute-start.26 = (s32[4,8]{1,0:T(4,128)S(1)}, s32[4,8]{1,0:T(4,128)S(1)}, u32[]{:S(2)}, u32[]{:S(2)}) collective-permute-start(s32[4,8]{1,0:T(4,128)S(1)} %collective-permute-done.3.refs_1_), channel_id=1, source_target_pairs={{0,24},{8,16},{16,8},{24,0},{1,25},{9,17},{17,9},{25,1},{2,26},{10... | collective-permute-start | bytes 392 | tf_op jit(solution)/shard_map/ppermute | solution.py:23
  79.1 3.6 %collective-permute-start.24 = (s32[4,8]{1,0:T(4,128)S(1)}, s32[4,8]{1,0:T(4,128)S(1)}, u32[]{:S(2)}, u32[]{:S(2)}) collective-permute-start(s32[4,8]{1,0:T(4,128)S(1)} %collective-permute-done.3.refs_1_), channel_id=1, source_target_pairs={{0,16},{8,24},{16,0},{24,8},{1,17},{9,25},{17,1},{25,9},{2,18},{10... | collective-permute-start | bytes 392 | tf_op jit(solution)/shard_map/ppermute | solution.py:23
  82.7 3.6 %collective-permute-start.22 = (s32[4,8]{1,0:T(4,128)S(1)}, s32[4,8]{1,0:T(4,128)S(1)}, u32[]{:S(2)}, u32[]{:S(2)}) collective-permute-start(s32[4,8]{1,0:T(4,128)S(1)} %collective-permute-done.3.refs_1_), channel_id=1, source_target_pairs={{0,8},{8,0},{16,24},{24,16},{1,9},{9,1},{17,25},{25,17},{2,10},{10... | collective-permute-start | bytes 392 | tf_op jit(solution)/shard_map/ppermute | solution.py:23
  84.2 5.2 %collective-permute-start.16 = (bf16[64,256]{1,0:T(8,128)(2,1)S(1)}, bf16[64,256]{1,0:T(8,128)(2,1)S(1)}, u32[]{:S(2)}, u32[]{:S(2)}) collective-permute-start(bf16[64,256]{1,0:T(8,128)(2,1)S(1)} %get-tuple-element.24), channel_id=1, source_target_pairs={{0,2},{1,3},{2,0},{3,1},{4,6},{5,7},{6,4},{7,5},{8,10},{9,11},{10,... | collective-permute-start | bytes 98312 | tf_op jit(solution)/shard_map/ppermute | solution.py:23
  86.3 5.0 %collective-permute-start.18 = (bf16[64,1024]{1,0:T(8,128)(2,1)S(1)}, bf16[64,1024]{1,0:T(8,128)(2,1)S(1)}, u32[]{:S(2)}, u32[]{:S(2)}) collective-permute-start(bf16[64,1024]{1,0:T(8,128)(2,1)S(1)} %get-tuple-element.28), channel_id=1, source_target_pairs={{0,2},{1,3},{2,0},{3,1},{4,6},{5,7},{6,4},{7,5},{8,10},{9,11},{10,... | collective-permute-start | bytes 393224 | tf_op jit(solution)/shard_map/ppermute | solution.py:23
  89.3 7.7 %collective-permute-start.19 = (bf16[64,1024]{1,0:T(8,128)(2,1)S(1)}, bf16[64,1024]{1,0:T(8,128)(2,1)S(1)}, u32[]{:S(2)}, u32[]{:S(2)}) collective-permute-start(bf16[64,1024]{1,0:T(8,128)(2,1)S(1)} %get-tuple-element.29), channel_id=1, source_target_pairs={{0,4},{1,5},{2,6},{3,7},{4,0},{5,1},{6,2},{7,3},{8,12},{9,13},{10,... | collective-permute-start | bytes 393224 | tf_op jit(solution)/shard_map/ppermute | solution.py:23
  89.3 9.2 %collective-permute-start.20 = (bf16[64,1024]{1,0:T(8,128)(2,1)S(1)}, bf16[64,1024]{1,0:T(8,128)(2,1)S(1)}, u32[]{:S(2)}, u32[]{:S(2)}) collective-permute-start(bf16[64,1024]{1,0:T(8,128)(2,1)S(1)} %get-tuple-element.30), channel_id=1, source_target_pairs={{0,6},{1,7},{2,4},{3,5},{4,2},{5,3},{6,0},{7,1},{8,14},{9,15},{10,... | collective-permute-start | bytes 393224 | tf_op jit(solution)/shard_map/ppermute | solution.py:23
  91.3 14.7 %collective-permute-start.33 = (bf16[512,128]{1,0:T(8,128)(2,1)S(1)}, bf16[512,128]{1,0:T(8,128)(2,1)S(1)}, u32[]{:S(2)}, u32[]{:S(2)}) collective-permute-start(bf16[512,128]{1,0:T(8,128)(2,1)S(1)} %get-tuple-element.32.refs_0_), channel_id=1, source_target_pairs={{0,24},{8,16},{16,8},{24,0},{1,25},{9,17},{17,9},{25,1},{2,26},{10... | collective-permute-start | bytes 393224 | tf_op jit(solution)/shard_map/ppermute | solution.py:23
  97.0 9.0 %collective-permute-start.30 = (bf16[512,128]{1,0:T(8,128)(2,1)S(1)}, bf16[512,128]{1,0:T(8,128)(2,1)S(1)}, u32[]{:S(2)}, u32[]{:S(2)}) collective-permute-start(bf16[512,128]{1,0:T(8,128)(2,1)S(1)} %get-tuple-element.32.refs_0_), channel_id=1, source_target_pairs={{0,16},{8,24},{16,0},{24,8},{1,17},{9,25},{17,1},{25,9},{2,18},{10... | collective-permute-start | bytes 393224 | tf_op jit(solution)/shard_map/ppermute | solution.py:23
  98.5 7.5 %collective-permute-start.27 = (bf16[512,128]{1,0:T(8,128)(2,1)S(1)}, bf16[512,128]{1,0:T(8,128)(2,1)S(1)}, u32[]{:S(2)}, u32[]{:S(2)}) collective-permute-start(bf16[512,128]{1,0:T(8,128)(2,1)S(1)} %get-tuple-element.32.refs_0_), channel_id=1, source_target_pairs={{0,8},{8,0},{16,24},{24,16},{1,9},{9,1},{17,25},{25,17},{2,10},{10... | collective-permute-start | bytes 393224 | tf_op jit(solution)/shard_map/ppermute | solution.py:23

commit v2 on v1

v2 whole, which is shorter than its diff:
```python
import functools
import math

import jax
import jax.numpy as jnp
from jax import lax
from jax.experimental import pallas as pl
from jax.experimental.pallas import tpu as pltpu
from jax.sharding import PartitionSpec as P

C = 1024
H = 512
DILATION_SIZE = 4
SEG = 8
BF16 = jnp.bfloat16
F32 = jnp.float32
VMEM = pl.BlockSpec(memory_space=pltpu.VMEM)
SMEM = pl.BlockSpec(memory_space=pltpu.SMEM)
ANY = pl.BlockSpec(memory_space=pl.ANY)
HBM = pl.BlockSpec(memory_space=pltpu.HBM)


def swap(value, axis, distance):
    count = lax.axis_size(axis)
    return lax.ppermute(value, axis, [(i, i ^ distance) for i in range(count)])


def exchange(copies, axis):
    return lax.all_to_all(copies, axis, split_axis=0, concat_axis=0, tiled=True)


def call(body, out_shapes, inputs, specs, scratch=(), out_specs=None, after=(), work=2e10, room=12, name=""):
    def run(*refs):
        body(*refs[len(after) :])

    return pl.pallas_call(
        run,
        out_shape=out_shapes,
        in_specs=[ANY] * len(after) + list(specs),
        out_specs=out_specs if out_specs is not None else [VMEM] * len(out_shapes),
        scratch_shapes=list(scratch),
        compiler_params=pltpu.CompilerParams(vmem_limit_bytes=room * 1024 * 1024),
        cost_estimate=pl.CostEstimate(flops=int(work), bytes_accessed=0, transcendentals=0),
    )(*after, *inputs)


def shaped(shape, dtype):
    return jax.ShapeDtypeStruct(shape, dtype)


def roll_half(first, second):
    row = lax.broadcasted_iota(jnp.int32, first.shape, 0)
    return pltpu.roll(jnp.where(row >= 4, first, second), 4, 0)


def pick(me_ref, grad_ref, *outs):
    half = outs[0].shape[1] // 2
    q = lax.rem(me_ref[0], grad_ref.shape[1] // half)
    for pair, out in enumerate(outs):
        for part in range(2):
            start = pl.multiple_of((q ^ (2 * pair + part)) * half, half)
            out[:, part * half : (part + 1) * half] = grad_ref[:, pl.ds(start, half)]


def stack_weight(own_ref, other_ref, out_ref):
    width = own_ref.shape[0]
    for tap in range(3):
        for part, ref in enumerate((own_ref, other_ref)):
            start = (2 * tap + part) * width
            out_ref[start : start + width, :] = ref[:, tap * C : (tap + 1) * C]


def place(source, seg_count, chips, me):
    apart = (source // seg_count) ^ me
    return ((apart & 1) * chips + (apart >> 1)) * seg_count + lax.rem(source, seg_count)


def find_follows(chips, me, source, follow_ref, table):
    peers = 2 * chips
    segments = follow_ref.shape[1]
    seg_count = segments // peers
    for i in range(segments):
        follow_ref[table, i] = segments * SEG
    for peer in range(peers):
        slot = place(peer * seg_count, seg_count, chips, me)
        for position in range(seg_count):
            found = source(peer, position)

            @pl.when(found >= 0)
            def _():
                follow_ref[table, place(found, seg_count, chips, me)] = (slot + position) * SEG


def follows(chips, me_ref, table_ref, follow_ref):
    find_follows(chips, me_ref[0], lambda peer, position: table_ref[peer, position], follow_ref, 0)


def far_follows(chips, me_ref, *refs):
    blocks, (follow_ref, raw_ref, wide_ref, table_ref, sems) = refs[:-5], refs[-5:]
    count = len(blocks)
    seg_count = follow_ref.shape[1] // (2 * chips)
    loads = []
    for i, block in enumerate(blocks):
        rows = pl.ds(block.shape[0] - 16, 16)
        loads.append(pltpu.make_async_copy(block.at[rows, pl.ds(0, 128)], raw_ref.at[i], sems.at[i]))
        loads[-1].start()
    for load in loads:
        load.wait()
    wide_ref[...] = raw_ref[...].astype(F32).astype(jnp.int32)
    moved = pltpu.make_async_copy(wide_ref, table_ref, sems.at[0])
    moved.start()
    moved.wait()

    def one(table, carry):
        find_follows(
            chips,
            me_ref[0],
            lambda peer, position: table_ref[table, 0, peer * seg_count + position],
            follow_ref,
            table,
        )
        return carry

    lax.fori_loop(0, count, one, 0)


def stack(table_ref, *refs):
    blocks, (rows_ref, copy_ref) = refs[:-2], refs[-2:]
    count = blocks[0].shape[0]
    for slot, block in enumerate(blocks):
        rows_ref[slot * count : (slot + 1) * count, :] = block[...]
        copy_ref[slot * count : (slot + 1) * count, :] = block[...]
    peers, seg_count = table_ref.shape
    lane = lax.broadcasted_iota(jnp.int32, (16, 128), 1)
    value = jnp.zeros((16, 128), jnp.int32)
    for peer in range(peers):
        for position in range(seg_count):
            value = jnp.where(lane == peer * seg_count + position, table_ref[peer, position], value)
    total = rows_ref.shape[0]
    copy_ref[total:, :] = jnp.zeros((16, C), BF16)
    copy_ref[total:, :128] = value.astype(F32).astype(BF16)


def forward(me_ref, table_ref, weight_ref, own_ref, other_ref, grad_ref, act_ref, sent_ref, rows_ref, early_ref):
    own_class = own_ref.shape[0]
    peers, seg_count = table_ref.shape
    me = me_ref[0]
    rows_ref[:own_class, :] = own_ref[...]
    rows_ref[own_class:, :] = other_ref[...]
    total = 2 * own_class
    wide = weight_ref.shape[0] // 3
    nt = (((1,), (1,)), ((), ()))
    early_ref[:total, :] = lax.dot_general(
        rows_ref[...], weight_ref[: 2 * wide, :], nt, preferred_element_type=F32
    )
    early_ref[total:, :] = jnp.zeros((SEG, 2 * wide), F32)
    act_ref[...] = lax.dot_general(
        rows_ref[:own_class, :], weight_ref[2 * wide :, :], nt, preferred_element_type=F32
    )
    is_filter = me_ref[0] < me_ref[1]
    for segment in range(own_class // SEG):
        at = segment * SEG
        source = table_ref[me ^ (2 * (segment // seg_count)), segment % seg_count]
        found = place(jnp.maximum(source, 0), seg_count, peers // 2, me)
        source = pl.multiple_of(jnp.where(source >= 0, found * SEG, total), SEG)
        carried = early_ref[pl.ds(source, SEG), :]
        preact = (
            act_ref[at : at + SEG, :]
            + carried[:, :wide]
            + roll_half(carried[:, wide:], early_ref[at : at + SEG, wide:])
        )
        act_ref[at : at + SEG, :] = jnp.where(is_filter, jnp.tanh(preact), jax.nn.sigmoid(preact))
    sent_ref[:own_class, :] = act_ref[...].astype(BF16)
    sent_ref[own_class:, :] = grad_ref[...]


def gate(me_ref, act_ref, other_ref, *refs):
    grads, outs, pre_ref = list(refs[:-3]), refs[-3:-1], refs[-1]
    count = outs[0].shape[0]
    is_filter = me_ref[0] < me_ref[1]
    slots = len(grads) + 1
    grads.insert(slots // 2, other_ref.at[slots * count :, :])
    for slot, grad in enumerate(grads):
        at = slot * count
        there = (slot ^ (slots // 2)) * count
        mine = act_ref[at : at + count, :]
        theirs = other_ref[there : there + count, :].astype(F32)
        upstream = grad[...].astype(F32)
        if slot < len(outs):
            outs[slot][...] = (mine * theirs).astype(BF16)
        for_filter = upstream * theirs * (1.0 - mine * mine)
        for_gate = upstream * theirs * mine * (1.0 - mine)
        pre_ref[at : at + count, :] = jnp.where(is_filter, for_filter, for_gate).astype(BF16)


def input_grad(follow_ref, own_ref, other_ref, weight_ref, gated_ref, *refs):
    sends, here_ref, pre_ref, routed_ref = refs[:-3], refs[-3], refs[-2], refs[-1]
    total, wide = own_ref.shape
    width = wide // 2
    pre_ref[:total, :] = own_ref[...].astype(F32)
    pre_ref[total : 2 * total, :width] = other_ref[:, width:].astype(F32)
    pre_ref[total : 2 * total, width:] = other_ref[:, :width].astype(F32)
    pre_ref[2 * total :, :] = jnp.zeros((SEG, wide), F32)
    for segment in range(total // SEG):
        at = segment * SEG
        follow = pl.multiple_of(follow_ref[0, segment], SEG)
        carried = pre_ref[pl.ds(follow, SEG), :]
        local = pre_ref[at : at + SEG, :]
        routed_ref[at : at + SEG, :wide] = carried
        routed_ref[at : at + SEG, wide : 2 * wide] = roll_half(local, carried)
        routed_ref[at : at + SEG, 2 * wide :] = local
    count = here_ref.shape[0]
    fold = C // wide
    for i in range(fold):
        piece = gated_ref[i * (count // fold) : (i + 1) * (count // fold), :]
        sends[0][count:, i * wide : (i + 1) * wide] = piece
    routed = routed_ref[...].astype(BF16)
    here_ref[...] = routed[:count, :]
    part = jnp.dot(routed[count:, :], weight_ref[...], preferred_element_type=F32)
    for slot, out in enumerate(sends):
        out[:count, :] = part[slot * count : (slot + 1) * count, :].astype(BF16)


def spread(own_ref, other_ref, copies_ref):
    total, wide = own_ref.shape
    width = wide // 2
    for copy in range(copies_ref.shape[0]):
        copies_ref[copy, :total, :] = own_ref[:, :width]
        copies_ref[copy, total:, :] = other_ref[:, width:]


def nothing(*refs):
    pass


def held(values, after):
    return pl.pallas_call(
        nothing,
        out_shape=[shaped(value.shape, value.dtype) for value in values],
        in_specs=[ANY] * (len(values) + len(after)),
        out_specs=[ANY] * len(values),
        input_output_aliases={i: i for i in range(len(values))},
        compiler_params=pltpu.CompilerParams(vmem_limit_bytes=2**20),
        cost_estimate=pl.CostEstimate(flops=10**10, bytes_accessed=0, transcendentals=0),
    )(*values, *after)


def weight_grad(which, scale, group_ref, follow_ref, *refs):
    first_ref = refs[0] if len(which) > 1 else None
    sent_pre_ref = refs[-5 - 2 * len(which)]
    signals = refs[-4 - 2 * len(which) : -4]
    out_ref, pre_ref, routed_ref, rows_ref = refs[-4:]
    total = pre_ref.shape[0] - SEG
    width = pre_ref.shape[1]
    pre_ref[total:, :] = jnp.zeros((SEG, width), F32)
    for i, distance in enumerate(which):
        base = i * total
        pre_ref[:total, :] = sent_pre_ref[group_ref[0] ^ distance].astype(F32)
        rows_ref[base : base + total // 2, :] = signals[2 * i][: total // 2, :]
        rows_ref[base + total // 2 : base + total, :] = signals[2 * i + 1][: total // 2, :]
        for segment in range(total // SEG):
            at = segment * SEG
            follow = pl.multiple_of(follow_ref[i, segment], SEG)
            carried = pre_ref[pl.ds(follow, SEG), :]
            local = pre_ref[at : at + SEG, :]
            at += base
            routed_ref[at : at + SEG, :width] = carried
            routed_ref[at : at + SEG, width : 2 * width] = roll_half(local, carried)
            routed_ref[at : at + SEG, 2 * width :] = local
    product = lax.dot_general(
        routed_ref[...].astype(BF16), rows_ref[...], (((0,), (0,)), ((), ())), preferred_element_type=F32
    )
    for tap in range(3):
        here = slice(tap * C, (tap + 1) * C)
        value = product[tap * width : (tap + 1) * width, :]
        if first_ref is not None:
            value = (value + first_ref[:, here]) * scale
        out_ref[:, here] = value


def finish(me_ref, here_ref, weight_ref, gated_ref, *refs):
    parts, (grad_ref, out_ref) = refs[:-2], refs[-2:]
    count = grad_ref.shape[0]
    total = jnp.dot(here_ref[...], weight_ref[...], preferred_element_type=F32)
    for part in parts:
        total = total + part[:count, :].astype(F32)
    grad_ref[...] = total.astype(BF16)
    wide = gated_ref.shape[1]
    width = wide // 2
    fold = C // wide
    short = count // fold
    q = lax.rem(me_ref[0], out_ref.shape[1] // width)
    for part in range(2):
        here = slice(part * width, (part + 1) * width)
        out_ref[:, pl.ds(pl.multiple_of((q ^ part) * width, width), width)] = gated_ref[:, here]
        start = pl.multiple_of((q ^ (2 + part)) * width, width)
        for i in range(fold):
            piece = parts[0][count:, i * wide + part * width : i * wide + (part + 1) * width]
            out_ref[i * short : (i + 1) * short, pl.ds(start, width)] = piece


def by_channels(signal, grad_gated, conv_weight, source_seg):
    peers, groups = lax.axis_size("fsdp"), lax.axis_size("dp")
    chips = peers // 2
    seg_count = source_seg.shape[1]
    rows, width = signal.shape[0], conv_weight.shape[0]
    own_class, all_rows = chips * rows, peers * rows
    wide = 2 * width
    half_chips = chips // 2
    me = lax.axis_index("fsdp").astype(jnp.int32)
    group = lax.axis_index("dp").astype(jnp.int32)
    who = jnp.stack([me, jnp.int32(peers // 2)])

    fold = C // wide
    own_rows = [signal] + [swap(signal, "fsdp", 2 * k) for k in range(1, chips)]
    picked = call(
        pick, [shaped((rows, wide), BF16)] * half_chips, [who, grad_gated], [SMEM, VMEM], name="pick"
    )
    other_weight = swap(conv_weight, "fsdp", 1)
    weight = call(
        stack_weight, [shaped((3 * wide, C), BF16)], [conv_weight, other_weight], [VMEM] * 2, name="wstack"
    )[0]
    table = exchange(jnp.broadcast_to(source_seg[None], (peers, 1, seg_count)), "fsdp").reshape(peers, seg_count)
    own_stack, own_copy = call(
        stack,
        [shaped((own_class, C), BF16), shaped((own_class + 16, C), BF16)],
        [table, *own_rows],
        [SMEM] + [VMEM] * chips,
        name="stack",
    )
    other_stack = swap(own_stack, "fsdp", 1)
    act, sent = call(
        forward,
        [shaped((own_class, wide), F32), shaped((own_class + rows, wide), BF16)],
        [who, table, weight, own_stack, other_stack, picked[0]],
        [SMEM, SMEM] + [VMEM] * 4,
        [pltpu.VMEM((all_rows, C), BF16), pltpu.VMEM((all_rows + SEG, 2 * wide), F32)],
        name="forward",
    )
    partner = swap(sent, "fsdp", peers // 2)
    grads = [picked[0], swap(picked[1], "fsdp", 2), swap(picked[1], "fsdp", 6)]

    follow = call(
        functools.partial(follows, chips),
        [shaped((1, peers * seg_count), jnp.int32)],
        [who, table],
        [SMEM, SMEM],
        out_specs=[SMEM],
        after=[sent],
        name="follow",
    )[0]
    far_own = [swap(own_copy, "dp", d) for d in (1, 2)]
    *far_own, own_copy = held([*far_own, own_copy], [follow])
    last_own = swap(own_copy, "dp", 3)
    far_other = [swap(block, "fsdp", 1) for block in far_own]

    *gated, pre = call(
        gate,
        [shaped((rows, wide), BF16)] * half_chips + [shaped((own_class, wide), BF16)],
        [who, act, partner, *grads],
        [SMEM] + [VMEM] * (2 + len(grads)),
        after=[own_copy],
        name="gate",
    )
    other_pre = swap(pre, "fsdp", 1)
    *sends, here = call(
        input_grad,
        [shaped((rows + rows // fold, C), BF16)]
        + [shaped((rows, C), BF16)] * (chips - 2)
        + [shaped((rows, 3 * wide), BF16)],
        [follow, pre, other_pre, weight, gated[1]],
        [SMEM, VMEM, VMEM, VMEM, VMEM],
        [pltpu.VMEM((all_rows + SEG, wide), F32), pltpu.VMEM((own_class, 3 * wide), F32)],
        after=far_other,
        name="input",
    )
    parts = [swap(part, "fsdp", 2 * (k + 1)) for k, part in enumerate(sends)]
    sent_pre = call(
        spread, [shaped((groups, all_rows, width), BF16)], [pre, other_pre], [VMEM] * 2, after=[here], name="spread"
    )[0]
    far_pre = exchange(sent_pre, "dp")

    def grads_of(which, found, inputs, first, name):
        count = len(which)
        return call(
            functools.partial(weight_grad, which, 1.0 / math.sqrt(all_rows * groups)),
            [shaped((width, 3 * C), F32)],
            [group[None], found, *first, *inputs],
            [SMEM, SMEM] + [VMEM] * (len(inputs) + len(first)),
            [
                pltpu.VMEM((all_rows + SEG, width), F32),
                pltpu.VMEM((count * all_rows, 3 * width), F32),
                pltpu.VMEM((count * all_rows, C), BF16),
            ],
            room=24,
            name=name,
        )[0]

    near = grads_of([0], follow, [sent_pre, own_stack, other_stack], [], "near")
    last_own = held([last_own], [near])[0]
    far_own.append(last_own)
    far_other.append(swap(last_own, "fsdp", 1))
    far_follow = call(
        functools.partial(far_follows, chips),
        [shaped((groups - 1, peers * seg_count), jnp.int32)],
        [who, *far_own],
        [SMEM] + [ANY] * len(far_own),
        [
            pltpu.VMEM((groups - 1, 16, 128), BF16),
            pltpu.VMEM((groups - 1, 16, 128), jnp.int32),
            pltpu.SMEM((groups - 1, 16, 128), jnp.int32),
            pltpu.SemaphoreType.DMA((groups - 1,)),
        ],
        out_specs=[SMEM],
        name="farfollow",
    )[0]
    grad_in, gated_out = call(
        finish,
        [shaped((rows, C), BF16), shaped((rows, H), BF16)],
        [who, here, weight, gated[0], *parts],
        [SMEM] + [VMEM] * (chips + 2),
        name="finish",
    )
    far_signals = [block for pair in zip(far_own, far_other) for block in pair]
    grad_weight = grads_of(list(range(1, groups)), far_follow, [far_pre, *far_signals], [near], "far")
    return gated_out, grad_in, grad_weight


def tap_starts(context_row_block):
    return [context_row_block - (2 - selected_index) * DILATION_SIZE for selected_index in range(3)]


def by_rows(signal, grad_gated, conv_weight, source_seg):
    peer_count = lax.axis_size("fsdp")
    seg_count = source_seg.shape[1]
    row_count = signal.shape[0]
    seg_rows = row_count // seg_count
    context_row_block = 2 * DILATION_SIZE
    starts = tap_starts(context_row_block)
    segments = signal.reshape(seg_count, seg_rows, C)
    sources = source_seg[0]
    source_dev = jnp.where(sources >= 0, sources // seg_count, -1)
    peers = jnp.arange(peer_count, dtype=jnp.int32)
    request_mask = (source_dev[None, :] == peers[:, None]).astype(jnp.int32)
    asked = lax.all_to_all(request_mask, "fsdp", split_axis=0, concat_axis=0, tiled=True)
    send_table = asked.astype(jnp.bfloat16)
    recv_table = (source_dev[:, None] == peers[None, :]).astype(jnp.bfloat16)
    outgoing = jnp.einsum(
        "ns,slc->nlc", send_table, segments, preferred_element_type=jnp.float32
    ).astype(jnp.bfloat16)
    incoming = lax.all_to_all(outgoing, "fsdp", split_axis=0, concat_axis=0, tiled=True)
    carries = jnp.einsum(
        "sn,nlc->slc", recv_table, incoming, preferred_element_type=jnp.float32
    ).astype(jnp.bfloat16)
    extended = jnp.concatenate([carries, segments], axis=1)
    full_weight = lax.all_gather(conv_weight, "fsdp", axis=0, tiled=True)
    contract_final_axis = (((1,), (1,)), ((), ()))
    contract_first = (((0,), (0,)), ((), ()))
    windows = [extended[:, start : start + seg_rows, :].reshape(row_count, C) for start in starts]
    preact = sum(
        (
            lax.dot_general(
                windows[selected_index],
                full_weight[:, selected_index * C : (selected_index + 1) * C],
                contract_final_axis,
                preferred_element_type=jnp.float32,
            )
            for selected_index in range(3)
        )
    )
    filter_act = jnp.tanh(preact[:, :H])
    gate_act = jax.nn.sigmoid(preact[:, H:])
    gated_out = (filter_act * gate_act).astype(jnp.bfloat16)
    upstream_wide = grad_gated.astype(jnp.float32)
    grad_pre = jnp.concatenate(
        [
            upstream_wide * gate_act * (1.0 - filter_act * filter_act),
            upstream_wide * filter_act * gate_act * (1.0 - gate_act),
        ],
        axis=1,
    ).astype(jnp.bfloat16)
    partial_value = jnp.concatenate(
        [
            lax.dot_general(
                grad_pre,
                windows[selected_index],
                contract_first,
                preferred_element_type=jnp.float32,
            ).astype(jnp.bfloat16)
            for selected_index in range(3)
        ],
        axis=1,
    )
    arrived = lax.all_to_all(partial_value, "fsdp", split_axis=0, concat_axis=0, tiled=True)
    shard_sum = jnp.sum(arrived.reshape(peer_count, -1, 3 * C), axis=0, dtype=jnp.float32)
    group_total = lax.psum(shard_sum, "dp")
    total_token_count = row_count * peer_count * lax.axis_size("dp")
    grad_weight = group_total * (1.0 / math.sqrt(total_token_count))
    back_proj = jnp.dot(grad_pre, full_weight, preferred_element_type=jnp.float32)
    back_proj = back_proj.reshape(seg_count, seg_rows, 3 * C)
    grad_ext = jnp.zeros((seg_count, context_row_block + seg_rows, C), jnp.float32)
    for selected_index, start in enumerate(starts):
        grad_ext = grad_ext.at[:, start : start + seg_rows, :].add(
            back_proj[:, :, selected_index * C : (selected_index + 1) * C]
        )
    outgoing_grad = jnp.einsum(
        "sn,slc->nlc",
        recv_table.astype(jnp.float32),
        grad_ext[:, :context_row_block, :],
        precision=lax.Precision.HIGHEST,
    )
    incoming_grad = lax.all_to_all(outgoing_grad, "fsdp", split_axis=0, concat_axis=0, tiled=True)
    tail_grad = jnp.einsum(
        "ns,nlc->slc",
        send_table.astype(jnp.float32),
        incoming_grad,
        precision=lax.Precision.HIGHEST,
    )
    grad_in = (
        grad_ext[:, context_row_block:, :].at[:, seg_rows - context_row_block :, :].add(tail_grad)
    )
    grad_in = grad_in.reshape(row_count, C).astype(jnp.bfloat16)
    return (gated_out, grad_in, grad_weight)


def per_device(signal, grad_gated, conv_weight, source_seg):
    peers, groups = lax.axis_size("fsdp"), lax.axis_size("dp")
    rows, seg_count = signal.shape[0], source_seg.shape[1]
    fits = (
        rows == SEG * seg_count
        and conv_weight.shape[0] % 128 == 0
        and peers & (peers - 1) == 0
        and groups & (groups - 1) == 0
        and peers == 8
        and groups == 4
        and groups * peers * rows <= 2048
        and rows % 64 == 0
        and peers * seg_count <= 128
    )
    plan = by_channels if fits else by_rows
    return plan(signal, grad_gated, conv_weight, source_seg)


def solution(mesh):
    placed = (
        P(("dp", "fsdp"), None),
        P(("dp", "fsdp"), None),
        P("fsdp", None),
        P(("dp", "fsdp"), None),
    )
    return jax.shard_map(
        per_device,
        mesh=mesh,
        in_specs=placed,
        out_specs=(P(("dp", "fsdp"), None), P(("dp", "fsdp"), None), P("fsdp", None)),
        check_vma=False,
    )
```

time: 110 us -> 68.5 us (0.62)
  waiting for transfers between devices: 47.7 us -> 11.3 us
  starting transfers between devices: 38.3 us -> 27.9 us
  Pallas kernels: 16.3 us -> 20 us
  local copies, waits for them, and re-layouts: 5.77 us -> 7.79 us
    ppermute x36 -> x18, waiting for transfers between devices: 47.7 us -> 11.2 us  [swap(): return lax.ppermute(value, axis, [(i, i ^ distance) for i in range(count)])]
    ppermute x36 -> x18, starting transfers between devices: 38.3 us -> 19.4 us  [swap(): return lax.ppermute(value, axis, [(i, i ^ distance) for i in range(count)])]
    all_to_all x0 -> x2, starting transfers between devices: none -> 8.57 us  [exchange(): return lax.all_to_all(copies, axis, split_axis=0, concat_axis=0, tiled=True)]
    pallas_call x11 -> x14, Pallas kernels: 16.3 us -> 20 us  [the longest x12 20 us: call(): pl.pallas_call(run, out_shape=out_shapes, in_specs=[ANY] * len(after) + l...]
    unnamed x17 -> x28, local copies, waits for them, and re-layouts: 5.11 us -> 6.54 us
    broadcast_in_dim x0 -> x1, local copies, waits for them, and re-layouts: none -> 1.25 us  [by_channels(): jnp.broadcast_to(source_seg[None], (peers, 1, seg_count))]
  transfers between devices with their start and end apart: 36 -> 20, of which waited for: 18 -> 6; matrix products, arithmetic and copies ran while one was open for 4% -> 2% of each run, Pallas kernels for 11% -> 24%
where the time goes in v2:
time: 68.5 us; the launch traced here: 67.9 us
  starting transfers between devices  27.9 us (41%)
  Pallas kernels  20 us (29%)
  waiting for transfers between devices  11.3 us (16%)
  local copies, waits for them, and re-layouts  7.79 us (11%)
  between operations  0.87 us (1%)
    pallas_call x12, Pallas kernels, call(): pl.pallas_call(run, out_shape=out_shapes, in_specs=[ANY] * len(after) + l...  20 us
    ppermute x18, starting transfers between devices, swap(): return lax.ppermute(value, axis, [(i, i ^ distance) for i in range(count)])  19.4 us
    ppermute x18, waiting for transfers between devices, swap(): return lax.ppermute(value, axis, [(i, i ^ distance) for i in range(count)])  11.2 us
    all_to_all x2, starting transfers between devices, exchange(): return lax.all_to_all(copies, axis, split_axis=0, concat_axis=0, tiled=True)  8.57 us
    unnamed x28, local copies, waits for them, and re-layouts  6.54 us
  transfers between devices with their start and end apart: 20, of which 6 were waited for; matrix products, arithmetic and copies ran while one was open for 2% of the time, Pallas kernels for 24%

profile of v2, /device:TPU:0, one launch (start us, length us, event | category | flops | bytes accessed | tf_op | source)
XLA Modules:
  0.0 67.9 jit_solution(5888839204480932631)
XLA Ops:
  0.6 4.1 %collective-permute-start.1 = (bf16[64,1024]{1,0:T(8,128)(2,1)}, bf16[64,1024]{1,0:T(8,128)(2,1)S(1)}, u32[]{:S(2)}, u32[]{:S(2)}) collective-permute-start(bf16[64,1024]{1,0:T(8,128)(2,1)} %refs_1_.2), channel_id=1, source_target_pairs={{0,4},{1,5},{2,6},{3,7},{4,0},{5,1},{6,2},{7,3},{8,12},{9,13},{10,... | collective-permute-start | bytes 393224 | tf_op jit(solution)/shard_map/ppermute | solution.py:25
  4.7 1.6 %collective-permute-start = (bf16[64,1024]{1,0:T(8,128)(2,1)}, bf16[64,1024]{1,0:T(8,128)(2,1)S(1)}, u32[]{:S(2)}, u32[]{:S(2)}) collective-permute-start(bf16[64,1024]{1,0:T(8,128)(2,1)} %refs_1_.2), channel_id=1, source_target_pairs={{0,2},{1,3},{2,0},{3,1},{4,6},{5,7},{6,4},{7,5},{8,10},{9,11},{10,... | collective-permute-start | bytes 393224 | tf_op jit(solution)/shard_map/ppermute | solution.py:25
  6.3 0.0 collective-permute-start.2
  6.3 1.2 %broadcast_in_dim.13 = s32[8,1,8]{2,1,0:T(1,128)} broadcast(s32[8]{0:T(128)} %bitcast.7), dimensions={2} | broadcast | bytes 288 | tf_op jit(solution)/shard_map/broadcast_in_dim | solution.py:323
  7.6 5.1 %all-to-all-start = ((s32[8,1,8]{2,1,0:T(1,128)}), s32[8,1,8]{2,1,0:T(1,128)S(1)}, u32[]{:S(2)}, u32[]{:S(2)}) async-start(s32[8,1,8]{2,1,0:T(1,128)} %broadcast_in_dim.13), calls=%async_computation | async-start | bytes 8192 | tf_op jit(solution)/shard_map/all_to_all | solution.py:29
  12.7 0.1 pad_add_fusion.refs_0_.refs_1_
  12.7 0.8 %copy-done.6 = bf16[64,512]{1,0:T(8,128)(2,1)S(1)} copy-done((bf16[64,512]{1,0:T(8,128)(2,1)S(1)}, bf16[64,512]{1,0:T(8,128)(2,1)}, u32[]{:S(2)}) %copy-start.6) | copy-done | bytes 65560
  13.6 0.6 shard_map.69
  14.1 3.9 %collective-permute-start.11 = (bf16[64,256]{1,0:T(8,128)(2,1)S(1)}, bf16[64,256]{1,0:T(8,128)(2,1)S(1)}, u32[]{:S(2)}, u32[]{:S(2)}) collective-permute-start(bf16[64,256]{1,0:T(8,128)(2,1)S(1)} %get-tuple-element.29), channel_id=1, source_target_pairs={{0,6},{1,7},{2,4},{3,5},{4,2},{5,3},{6,0},{7,1},{8,14},{9,15},{10,... | collective-permute-start | bytes 98312 | tf_op jit(solution)/shard_map/ppermute | solution.py:25
  18.0 0.0 collective-permute-start.10
  18.0 0.0 collective-permute-done.1.refs_3_
  18.0 0.0 copy-done
  18.0 0.1 collective-permute-start.5
  18.1 0.0 all-to-all-done
  18.1 0.0 collective-permute-done.refs_2_
  18.1 0.0 collective-permute-done.2.refs_4_
  18.2 0.7 %shard_map.67 = (bf16[256,1024]{1,0:T(8,128)(2,1)S(1)}, bf16[272,1024]{1,0:T(8,128)(2,1)S(1)}) custom-call(s32[8,8]{1,0:T(8,128)S(1)} %bitcast.4, bf16[64,1024]{1,0:T(8,128)(2,1)S(1)} %copy-done.5, bf16[64,1024]{1,0:T(8,128)(2,1)S(1)} %collective-permute-done.refs_2_, bf16[64,1024]{1,0:T(8,128)(2,1)S(1)} %collective-permute-done.1.refs_3_, ...), custom_call_target="tpu_custom_call" | custom-call | flops 20000000000 | tf_op jit(solution)/shard_map/pallas_call | solution.py:36
  18.9 0.0 copy-start.1
  18.9 1.6 %collective-permute-start.4 = (bf16[272,1024]{1,0:T(8,128)(2,1)S(1)}, bf16[272,1024]{1,0:T(8,128)(2,1)S(1)}, u32[]{:S(2)}, u32[]{:S(2)}) collective-permute-start(bf16[272,1024]{1,0:T(8,128)(2,1)S(1)} %get-tuple-element.21.refs_2_), channel_id=1, source_target_pairs={{0,16},{8,24},{16,0},{24,8},{1,17},{9,25},{17,1},{25,9},{2,18},{10... | collective-permute-start | bytes 1671176 | tf_op jit(solution)/shard_map/ppermute | solution.py:25
  20.5 1.5 %collective-permute-start.3 = (bf16[272,1024]{1,0:T(8,128)(2,1)S(1)}, bf16[272,1024]{1,0:T(8,128)(2,1)}, u32[]{:S(2)}, u32[]{:S(2)}) collective-permute-start(bf16[272,1024]{1,0:T(8,128)(2,1)S(1)} %get-tuple-element.21.refs_2_), channel_id=1, source_target_pairs={{0,8},{8,0},{16,24},{24,16},{1,9},{9,1},{17,25},{25,17},{2,10},{10... | collective-permute-start | bytes 1671176 | tf_op jit(solution)/shard_map/ppermute | solution.py:25
  21.9 0.0 collective-permute-done.5.refs_1_
  21.9 0.0 collective-permute-start.6
  22.0 0.1 shard_map.68.refs_2_.refs_5_
  22.1 0.0 copy-start.9
  22.1 1.8 %collective-permute-done.6.refs_4_ = bf16[256,1024]{1,0:T(8,128)(2,1)S(1)} collective-permute-done((bf16[256,1024]{1,0:T(8,128)(2,1)S(1)}, bf16[256,1024]{1,0:T(8,128)(2,1)S(1)}, u32[]{:S(2)}, u32[]{:S(2)}) %collective-permute-start.6) | collective-permute-done | bytes 524320 | tf_op jit(solution)/shard_map/ppermute | solution.py:25
  23.9 1.6 %shard_map.70 = (f32[256,256]{1,0:T(8,128)S(1)}, bf16[320,256]{1,0:T(8,128)(2,1)S(1)}) custom-call(s32[2]{0:T(128)S(1)} %pad_add_fusion.refs_0_.refs_1_, s32[8,8]{1,0:T(8,128)S(1)} %bitcast.5, bf16[768,1024]{1,0:T(8,128)(2,1)S(1)} %shard_map.68.refs_2_.refs_5_, bf16[256,1024]{1,0:T(8,128)(2,1)S(1)} %get-tuple-element.22.refs_3_, ...), custom_call_target="tpu_custom_call" | custom-call | flops 20000000000 | tf_op jit(solution)/shard_map/pallas_call | solution.py:36
  25.5 0.0 copy-done.9
  25.5 1.7 %shard_map.71.refs_3_.refs_2_.refs_1_ = s32[1,64]{1,0:T(1,128)S(1)} custom-call(bf16[320,256]{1,0:T(8,128)(2,1)S(1)} %get-tuple-element.24.refs_0_, s32[2]{0:T(128)S(1)} %pad_add_fusion.refs_0_.refs_1_, s32[8,8]{1,0:T(8,128)S(1)} %bitcast.6), custom_call_target="tpu_custom_call" | custom-call | flops 20000000000 | tf_op jit(solution)/shard_map/pallas_call | solution.py:36
  27.2 1.5 %collective-permute-start.9 = (bf16[320,256]{1,0:T(8,128)(2,1)S(1)}, bf16[320,256]{1,0:T(8,128)(2,1)S(1)}, u32[]{:S(2)}, u32[]{:S(2)}) collective-permute-start(bf16[320,256]{1,0:T(8,128)(2,1)S(1)} %get-tuple-element.24.refs_0_), channel_id=1, source_target_pairs={{0,4},{1,5},{2,6},{3,7},{4,0},{5,1},{6,2},{7,3},{8,12},{9,13},{10,... | collective-permute-start | bytes 491528 | tf_op jit(solution)/shard_map/ppermute | solution.py:25
  28.8 5.2 %collective-permute-done.4.refs_1_ = bf16[272,1024]{1,0:T(8,128)(2,1)S(1)} collective-permute-done((bf16[272,1024]{1,0:T(8,128)(2,1)S(1)}, bf16[272,1024]{1,0:T(8,128)(2,1)S(1)}, u32[]{:S(2)}, u32[]{:S(2)}) %collective-permute-start.4) | collective-permute-done | bytes 557088 | tf_op jit(solution)/shard_map/ppermute | solution.py:25
  33.9 1.3 %collective-permute-done.3.refs_0_ = bf16[272,1024]{1,0:T(8,128)(2,1)} collective-permute-done((bf16[272,1024]{1,0:T(8,128)(2,1)S(1)}, bf16[272,1024]{1,0:T(8,128)(2,1)}, u32[]{:S(2)}, u32[]{:S(2)}) %collective-permute-start.3) | collective-permute-done | bytes 557088 | tf_op jit(solution)/shard_map/ppermute | solution.py:25
  35.3 0.0 collective-permute-start.7
  35.3 0.5 collective-permute-start.8
  35.8 0.0 collective-permute-done.11.refs_6_
  35.8 0.0 collective-permute-done.10.refs_5_
  35.8 2.2 %collective-permute-done.9.refs_3_ = bf16[320,256]{1,0:T(8,128)(2,1)S(1)} collective-permute-done((bf16[320,256]{1,0:T(8,128)(2,1)S(1)}, bf16[320,256]{1,0:T(8,128)(2,1)S(1)}, u32[]{:S(2)}, u32[]{:S(2)}) %collective-permute-start.9) | collective-permute-done | bytes 163872 | tf_op jit(solution)/shard_map/ppermute | solution.py:25
  38.0 0.6 shard_map.73
  38.6 0.1 collective-permute-start.12
  38.7 1.0 %collective-permute-start.16 = (bf16[272,1024]{1,0:T(8,128)(2,1)S(1)}, bf16[272,1024]{1,0:T(8,128)(2,1)S(1)}, u32[]{:S(2)}, u32[]{:S(2)}) collective-permute-start(bf16[272,1024]{1,0:T(8,128)(2,1)S(1)} %get-tuple-element.27.refs_0_), channel_id=1, source_target_pairs={{0,24},{8,16},{16,8},{24,0},{1,25},{9,17},{17,9},{25,1},{2,26},{10... | collective-permute-start | bytes 1671176 | tf_op jit(solution)/shard_map/ppermute | solution.py:25
  39.6 0.4 collective-permute-done.12.refs_4_.refs_2_
  40.0 0.0 collective-permute-done.7.refs_0_.refs_5_
  40.0 0.0 collective-permute-done.8.refs_1_.refs_7_
  40.0 1.4 %copy-done.10 = bf16[768,1024]{1,0:T(8,128)(2,1)S(1)} copy-done((bf16[768,1024]{1,0:T(8,128)(2,1)S(1)}, bf16[768,1024]{1,0:T(8,128)(2,1)}, u32[]{:S(2)}) %copy-start.10) | copy-done | bytes 1572888
  41.4 1.7 %shard_map.74 = (bf16[80,1024]{1,0:T(8,128)(2,1)S(1)}, bf16[64,1024]{1,0:T(8,128)(2,1)}, bf16[64,1024]{1,0:T(8,128)(2,1)}, bf16[64,768]{1,0:T(8,128)(2,1)S(1)}) custom-call(bf16[272,1024]{1,0:T(8,128)(2,1)S(1)} %collective-permute-done.7.refs_0_.refs_5_, bf16[272,1024]{1,0:T(8,128)(2,1)S(1)} %collective-permute-done.8.refs_1_.refs_7_, ...), custom_call_target="tpu_custom_call" | custom-call | flops 20000000000 | tf_op jit(solution)/shard_map/pallas_call | solution.py:36
  43.2 0.0 collective-permute-start.14
  43.2 2.5 %collective-permute-start.15 = (bf16[64,1024]{1,0:T(8,128)(2,1)}, bf16[64,1024]{1,0:T(8,128)(2,1)}, u32[]{:S(2)}, u32[]{:S(2)}) collective-permute-start(bf16[64,1024]{1,0:T(8,128)(2,1)} %get-tuple-element.36), channel_id=1, source_target_pairs={{0,6},{1,7},{2,4},{3,5},{4,2},{5,3},{6,0},{7,1},{8,14},{9,15},{10,... | collective-permute-start | bytes 393224 | tf_op jit(solution)/shard_map/ppermute | solution.py:25
  45.7 1.0 %collective-permute-start.13 = (bf16[80,1024]{1,0:T(8,128)(2,1)S(1)}, bf16[80,1024]{1,0:T(8,128)(2,1)}, u32[]{:S(2)}, u32[]{:S(2)}) collective-permute-start(bf16[80,1024]{1,0:T(8,128)(2,1)S(1)} %get-tuple-element.34), channel_id=1, source_target_pairs={{0,2},{1,3},{2,0},{3,1},{4,6},{5,7},{6,4},{7,5},{8,10},{9,11},{10,... | collective-permute-start | bytes 491528 | tf_op jit(solution)/shard_map/ppermute | solution.py:25
  46.7 0.9 %shard_map.76.refs_2_ = bf16[4,512,128]{2,1,0:T(8,128)(2,1)} custom-call(bf16[64,768]{1,0:T(8,128)(2,1)S(1)} %get-tuple-element.32.refs_1_.refs_0_, bf16[256,256]{1,0:T(8,128)(2,1)S(1)} %get-tuple-element.30.refs_3_.refs_1_, bf16[256,256]{1,0:T(8,128)(2,1)S(1)} %collective-permute-done.12.refs_4_.refs_2_), custom_call_target="tpu_custom_call" | custom-call | flops 20000000000 | tf_op jit(solution)/shard_map/pallas_call | solution.py:36
  47.5 3.5 %all-to-all-start.1 = ((bf16[4,512,128]{2,1,0:T(8,128)(2,1)}), bf16[4,512,128]{2,1,0:T(8,128)(2,1)S(1)}, u32[]{:S(2)}, u32[]{:S(2)}) async-start(bf16[4,512,128]{2,1,0:T(8,128)(2,1)} %shard_map.76.refs_2_), calls=%async_computation.1 | async-start | bytes 1048576 | tf_op jit(solution)/shard_map/all_to_all | solution.py:29
  51.0 1.0 %copy-done.2 = bf16[256,1024]{1,0:T(8,128)(2,1)S(1)} copy-done((bf16[256,1024]{1,0:T(8,128)(2,1)S(1)}, bf16[256,1024]{1,0:T(8,128)(2,1)}, u32[]{:S(2)}) %copy-start.2) | copy-done | bytes 524312
  52.1 1.0 %copy-done.4 = bf16[256,1024]{1,0:T(8,128)(2,1)S(1)} copy-done((bf16[256,1024]{1,0:T(8,128)(2,1)S(1)}, bf16[256,1024]{1,0:T(8,128)(2,1)}, u32[]{:S(2)}) %copy-start.4) | copy-done | bytes 524312
  53.1 1.7 %shard_map.77.refs_1_.refs_2_ = f32[128,3072]{1,0:T(8,128)S(1)} custom-call(s32[1]{0:T(128)} %bitcast.3.refs_0_, s32[1,64]{1,0:T(1,128)S(1)} %shard_map.71.refs_3_.refs_2_.refs_1_, bf16[4,512,128]{2,1,0:T(8,128)(2,1)} %shard_map.76.refs_2_, bf16[256,1024]{1,0:T(8,128)(2,1)S(1)} %copy-done.2, bf16[256,1024]{1,0:T(8,128)(2,1)S(1)} %copy-done.4), custom_call_target="tpu_custom_call" | custom-call | flops 20000000000 | tf_op jit(solution)/shard_map/pallas_call | solution.py:36
  54.8 0.4 collective-permute-done.16.refs_0_
  55.2 0.8 %copy-done.7 = f32[128,3072]{1,0:T(8,128)} copy-done((f32[128,3072]{1,0:T(8,128)}, f32[128,3072]{1,0:T(8,128)S(1)}, u32[]{:S(2)}) %copy-start.7) | copy-done | bytes 1572888
  56.0 4.6 %shard_map.79.refs_1_ = s32[3,64]{1,0:T(4,128)S(1)} custom-call(s32[2]{0:T(128)S(1)} %pad_add_fusion.refs_0_.refs_1_, bf16[272,1024]{1,0:T(8,128)(2,1)} %get-tuple-element.25.refs_1_.refs_4_, bf16[272,1024]{1,0:T(8,128)(2,1)S(1)} %get-tuple-element.26.refs_2_.refs_6_, bf16[272,1024]{1,0:T(8,128)(2,1)S(1)} %shard_map.78.refs_3_.refs_8_), custom_call_target="tpu_custom_call" | custom-call | flops 20000000000 | tf_op jit(solution)/shard_map/pallas_call | solution.py:36
  60.6 0.1 collective-permute-start.17
  60.7 0.0 collective-permute-done.14.refs_5_
  60.7 0.0 collective-permute-done.15.refs_6_
  60.7 0.0 collective-permute-done.13.refs_4_
  60.7 2.1 %shard_map.75 = (bf16[64,1024]{1,0:T(8,128)(2,1)}, bf16[64,512]{1,0:T(8,128)(2,1)}) custom-call(s32[2]{0:T(128)S(1)} %pad_add_fusion.refs_0_.refs_1_, bf16[64,768]{1,0:T(8,128)(2,1)S(1)} %copy-done.13, bf16[768,1024]{1,0:T(8,128)(2,1)S(1)} %copy-done.11, bf16[64,256]{1,0:T(8,128)(2,1)S(1)} %get-tuple-element.33.refs_3_, ...), custom_call_target="tpu_custom_call" | custom-call | flops 20000000000 | tf_op jit(solution)/shard_map/pallas_call | solution.py:36
  62.9 0.0 all-to-all-done.1.refs_3_
  62.9 0.0 collective-permute-done.17.refs_9_
  62.9 1.4 %copy-done.8 = f32[128,3072]{1,0:T(8,128)S(1)} copy-done((f32[128,3072]{1,0:T(8,128)S(1)}, f32[128,3072]{1,0:T(8,128)}, u32[]{:S(2)}) %copy-start.8) | copy-done | bytes 1572888
  64.3 3.7 %shard_map.80 = f32[128,3072]{1,0:T(8,128)} custom-call(s32[1]{0:T(128)} %bitcast.3.refs_0_, s32[3,64]{1,0:T(4,128)S(1)} %shard_map.79.refs_1_, f32[128,3072]{1,0:T(8,128)S(1)} %copy-done.8, bf16[4,512,128]{2,1,0:T(8,128)(2,1)S(1)} %all-to-all-done.1.refs_3_, bf16[272,1024]{1,0:T(8,128)(2,1)} %get-tuple-element.25.refs_1_.refs_4_, ...), custom_call_target="tpu_custom_call" | custom-call | flops 20000000000 | tf_op jit(solution)/shard_map/pallas_call | solution.py:36
  (20 shorter events, 0.0 us)
Async XLA Ops:
  0.6 17.4 %collective-permute-start.1 = (bf16[64,1024]{1,0:T(8,128)(2,1)}, bf16[64,1024]{1,0:T(8,128)(2,1)S(1)}, u32[]{:S(2)}, u32[]{:S(2)}) collective-permute-start(bf16[64,1024]{1,0:T(8,128)(2,1)} %refs_1_.2), channel_id=1, source_target_pairs={{0,4},{1,5},{2,6},{3,7},{4,0},{5,1},{6,2},{7,3},{8,12},{9,13},{10,... | collective-permute-start | bytes 393224 | tf_op jit(solution)/shard_map/ppermute | solution.py:25
  4.7 13.4 %collective-permute-start = (bf16[64,1024]{1,0:T(8,128)(2,1)}, bf16[64,1024]{1,0:T(8,128)(2,1)S(1)}, u32[]{:S(2)}, u32[]{:S(2)}) collective-permute-start(bf16[64,1024]{1,0:T(8,128)(2,1)} %refs_1_.2), channel_id=1, source_target_pairs={{0,2},{1,3},{2,0},{3,1},{4,6},{5,7},{6,4},{7,5},{8,10},{9,11},{10,... | collective-permute-start | bytes 393224 | tf_op jit(solution)/shard_map/ppermute | solution.py:25
  6.3 11.8 %collective-permute-start.2 = (bf16[64,1024]{1,0:T(8,128)(2,1)}, bf16[64,1024]{1,0:T(8,128)(2,1)S(1)}, u32[]{:S(2)}, u32[]{:S(2)}) collective-permute-start(bf16[64,1024]{1,0:T(8,128)(2,1)} %refs_1_.2), channel_id=1, source_target_pairs={{0,6},{1,7},{2,4},{3,5},{4,2},{5,3},{6,0},{7,1},{8,14},{9,15},{10,... | collective-permute-start | bytes 393224 | tf_op jit(solution)/shard_map/ppermute | solution.py:25
  7.6 10.6 %all-to-all-start = ((s32[8,1,8]{2,1,0:T(1,128)}), s32[8,1,8]{2,1,0:T(1,128)S(1)}, u32[]{:S(2)}, u32[]{:S(2)}) async-start(s32[8,1,8]{2,1,0:T(1,128)} %broadcast_in_dim.13), calls=%async_computation | async-start | bytes 8192 | tf_op jit(solution)/shard_map/all_to_all | solution.py:29
  12.7 0.8 %copy-start.6 = (bf16[64,512]{1,0:T(8,128)(2,1)S(1)}, bf16[64,512]{1,0:T(8,128)(2,1)}, u32[]{:S(2)}) copy-start(bf16[64,512]{1,0:T(8,128)(2,1)} %refs_1_.3) | copy-start | bytes 196612
  13.6 4.5 %copy-start = (bf16[128,3072]{1,0:T(8,128)(2,1)S(1)}, bf16[128,3072]{1,0:T(8,128)(2,1)}, u32[]{:S(2)}) copy-start(bf16[128,3072]{1,0:T(8,128)(2,1)} %refs_0_.1) | copy-start | bytes 2359300
  13.6 4.6 %copy-start.5 = (bf16[64,1024]{1,0:T(8,128)(2,1)S(1)}, bf16[64,1024]{1,0:T(8,128)(2,1)}, u32[]{:S(2)}) copy-start(bf16[64,1024]{1,0:T(8,128)(2,1)} %refs_1_.2) | copy-start | bytes 393220
  14.1 21.7 %collective-permute-start.11 = (bf16[64,256]{1,0:T(8,128)(2,1)S(1)}, bf16[64,256]{1,0:T(8,128)(2,1)S(1)}, u32[]{:S(2)}, u32[]{:S(2)}) collective-permute-start(bf16[64,256]{1,0:T(8,128)(2,1)S(1)} %get-tuple-element.29), channel_id=1, source_target_pairs={{0,6},{1,7},{2,4},{3,5},{4,2},{5,3},{6,0},{7,1},{8,14},{9,15},{10,... | collective-permute-start | bytes 98312 | tf_op jit(solution)/shard_map/ppermute | solution.py:25
  18.0 17.8 %collective-permute-start.10 = (bf16[64,256]{1,0:T(8,128)(2,1)S(1)}, bf16[64,256]{1,0:T(8,128)(2,1)S(1)}, u32[]{:S(2)}, u32[]{:S(2)}) collective-permute-start(bf16[64,256]{1,0:T(8,128)(2,1)S(1)} %get-tuple-element.29), channel_id=1, source_target_pairs={{0,2},{1,3},{2,0},{3,1},{4,6},{5,7},{6,4},{7,5},{8,10},{9,11},{10,... | collective-permute-start | bytes 98312 | tf_op jit(solution)/shard_map/ppermute | solution.py:25
  18.0 3.9 %collective-permute-start.5 = (bf16[128,3072]{1,0:T(8,128)(2,1)S(1)}, bf16[128,3072]{1,0:T(8,128)(2,1)S(1)}, u32[]{:S(2)}, u32[]{:S(2)}) collective-permute-start(bf16[128,3072]{1,0:T(8,128)(2,1)S(1)} %copy-done), channel_id=1, source_target_pairs={{0,1},{1,0},{2,3},{3,2},{4,5},{5,4},{6,7},{7,6},{8,9},{9,8},{10,11... | collective-permute-start | bytes 2359304 | tf_op jit(solution)/shard_map/ppermute | solution.py:25
  18.9 5.0 %copy-start.1 = (bf16[256,1024]{1,0:T(8,128)(2,1)}, bf16[256,1024]{1,0:T(8,128)(2,1)S(1)}, u32[]{:S(2)}) copy-start(bf16[256,1024]{1,0:T(8,128)(2,1)S(1)} %get-tuple-element.22.refs_3_) | copy-start | bytes 1572868
  18.9 15.1 %collective-permute-start.4 = (bf16[272,1024]{1,0:T(8,128)(2,1)S(1)}, bf16[272,1024]{1,0:T(8,128)(2,1)S(1)}, u32[]{:S(2)}, u32[]{:S(2)}) collective-permute-start(bf16[272,1024]{1,0:T(8,128)(2,1)S(1)} %get-tuple-element.21.refs_2_), channel_id=1, source_target_pairs={{0,16},{8,24},{16,0},{24,8},{1,17},{9,25},{17,1},{25,9},{2,18},{10... | collective-permute-start | bytes 1671176 | tf_op jit(solution)/shard_map/ppermute | solution.py:25
  20.5 14.8 %collective-permute-start.3 = (bf16[272,1024]{1,0:T(8,128)(2,1)S(1)}, bf16[272,1024]{1,0:T(8,128)(2,1)}, u32[]{:S(2)}, u32[]{:S(2)}) collective-permute-start(bf16[272,1024]{1,0:T(8,128)(2,1)S(1)} %get-tuple-element.21.refs_2_), channel_id=1, source_target_pairs={{0,8},{8,0},{16,24},{24,16},{1,9},{9,1},{17,25},{25,17},{2,10},{10... | collective-permute-start | bytes 1671176 | tf_op jit(solution)/shard_map/ppermute | solution.py:25
  21.9 1.9 %collective-permute-start.6 = (bf16[256,1024]{1,0:T(8,128)(2,1)S(1)}, bf16[256,1024]{1,0:T(8,128)(2,1)S(1)}, u32[]{:S(2)}, u32[]{:S(2)}) collective-permute-start(bf16[256,1024]{1,0:T(8,128)(2,1)S(1)} %get-tuple-element.22.refs_3_), channel_id=1, source_target_pairs={{0,1},{1,0},{2,3},{3,2},{4,5},{5,4},{6,7},{7,6},{8,9},{9,8},{10,11... | collective-permute-start | bytes 1572872 | tf_op jit(solution)/shard_map/ppermute | solution.py:25
  22.1 3.5 %copy-start.9 = (bf16[768,1024]{1,0:T(8,128)(2,1)}, bf16[768,1024]{1,0:T(8,128)(2,1)S(1)}, u32[]{:S(2)}) copy-start(bf16[768,1024]{1,0:T(8,128)(2,1)S(1)} %shard_map.68.refs_2_.refs_5_) | copy-start | bytes 4718596
  23.9 1.7 %copy-start.3 = (bf16[256,1024]{1,0:T(8,128)(2,1)}, bf16[256,1024]{1,0:T(8,128)(2,1)S(1)}, u32[]{:S(2)}) copy-start(bf16[256,1024]{1,0:T(8,128)(2,1)S(1)} %collective-permute-done.6.refs_4_) | copy-start | bytes 1572868
  27.2 10.7 %collective-permute-start.9 = (bf16[320,256]{1,0:T(8,128)(2,1)S(1)}, bf16[320,256]{1,0:T(8,128)(2,1)S(1)}, u32[]{:S(2)}, u32[]{:S(2)}) collective-permute-start(bf16[320,256]{1,0:T(8,128)(2,1)S(1)} %get-tuple-element.24.refs_0_), channel_id=1, source_target_pairs={{0,4},{1,5},{2,6},{3,7},{4,0},{5,1},{6,2},{7,3},{8,12},{9,13},{10,... | collective-permute-start | bytes 491528 | tf_op jit(solution)/shard_map/ppermute | solution.py:25
  35.3 4.7 %collective-permute-start.7 = (bf16[272,1024]{1,0:T(8,128)(2,1)}, bf16[272,1024]{1,0:T(8,128)(2,1)S(1)}, u32[]{:S(2)}, u32[]{:S(2)}) collective-permute-start(bf16[272,1024]{1,0:T(8,128)(2,1)} %get-tuple-element.25.refs_1_.refs_4_), channel_id=1, source_target_pairs={{0,1},{1,0},{2,3},{3,2},{4,5},{5,4},{6,7},{7,6},{8,9},{9,8},{10,11... | collective-permute-start | bytes 1671176 | tf_op jit(solution)/shard_map/ppermute | solution.py:25
  35.3 4.7 %collective-permute-start.8 = (bf16[272,1024]{1,0:T(8,128)(2,1)S(1)}, bf16[272,1024]{1,0:T(8,128)(2,1)S(1)}, u32[]{:S(2)}, u32[]{:S(2)}) collective-permute-start(bf16[272,1024]{1,0:T(8,128)(2,1)S(1)} %get-tuple-element.26.refs_2_.refs_6_), channel_id=1, source_target_pairs={{0,1},{1,0},{2,3},{3,2},{4,5},{5,4},{6,7},{7,6},{8,9},{9,8},{10,11... | collective-permute-start | bytes 1671176 | tf_op jit(solution)/shard_map/ppermute | solution.py:25
  38.6 1.4 %collective-permute-start.12 = (bf16[256,256]{1,0:T(8,128)(2,1)S(1)}, bf16[256,256]{1,0:T(8,128)(2,1)S(1)}, u32[]{:S(2)}, u32[]{:S(2)}) collective-permute-start(bf16[256,256]{1,0:T(8,128)(2,1)S(1)} %get-tuple-element.30.refs_3_.refs_1_), channel_id=1, source_target_pairs={{0,1},{1,0},{2,3},{3,2},{4,5},{5,4},{6,7},{7,6},{8,9},{9,8},{10,11... | collective-permute-start | bytes 393224 | tf_op jit(solution)/shard_map/ppermute | solution.py:25
  38.7 16.5 %collective-permute-start.16 = (bf16[272,1024]{1,0:T(8,128)(2,1)S(1)}, bf16[272,1024]{1,0:T(8,128)(2,1)S(1)}, u32[]{:S(2)}, u32[]{:S(2)}) collective-permute-start(bf16[272,1024]{1,0:T(8,128)(2,1)S(1)} %get-tuple-element.27.refs_0_), channel_id=1, source_target_pairs={{0,24},{8,16},{16,8},{24,0},{1,25},{9,17},{17,9},{25,1},{2,26},{10... | collective-permute-start | bytes 1671176 | tf_op jit(solution)/shard_map/ppermute | solution.py:25
  40.0 1.4 %copy-start.10 = (bf16[768,1024]{1,0:T(8,128)(2,1)S(1)}, bf16[768,1024]{1,0:T(8,128)(2,1)}, u32[]{:S(2)}) copy-start(bf16[768,1024]{1,0:T(8,128)(2,1)} %copy-done.9) | copy-start | bytes 4718596
  43.2 4.4 %copy-start.12 = (bf16[64,768]{1,0:T(8,128)(2,1)}, bf16[64,768]{1,0:T(8,128)(2,1)S(1)}, u32[]{:S(2)}) copy-start(bf16[64,768]{1,0:T(8,128)(2,1)S(1)} %get-tuple-element.32.refs_1_.refs_0_) | copy-start | bytes 294916
  43.2 17.5 %collective-permute-start.14 = (bf16[64,1024]{1,0:T(8,128)(2,1)}, bf16[64,1024]{1,0:T(8,128)(2,1)}, u32[]{:S(2)}, u32[]{:S(2)}) collective-permute-start(bf16[64,1024]{1,0:T(8,128)(2,1)} %get-tuple-element.35), channel_id=1, source_target_pairs={{0,4},{1,5},{2,6},{3,7},{4,0},{5,1},{6,2},{7,3},{8,12},{9,13},{10,... | collective-permute-start | bytes 393224 | tf_op jit(solution)/shard_map/ppermute | solution.py:25
  43.2 17.5 %collective-permute-start.15 = (bf16[64,1024]{1,0:T(8,128)(2,1)}, bf16[64,1024]{1,0:T(8,128)(2,1)}, u32[]{:S(2)}, u32[]{:S(2)}) collective-permute-start(bf16[64,1024]{1,0:T(8,128)(2,1)} %get-tuple-element.36), channel_id=1, source_target_pairs={{0,6},{1,7},{2,4},{3,5},{4,2},{5,3},{6,0},{7,1},{8,14},{9,15},{10,... | collective-permute-start | bytes 393224 | tf_op jit(solution)/shard_map/ppermute | solution.py:25
  45.7 15.0 %collective-permute-start.13 = (bf16[80,1024]{1,0:T(8,128)(2,1)S(1)}, bf16[80,1024]{1,0:T(8,128)(2,1)}, u32[]{:S(2)}, u32[]{:S(2)}) collective-permute-start(bf16[80,1024]{1,0:T(8,128)(2,1)S(1)} %get-tuple-element.34), channel_id=1, source_target_pairs={{0,2},{1,3},{2,0},{3,1},{4,6},{5,7},{6,4},{7,5},{8,10},{9,11},{10,... | collective-permute-start | bytes 491528 | tf_op jit(solution)/shard_map/ppermute | solution.py:25
  47.5 15.3 %all-to-all-start.1 = ((bf16[4,512,128]{2,1,0:T(8,128)(2,1)}), bf16[4,512,128]{2,1,0:T(8,128)(2,1)S(1)}, u32[]{:S(2)}, u32[]{:S(2)}) async-start(bf16[4,512,128]{2,1,0:T(8,128)(2,1)} %shard_map.76.refs_2_), calls=%async_computation.1 | async-start | bytes 1048576 | tf_op jit(solution)/shard_map/all_to_all | solution.py:29
  51.0 1.0 %copy-start.2 = (bf16[256,1024]{1,0:T(8,128)(2,1)S(1)}, bf16[256,1024]{1,0:T(8,128)(2,1)}, u32[]{:S(2)}) copy-start(bf16[256,1024]{1,0:T(8,128)(2,1)} %copy-done.1) | copy-start | bytes 1572868
  52.1 1.0 %copy-start.4 = (bf16[256,1024]{1,0:T(8,128)(2,1)S(1)}, bf16[256,1024]{1,0:T(8,128)(2,1)}, u32[]{:S(2)}) copy-start(bf16[256,1024]{1,0:T(8,128)(2,1)} %copy-done.3) | copy-start | bytes 1572868
  54.8 1.2 %copy-start.7 = (f32[128,3072]{1,0:T(8,128)}, f32[128,3072]{1,0:T(8,128)S(1)}, u32[]{:S(2)}) copy-start(f32[128,3072]{1,0:T(8,128)S(1)} %shard_map.77.refs_1_.refs_2_) | copy-start | bytes 4718596
  56.0 4.7 %copy-start.11 = (bf16[768,1024]{1,0:T(8,128)(2,1)S(1)}, bf16[768,1024]{1,0:T(8,128)(2,1)}, u32[]{:S(2)}) copy-start(bf16[768,1024]{1,0:T(8,128)(2,1)} %copy-done.9) | copy-start | bytes 4718596
  56.0 4.8 %copy-start.13 = (bf16[64,768]{1,0:T(8,128)(2,1)S(1)}, bf16[64,768]{1,0:T(8,128)(2,1)}, u32[]{:S(2)}) copy-start(bf16[64,768]{1,0:T(8,128)(2,1)} %copy-done.12) | copy-start | bytes 294916
  60.6 2.3 %collective-permute-start.17 = (bf16[272,1024]{1,0:T(8,128)(2,1)S(1)}, bf16[272,1024]{1,0:T(8,128)(2,1)S(1)}, u32[]{:S(2)}, u32[]{:S(2)}) collective-permute-start(bf16[272,1024]{1,0:T(8,128)(2,1)S(1)} %shard_map.78.refs_3_.refs_8_), channel_id=1, source_target_pairs={{0,1},{1,0},{2,3},{3,2},{4,5},{5,4},{6,7},{7,6},{8,9},{9,8},{10,11... | collective-permute-start | bytes 1671176 | tf_op jit(solution)/shard_map/ppermute | solution.py:25
  62.9 1.4 %copy-start.8 = (f32[128,3072]{1,0:T(8,128)S(1)}, f32[128,3072]{1,0:T(8,128)}, u32[]{:S(2)}) copy-start(f32[128,3072]{1,0:T(8,128)} %copy-done.7) | copy-start | bytes 4718596

commit v3 on v2

--- a/solution.py
+++ b/solution.py
@@ -29,7 +29,7 @@
     return lax.all_to_all(copies, axis, split_axis=0, concat_axis=0, tiled=True)
 
 
-def call(body, out_shapes, inputs, specs, scratch=(), out_specs=None, after=(), work=2e10, room=12, name=""):
+def call(body, out_shapes, inputs, specs, scratch=(), out_specs=None, after=(), work=1e10, room=12):
     def run(*refs):
         body(*refs[len(after) :])
 
@@ -75,70 +75,26 @@
     return ((apart & 1) * chips + (apart >> 1)) * seg_count + lax.rem(source, seg_count)
 
 
-def find_follows(chips, me, source, follow_ref, table):
-    peers = 2 * chips
-    segments = follow_ref.shape[1]
-    seg_count = segments // peers
-    for i in range(segments):
-        follow_ref[table, i] = segments * SEG
+def follows(chips, me_ref, table_ref, follow_ref):
+    peers, seg_count = table_ref.shape
+    me = me_ref[0]
+    for i in range(peers * seg_count):
+        follow_ref[i] = peers * seg_count
     for peer in range(peers):
         slot = place(peer * seg_count, seg_count, chips, me)
         for position in range(seg_count):
-            found = source(peer, position)
-
-            @pl.when(found >= 0)
+            source = table_ref[peer, position]
+
+            @pl.when(source >= 0)
             def _():
-                follow_ref[table, place(found, seg_count, chips, me)] = (slot + position) * SEG
-
-
-def follows(chips, me_ref, table_ref, follow_ref):
-    find_follows(chips, me_ref[0], lambda peer, position: table_ref[peer, position], follow_ref, 0)
-
-
-def far_follows(chips, me_ref, *refs):
-    blocks, (follow_ref, raw_ref, wide_ref, table_ref, sems) = refs[:-5], refs[-5:]
-    count = len(blocks)
-    seg_count = follow_ref.shape[1] // (2 * chips)
-    loads = []
-    for i, block in enumerate(blocks):
-        rows = pl.ds(block.shape[0] - 16, 16)
-        loads.append(pltpu.make_async_copy(block.at[rows, pl.ds(0, 128)], raw_ref.at[i], sems.at[i]))
-        loads[-1].start()
-    for load in loads:
-        load.wait()
-    wide_ref[...] = raw_ref[...].astype(F32).astype(jnp.int32)
-    moved = pltpu.make_async_copy(wide_ref, table_ref, sems.at[0])
-    moved.start()
-    moved.wait()
-
-    def one(table, carry):
-        find_follows(
-            chips,
-            me_ref[0],
-            lambda peer, position: table_ref[table, 0, peer * seg_count + position],
-            follow_ref,
-            table,
-        )
-        return carry
-
-    lax.fori_loop(0, count, one, 0)
-
-
-def stack(table_ref, *refs):
-    blocks, (rows_ref, copy_ref) = refs[:-2], refs[-2:]
+                follow_ref[place(source, seg_count, chips, me)] = slot + position
+
+
+def stack(*refs):
+    blocks, out_ref = refs[:-1], refs[-1]
     count = blocks[0].shape[0]
     for slot, block in enumerate(blocks):
-        rows_ref[slot * count : (slot + 1) * count, :] = block[...]
-        copy_ref[slot * count : (slot + 1) * count, :] = block[...]
-    peers, seg_count = table_ref.shape
-    lane = lax.broadcasted_iota(jnp.int32, (16, 128), 1)
-    value = jnp.zeros((16, 128), jnp.int32)
-    for peer in range(peers):
-        for position in range(seg_count):
-            value = jnp.where(lane == peer * seg_count + position, table_ref[peer, position], value)
-    total = rows_ref.shape[0]
-    copy_ref[total:, :] = jnp.zeros((16, C), BF16)
-    copy_ref[total:, :128] = value.astype(F32).astype(BF16)
+        out_ref[slot * count : (slot + 1) * count, :] = block[...]
 
 
 def forward(me_ref, table_ref, weight_ref, own_ref, other_ref, grad_ref, act_ref, sent_ref, rows_ref, early_ref):
@@ -203,7 +159,7 @@
     pre_ref[2 * total :, :] = jnp.zeros((SEG, wide), F32)
     for segment in range(total // SEG):
         at = segment * SEG
-        follow = pl.multiple_of(follow_ref[0, segment], SEG)
+        follow = pl.multiple_of(follow_ref[segment] * SEG, SEG)
         carried = pre_ref[pl.ds(follow, SEG), :]
         local = pre_ref[at : at + SEG, :]
         routed_ref[at : at + SEG, :wide] = carried
@@ -221,12 +177,26 @@
         out[:count, :] = part[slot * count : (slot + 1) * count, :].astype(BF16)
 
 
-def spread(own_ref, other_ref, copies_ref):
+def spread(follow_ref, own_ref, other_ref, copies_ref):
     total, wide = own_ref.shape
     width = wide // 2
+    lane = lax.broadcasted_iota(jnp.int32, (16, width), 1)
+    value = jnp.zeros((16, width), jnp.int32)
+    for segment in range(follow_ref.shape[0]):
+        value = jnp.where(lane == segment, follow_ref[segment], value)
+    value = value.astype(F32).astype(BF16)
     for copy in range(copies_ref.shape[0]):
         copies_ref[copy, :total, :] = own_ref[:, :width]
-        copies_ref[copy, total:, :] = other_ref[:, width:]
+        copies_ref[copy, total : 2 * total, :] = other_ref[:, width:]
+        copies_ref[copy, 2 * total :, :] = value
+
+
+def local(here_ref, weight_ref, out_ref):
+    out_ref[...] = jnp.dot(here_ref[...], weight_ref[...], preferred_element_type=F32)
+
+
+def mark(out_ref):
+    out_ref[...] = jnp.zeros(out_ref.shape, out_ref.dtype)
 
 
 def nothing(*refs):
@@ -241,29 +211,33 @@
         out_specs=[ANY] * len(values),
         input_output_aliases={i: i for i in range(len(values))},
         compiler_params=pltpu.CompilerParams(vmem_limit_bytes=2**20),
-        cost_estimate=pl.CostEstimate(flops=10**10, bytes_accessed=0, transcendentals=0),
+        cost_estimate=pl.CostEstimate(flops=10000000, bytes_accessed=0, transcendentals=0),
     )(*values, *after)
 
 
-def weight_grad(which, scale, group_ref, follow_ref, *refs):
-    first_ref = refs[0] if len(which) > 1 else None
-    sent_pre_ref = refs[-5 - 2 * len(which)]
-    signals = refs[-4 - 2 * len(which) : -4]
-    out_ref, pre_ref, routed_ref, rows_ref = refs[-4:]
-    total = pre_ref.shape[0] - SEG
-    width = pre_ref.shape[1]
-    pre_ref[total:, :] = jnp.zeros((SEG, width), F32)
-    for i, distance in enumerate(which):
-        base = i * total
-        pre_ref[:total, :] = sent_pre_ref[group_ref[0] ^ distance].astype(F32)
-        rows_ref[base : base + total // 2, :] = signals[2 * i][: total // 2, :]
-        rows_ref[base + total // 2 : base + total, :] = signals[2 * i + 1][: total // 2, :]
+def weight_grad(scale, group_ref, pre_ref, *refs):
+    blocks = refs[:-7]
+    out_ref, early_ref, routed_ref, rows_ref, wide_ref, follow_ref, sem = refs[-7:]
+    groups, total, width = early_ref.shape
+    total -= SEG
+    for i in range(groups):
+        wide_ref[i] = pre_ref[group_ref[0] ^ i, total:, :].astype(F32).astype(jnp.int32)
+    load = pltpu.make_async_copy(wide_ref, follow_ref, sem)
+    load.start()
+    for i, block in enumerate(blocks):
+        count = block.shape[0]
+        rows_ref[i * count : (i + 1) * count, :] = block[...]
+    for i in range(groups):
+        early_ref[i, :total, :] = pre_ref[group_ref[0] ^ i, :total, :].astype(F32)
+        early_ref[i, total:, :] = jnp.zeros((SEG, width), F32)
+    load.wait()
+    for i in range(groups):
         for segment in range(total // SEG):
             at = segment * SEG
-            follow = pl.multiple_of(follow_ref[i, segment], SEG)
-            carried = pre_ref[pl.ds(follow, SEG), :]
-            local = pre_ref[at : at + SEG, :]
-            at += base
+            follow = pl.multiple_of(follow_ref[i, 0, segment] * SEG, SEG)
+            carried = early_ref[i, pl.ds(follow, SEG), :]
+            local = early_ref[i, at : at + SEG, :]
+            at += i * total
             routed_ref[at : at + SEG, :width] = carried
             routed_ref[at : at + SEG, width : 2 * width] = roll_half(local, carried)
             routed_ref[at : at + SEG, 2 * width :] = local
@@ -271,17 +245,13 @@
         routed_ref[...].astype(BF16), rows_ref[...], (((0,), (0,)), ((), ())), preferred_element_type=F32
     )
     for tap in range(3):
-        here = slice(tap * C, (tap + 1) * C)
-        value = product[tap * width : (tap + 1) * width, :]
-        if first_ref is not None:
-            value = (value + first_ref[:, here]) * scale
-        out_ref[:, here] = value
-
-
-def finish(me_ref, here_ref, weight_ref, gated_ref, *refs):
+        out_ref[:, tap * C : (tap + 1) * C] = product[tap * width : (tap + 1) * width, :] * scale
+
+
+def finish(me_ref, kept_ref, gated_ref, *refs):
     parts, (grad_ref, out_ref) = refs[:-2], refs[-2:]
     count = grad_ref.shape[0]
-    total = jnp.dot(here_ref[...], weight_ref[...], preferred_element_type=F32)
+    total = kept_ref[...]
     for part in parts:
         total = total + part[:count, :].astype(F32)
     grad_ref[...] = total.astype(BF16)
@@ -314,20 +284,17 @@
     fold = C // wide
     own_rows = [signal] + [swap(signal, "fsdp", 2 * k) for k in range(1, chips)]
     picked = call(
-        pick, [shaped((rows, wide), BF16)] * half_chips, [who, grad_gated], [SMEM, VMEM], name="pick"
+        pick, [shaped((rows, wide), BF16)] * half_chips, [who, grad_gated], [SMEM, VMEM]
     )
     other_weight = swap(conv_weight, "fsdp", 1)
     weight = call(
-        stack_weight, [shaped((3 * wide, C), BF16)], [conv_weight, other_weight], [VMEM] * 2, name="wstack"
+        stack_weight, [shaped((3 * wide, C), BF16)], [conv_weight, other_weight], [VMEM] * 2
     )[0]
     table = exchange(jnp.broadcast_to(source_seg[None], (peers, 1, seg_count)), "fsdp").reshape(peers, seg_count)
-    own_stack, own_copy = call(
-        stack,
-        [shaped((own_class, C), BF16), shaped((own_class + 16, C), BF16)],
-        [table, *own_rows],
-        [SMEM] + [VMEM] * chips,
-        name="stack",
-    )
+    grads = [picked[0], swap(picked[1], "fsdp", 2), swap(picked[1], "fsdp", 6)]
+    own_stack = call(
+        stack, [shaped((own_class, C), BF16)], own_rows, [VMEM] * chips, after=[table, picked[0]]
+    )[0]
     other_stack = swap(own_stack, "fsdp", 1)
     act, sent = call(
         forward,
@@ -335,32 +302,24 @@
         [who, table, weight, own_stack, other_stack, picked[0]],
         [SMEM, SMEM] + [VMEM] * 4,
         [pltpu.VMEM((all_rows, C), BF16), pltpu.VMEM((all_rows + SEG, 2 * wide), F32)],
-        name="forward",
+        after=grads[1:],
     )
     partner = swap(sent, "fsdp", peers // 2)
-    grads = [picked[0], swap(picked[1], "fsdp", 2), swap(picked[1], "fsdp", 6)]
-
+    far_own = [swap(own_stack, "dp", d) for d in (1, 2, 3)]
     follow = call(
         functools.partial(follows, chips),
-        [shaped((1, peers * seg_count), jnp.int32)],
+        [shaped((peers * seg_count,), jnp.int32)],
         [who, table],
         [SMEM, SMEM],
         out_specs=[SMEM],
         after=[sent],
-        name="follow",
     )[0]
-    far_own = [swap(own_copy, "dp", d) for d in (1, 2)]
-    *far_own, own_copy = held([*far_own, own_copy], [follow])
-    last_own = swap(own_copy, "dp", 3)
-    far_other = [swap(block, "fsdp", 1) for block in far_own]
 
     *gated, pre = call(
         gate,
         [shaped((rows, wide), BF16)] * half_chips + [shaped((own_class, wide), BF16)],
         [who, act, partner, *grads],
         [SMEM] + [VMEM] * (2 + len(grads)),
-        after=[own_copy],
-        name="gate",
     )
     other_pre = swap(pre, "fsdp", 1)
     *sends, here = call(
@@ -371,58 +330,42 @@
         [follow, pre, other_pre, weight, gated[1]],
         [SMEM, VMEM, VMEM, VMEM, VMEM],
         [pltpu.VMEM((all_rows + SEG, wide), F32), pltpu.VMEM((own_class, 3 * wide), F32)],
-        after=far_other,
-        name="input",
     )
     parts = [swap(part, "fsdp", 2 * (k + 1)) for k, part in enumerate(sends)]
     sent_pre = call(
-        spread, [shaped((groups, all_rows, width), BF16)], [pre, other_pre], [VMEM] * 2, after=[here], name="spread"
+        spread,
+        [shaped((groups, all_rows + 16, width), BF16)],
+        [follow, pre, other_pre],
+        [SMEM, VMEM, VMEM],
     )[0]
-    far_pre = exchange(sent_pre, "dp")
-
-    def grads_of(which, found, inputs, first, name):
-        count = len(which)
-        return call(
-            functools.partial(weight_grad, which, 1.0 / math.sqrt(all_rows * groups)),
-            [shaped((width, 3 * C), F32)],
-            [group[None], found, *first, *inputs],
-            [SMEM, SMEM] + [VMEM] * (len(inputs) + len(first)),
-            [
-                pltpu.VMEM((all_rows + SEG, width), F32),
-                pltpu.VMEM((count * all_rows, 3 * width), F32),
-                pltpu.VMEM((count * all_rows, C), BF16),
-            ],
-            room=24,
-            name=name,
-        )[0]
-
-    near = grads_of([0], follow, [sent_pre, own_stack, other_stack], [], "near")
-    last_own = held([last_own], [near])[0]
-    far_own.append(last_own)
-    far_other.append(swap(last_own, "fsdp", 1))
-    far_follow = call(
-        functools.partial(far_follows, chips),
-        [shaped((groups - 1, peers * seg_count), jnp.int32)],
-        [who, *far_own],
-        [SMEM] + [ANY] * len(far_own),
-        [
-            pltpu.VMEM((groups - 1, 16, 128), BF16),
-            pltpu.VMEM((groups - 1, 16, 128), jnp.int32),
-            pltpu.SMEM((groups - 1, 16, 128), jnp.int32),
-            pltpu.SemaphoreType.DMA((groups - 1,)),
-        ],
-        out_specs=[SMEM],
-        name="farfollow",
+    all_pre = exchange(sent_pre, "dp")
+    kept = call(
+        local, [shaped((rows, C), F32)], [here, weight], [VMEM] * 2, after=[sent_pre]
     )[0]
     grad_in, gated_out = call(
         finish,
         [shaped((rows, C), BF16), shaped((rows, H), BF16)],
-        [who, here, weight, gated[0], *parts],
-        [SMEM] + [VMEM] * (chips + 2),
-        name="finish",
-    )
-    far_signals = [block for pair in zip(far_own, far_other) for block in pair]
-    grad_weight = grads_of(list(range(1, groups)), far_follow, [far_pre, *far_signals], [near], "far")
+        [who, kept, gated[0], *parts],
+        [SMEM] + [VMEM] * (chips + 1),
+    )
+    far_own = held(far_own, [all_pre])
+    far_other = [swap(block, "fsdp", 1) for block in far_own]
+    blocks = [own_stack, other_stack] + [block for pair in zip(far_own, far_other) for block in pair]
+    grad_weight = call(
+        functools.partial(weight_grad, 1.0 / math.sqrt(all_rows * groups)),
+        [shaped((width, 3 * C), F32)],
+        [group[None], all_pre, *blocks],
+        [SMEM] + [VMEM] * (1 + len(blocks)),
+        [
+            pltpu.VMEM((groups, all_rows + SEG, width), F32),
+            pltpu.VMEM((groups * all_rows, 3 * width), F32),
+            pltpu.VMEM((groups * all_rows, C), BF16),
+            pltpu.VMEM((groups, 16, width), jnp.int32),
+            pltpu.SMEM((groups, 16, width), jnp.int32),
+            pltpu.SemaphoreType.DMA,
+        ],
+        room=24,
+    )[0]
     return gated_out, grad_in, grad_weight
 
 

time: 68.5 us -> 63 us (0.920)
  Pallas kernels: 20 us -> 14 us
  waiting for transfers between devices: 11.3 us -> 14.9 us
  local copies, waits for them, and re-layouts: 7.79 us -> 6.16 us
  starting transfers between devices: 27.9 us -> 26.7 us
    pallas_call x12 -> x11, Pallas kernels: 20 us -> 14 us  [call(): pl.pallas_call(run, out_shape=out_shapes, in_specs=[ANY] * len(after) + l...]
    all_to_all x2, waiting for transfers between devices: 0.02 us -> 4.32 us  [exchange(): return lax.all_to_all(copies, axis, split_axis=0, concat_axis=0, tiled=True)]
    unnamed x28 -> x24, local copies, waits for them, and re-layouts: 6.54 us -> 4.91 us
    ppermute x18, starting transfers between devices: 19.4 us -> 17.9 us  [swap(): return lax.ppermute(value, axis, [(i, i ^ distance) for i in range(count)])]
  transfers between devices with their start and end apart: 20 -> 20, of which waited for: 6 -> 6; matrix products, arithmetic and copies ran while one was open for 2% -> 2% of each run, Pallas kernels for 24% -> 13%
where the time goes in v3:
time: 63 us; the launch traced here: 62.6 us
  starting transfers between devices  26.7 us (42%)
  waiting for transfers between devices  14.9 us (24%)
  Pallas kernels  14 us (22%)
  local copies, waits for them, and re-layouts  6.16 us (10%)
  between operations  0.84 us (1%)
    ppermute x18, starting transfers between devices, swap(): return lax.ppermute(value, axis, [(i, i ^ distance) for i in range(count)])  17.9 us
    pallas_call x11, Pallas kernels, call(): pl.pallas_call(run, out_shape=out_shapes, in_specs=[ANY] * len(after) + l...  14 us
    ppermute x18, waiting for transfers between devices, swap(): return lax.ppermute(value, axis, [(i, i ^ distance) for i in range(count)])  10.6 us
    all_to_all x2, starting transfers between devices, exchange(): return lax.all_to_all(copies, axis, split_axis=0, concat_axis=0, tiled=True)  8.82 us
    unnamed x24, local copies, waits for them, and re-layouts  4.91 us
    all_to_all x2, waiting for transfers between devices, exchange(): return lax.all_to_all(copies, axis, split_axis=0, concat_axis=0, tiled=True)  4.32 us
  transfers between devices with their start and end apart: 20, of which 6 were waited for; matrix products, arithmetic and copies ran while one was open for 2% of the time, Pallas kernels for 13%

profile of v3, /device:TPU:0, one launch (start us, length us, event | category | flops | bytes accessed | tf_op | source)
XLA Modules:
  0.0 62.6 jit_solution(397763426954320356)
XLA Ops:
  0.6 4.1 %collective-permute-start.4 = (bf16[64,1024]{1,0:T(8,128)(2,1)}, bf16[64,1024]{1,0:T(8,128)(2,1)S(1)}, u32[]{:S(2)}, u32[]{:S(2)}) collective-permute-start(bf16[64,1024]{1,0:T(8,128)(2,1)} %refs_2_.1), channel_id=1, source_target_pairs={{0,4},{1,5},{2,6},{3,7},{4,0},{5,1},{6,2},{7,3},{8,12},{9,13},{10,... | collective-permute-start | bytes 393224 | tf_op jit(solution)/shard_map/ppermute | solution.py:25
  4.7 1.6 %collective-permute-start.3 = (bf16[64,1024]{1,0:T(8,128)(2,1)}, bf16[64,1024]{1,0:T(8,128)(2,1)S(1)}, u32[]{:S(2)}, u32[]{:S(2)}) collective-permute-start(bf16[64,1024]{1,0:T(8,128)(2,1)} %refs_2_.1), channel_id=1, source_target_pairs={{0,2},{1,3},{2,0},{3,1},{4,6},{5,7},{6,4},{7,5},{8,10},{9,11},{10,... | collective-permute-start | bytes 393224 | tf_op jit(solution)/shard_map/ppermute | solution.py:25
  6.3 0.0 collective-permute-start.5
  6.3 1.2 %broadcast_in_dim.12 = s32[8,1,8]{2,1,0:T(1,128)} broadcast(s32[8]{0:T(128)} %bitcast.7), dimensions={2} | broadcast | bytes 288 | tf_op jit(solution)/shard_map/broadcast_in_dim | solution.py:293
  7.6 5.1 %all-to-all-start = ((s32[8,1,8]{2,1,0:T(1,128)}), s32[8,1,8]{2,1,0:T(1,128)S(1)}, u32[]{:S(2)}, u32[]{:S(2)}) async-start(s32[8,1,8]{2,1,0:T(1,128)} %broadcast_in_dim.12), calls=%async_computation | async-start | bytes 8192 | tf_op jit(solution)/shard_map/all_to_all | solution.py:29
  12.7 0.1 pad_add_fusion.refs_0_.refs_2_.refs_1_
  12.7 0.8 %copy-done.2 = bf16[64,512]{1,0:T(8,128)(2,1)S(1)} copy-done((bf16[64,512]{1,0:T(8,128)(2,1)S(1)}, bf16[64,512]{1,0:T(8,128)(2,1)}, u32[]{:S(2)}) %copy-start.2) | copy-done | bytes 65560
  13.6 0.6 shard_map.67
  14.1 3.9 %collective-permute-start.1 = (bf16[64,256]{1,0:T(8,128)(2,1)S(1)}, bf16[64,256]{1,0:T(8,128)(2,1)S(1)}, u32[]{:S(2)}, u32[]{:S(2)}) collective-permute-start(bf16[64,256]{1,0:T(8,128)(2,1)S(1)} %get-tuple-element.19), channel_id=1, source_target_pairs={{0,6},{1,7},{2,4},{3,5},{4,2},{5,3},{6,0},{7,1},{8,14},{9,15},{10,... | collective-permute-start | bytes 98312 | tf_op jit(solution)/shard_map/ppermute | solution.py:25
  18.0 0.0 collective-permute-start
  18.0 0.0 collective-permute-done.4.refs_4_
  18.0 0.0 copy-done
  18.0 0.1 collective-permute-start.2
  18.1 0.0 all-to-all-done
  18.1 0.0 collective-permute-done.3.refs_3_
  18.1 0.0 collective-permute-done.5.refs_5_
  18.2 0.5 collective-permute-start.6
  18.8 1.6 %collective-permute-done.2.refs_1_ = bf16[128,3072]{1,0:T(8,128)(2,1)S(1)} collective-permute-done((bf16[128,3072]{1,0:T(8,128)(2,1)S(1)}, bf16[128,3072]{1,0:T(8,128)(2,1)S(1)}, u32[]{:S(2)}, u32[]{:S(2)}) %collective-permute-start.2) | collective-permute-done | bytes 786464 | tf_op jit(solution)/shard_map/ppermute | solution.py:25
  20.4 0.1 shard_map.68.refs_4_.refs_3_.refs_2_
  20.5 0.0 copy-start.3
  20.5 0.0 collective-permute-done.1.refs_1_.refs_5_
  20.5 1.4 %collective-permute-done.refs_0_.refs_4_ = bf16[64,256]{1,0:T(8,128)(2,1)S(1)} collective-permute-done((bf16[64,256]{1,0:T(8,128)(2,1)S(1)}, bf16[64,256]{1,0:T(8,128)(2,1)S(1)}, u32[]{:S(2)}, u32[]{:S(2)}) %collective-permute-start) | collective-permute-done | bytes 32800 | tf_op jit(solution)/shard_map/ppermute | solution.py:25
  21.9 0.0 collective-permute-done.6.refs_6_.refs_3_
  22.0 1.7 %shard_map.70 = (f32[256,256]{1,0:T(8,128)S(1)}, bf16[320,256]{1,0:T(8,128)(2,1)S(1)}) custom-call(bf16[64,256]{1,0:T(8,128)(2,1)S(1)} %collective-permute-done.refs_0_.refs_4_, bf16[64,256]{1,0:T(8,128)(2,1)S(1)} %collective-permute-done.1.refs_1_.refs_5_, s32[2]{0:T(128)S(1)} %pad_add_fusion.refs_0_.refs_2_.refs_1_, s32[8,8]{1,0:T(8,128)S(1)} %bitcast.5, ...), custom_call_target="tpu_custom_call" | custom-call | flops 10000000000 | tf_op jit(solution)/shard_map/pallas_call | solution.py:36
  23.6 0.0 copy-done.3
  23.6 0.1 collective-permute-start.7
  23.7 2.5 %collective-permute-start.14 = (bf16[256,1024]{1,0:T(8,128)(2,1)S(1)}, bf16[256,1024]{1,0:T(8,128)(2,1)S(1)}, u32[]{:S(2)}, u32[]{:S(2)}) collective-permute-start(bf16[256,1024]{1,0:T(8,128)(2,1)S(1)} %shard_map.69.refs_5_.refs_2_), channel_id=1, source_target_pairs={{0,24},{8,16},{16,8},{24,0},{1,25},{9,17},{17,9},{25,1},{2,26},{10... | collective-permute-start | bytes 1572872 | tf_op jit(solution)/shard_map/ppermute | solution.py:25
  26.2 0.5 collective-permute-start.13
  26.7 0.5 collective-permute-start.12
  27.3 6.3 %collective-permute-done.7.refs_2_ = bf16[320,256]{1,0:T(8,128)(2,1)S(1)} collective-permute-done((bf16[320,256]{1,0:T(8,128)(2,1)S(1)}, bf16[320,256]{1,0:T(8,128)(2,1)S(1)}, u32[]{:S(2)}, u32[]{:S(2)}) %collective-permute-start.7) | collective-permute-done | bytes 163872 | tf_op jit(solution)/shard_map/ppermute | solution.py:25
  33.5 0.6 %shard_map.72 = (bf16[64,256]{1,0:T(8,128)(2,1)S(1)}, bf16[64,256]{1,0:T(8,128)(2,1)S(1)}, bf16[256,256]{1,0:T(8,128)(2,1)S(1)}) custom-call(s32[2]{0:T(128)S(1)} %pad_add_fusion.refs_0_.refs_2_.refs_1_, f32[256,256]{1,0:T(8,128)S(1)} %get-tuple-element.22.refs_1_, bf16[320,256]{1,0:T(8,128)(2,1)S(1)} %collective-permute-done.7.refs_2_, ...), custom_call_target="tpu_custom_call" | custom-call | flops 10000000000 | tf_op jit(solution)/shard_map/pallas_call | solution.py:36
  34.2 0.0 copy-start.10
  34.2 0.0 copy-start.4
  34.2 0.1 collective-permute-start.8
  34.3 1.7 %shard_map.71.refs_0_ = s32[64]{0:T(128)S(1)} custom-call(bf16[320,256]{1,0:T(8,128)(2,1)S(1)} %get-tuple-element.21.refs_0_, s32[2]{0:T(128)S(1)} %pad_add_fusion.refs_0_.refs_2_.refs_1_, s32[8,8]{1,0:T(8,128)S(1)} %bitcast.6), custom_call_target="tpu_custom_call" | custom-call | flops 10000000000 | tf_op jit(solution)/shard_map/pallas_call | solution.py:36
  36.0 0.0 collective-permute-done.8.refs_2_
  36.0 1.7 %shard_map.74 = (bf16[80,1024]{1,0:T(8,128)(2,1)S(1)}, bf16[64,1024]{1,0:T(8,128)(2,1)}, bf16[64,1024]{1,0:T(8,128)(2,1)}, bf16[64,768]{1,0:T(8,128)(2,1)S(1)}) custom-call(s32[64]{0:T(128)S(1)} %shard_map.71.refs_0_, bf16[256,256]{1,0:T(8,128)(2,1)S(1)} %get-tuple-element.23.refs_1_, bf16[256,256]{1,0:T(8,128)(2,1)S(1)} %collective-permute-done.8.refs_2_, ...), custom_call_target="tpu_custom_call" | custom-call | flops 10000000000 | tf_op jit(solution)/shard_map/pallas_call | solution.py:36
  37.8 0.6 %copy-done.8 = bf16[64,768]{1,0:T(8,128)(2,1)} copy-done((bf16[64,768]{1,0:T(8,128)(2,1)}, bf16[64,768]{1,0:T(8,128)(2,1)S(1)}, u32[]{:S(2)}) %copy-start.8) | copy-done | bytes 98328
  38.4 0.0 collective-permute-start.10
  38.4 1.5 %collective-permute-start.11 = (bf16[64,1024]{1,0:T(8,128)(2,1)}, bf16[64,1024]{1,0:T(8,128)(2,1)}, u32[]{:S(2)}, u32[]{:S(2)}) collective-permute-start(bf16[64,1024]{1,0:T(8,128)(2,1)} %get-tuple-element.29), channel_id=1, source_target_pairs={{0,6},{1,7},{2,4},{3,5},{4,2},{5,3},{6,0},{7,1},{8,14},{9,15},{10,... | collective-permute-start | bytes 393224 | tf_op jit(solution)/shard_map/ppermute | solution.py:25
  39.9 1.4 %shard_map.73.refs_0_ = bf16[4,528,128]{2,1,0:T(8,128)(2,1)} custom-call(s32[64]{0:T(128)S(1)} %shard_map.71.refs_0_, bf16[256,256]{1,0:T(8,128)(2,1)S(1)} %get-tuple-element.23.refs_1_, bf16[256,256]{1,0:T(8,128)(2,1)S(1)} %collective-permute-done.8.refs_2_), custom_call_target="tpu_custom_call" | custom-call | flops 10000000000 | tf_op jit(solution)/shard_map/pallas_call | solution.py:36
  41.3 3.7 %all-to-all-start.1 = ((bf16[4,528,128]{2,1,0:T(8,128)(2,1)}), bf16[4,528,128]{2,1,0:T(8,128)(2,1)S(1)}, u32[]{:S(2)}, u32[]{:S(2)}) async-start(bf16[4,528,128]{2,1,0:T(8,128)(2,1)} %shard_map.73.refs_0_), calls=%async_computation.1 | async-start | bytes 1081344 | tf_op jit(solution)/shard_map/all_to_all | solution.py:29
  45.0 0.0 collective-permute-done.14.refs_2_
  45.0 2.0 %collective-permute-start.9 = (bf16[80,1024]{1,0:T(8,128)(2,1)S(1)}, bf16[80,1024]{1,0:T(8,128)(2,1)S(1)}, u32[]{:S(2)}, u32[]{:S(2)}) collective-permute-start(bf16[80,1024]{1,0:T(8,128)(2,1)S(1)} %get-tuple-element.27), channel_id=1, source_target_pairs={{0,2},{1,3},{2,0},{3,1},{4,6},{5,7},{6,4},{7,5},{8,10},{9,11},{10,... | collective-permute-start | bytes 491528 | tf_op jit(solution)/shard_map/ppermute | solution.py:25
  47.0 1.4 %copy-done.5 = bf16[768,1024]{1,0:T(8,128)(2,1)S(1)} copy-done((bf16[768,1024]{1,0:T(8,128)(2,1)S(1)}, bf16[768,1024]{1,0:T(8,128)(2,1)}, u32[]{:S(2)}) %copy-start.5) | copy-done | bytes 1572888
  48.4 0.9 %copy-done.9 = bf16[64,768]{1,0:T(8,128)(2,1)S(1)} copy-done((bf16[64,768]{1,0:T(8,128)(2,1)S(1)}, bf16[64,768]{1,0:T(8,128)(2,1)}, u32[]{:S(2)}) %copy-start.9) | copy-done | bytes 98328
  49.3 0.4 shard_map.75.refs_1_
  49.7 0.0 copy-start.6
  49.7 0.7 %copy-done.6 = f32[64,1024]{1,0:T(8,128)} copy-done((f32[64,1024]{1,0:T(8,128)}, f32[64,1024]{1,0:T(8,128)S(1)}, u32[]{:S(2)}) %copy-start.6) | copy-done | bytes 262168
  50.4 0.0 collective-permute-done.13.refs_1_
  50.4 0.4 collective-permute-done.12.refs_0_
  50.9 4.3 %all-to-all-done.1.refs_3_.refs_1_ = bf16[4,528,128]{2,1,0:T(8,128)(2,1)S(1)} async-done(((bf16[4,528,128]{2,1,0:T(8,128)(2,1)}), bf16[4,528,128]{2,1,0:T(8,128)(2,1)S(1)}, u32[]{:S(2)}, u32[]{:S(2)}) %all-to-all-start.1) | async-done | bytes 540704 | tf_op jit(solution)/shard_map/all_to_all | solution.py:29
  55.2 0.0 collective-permute-start.15
  55.2 0.5 collective-permute-start.16
  55.7 0.0 collective-permute-done.10.refs_4_
  55.7 0.0 collective-permute-start.17
  55.7 0.0 collective-permute-done.11.refs_5_
  55.7 0.0 collective-permute-done.9.refs_3_
  55.7 0.4 copy-done.7
  56.1 1.7 %shard_map.76 = (bf16[64,1024]{1,0:T(8,128)(2,1)}, bf16[64,512]{1,0:T(8,128)(2,1)}) custom-call(s32[2]{0:T(128)S(1)} %pad_add_fusion.refs_0_.refs_2_.refs_1_, f32[64,1024]{1,0:T(8,128)S(1)} %copy-done.7, bf16[64,256]{1,0:T(8,128)(2,1)S(1)} %copy-done.11, bf16[80,1024]{1,0:T(8,128)(2,1)S(1)} %collective-permute-done.9.refs_3_, ...), custom_call_target="tpu_custom_call" | custom-call | flops 10000000000 | tf_op jit(solution)/shard_map/pallas_call | solution.py:36
  57.8 0.0 collective-permute-done.15.refs_5_
  57.8 0.0 collective-permute-done.16.refs_7_
  57.8 0.7 %collective-permute-done.17.refs_9_ = bf16[256,1024]{1,0:T(8,128)(2,1)S(1)} collective-permute-done((bf16[256,1024]{1,0:T(8,128)(2,1)S(1)}, bf16[256,1024]{1,0:T(8,128)(2,1)S(1)}, u32[]{:S(2)}, u32[]{:S(2)}) %collective-permute-start.17) | collective-permute-done | bytes 524320 | tf_op jit(solution)/shard_map/ppermute | solution.py:25
  58.6 4.1 %shard_map.78 = f32[128,3072]{1,0:T(8,128)} custom-call(s32[1]{0:T(128)} %bitcast.3.refs_0_, bf16[4,528,128]{2,1,0:T(8,128)(2,1)S(1)} %all-to-all-done.1.refs_3_.refs_1_, bf16[256,1024]{1,0:T(8,128)(2,1)S(1)} %shard_map.69.refs_5_.refs_2_, bf16[256,1024]{1,0:T(8,128)(2,1)S(1)} %collective-permute-done.6.refs_6_.refs_3_, ...), custom_call_target="tpu_custom_call" | custom-call | flops 10000000000 | tf_op jit(solution)/shard_map/pallas_call | solution.py:36
  (14 shorter events, 0.1 us)
Async XLA Ops:
  0.6 17.4 %collective-permute-start.4 = (bf16[64,1024]{1,0:T(8,128)(2,1)}, bf16[64,1024]{1,0:T(8,128)(2,1)S(1)}, u32[]{:S(2)}, u32[]{:S(2)}) collective-permute-start(bf16[64,1024]{1,0:T(8,128)(2,1)} %refs_2_.1), channel_id=1, source_target_pairs={{0,4},{1,5},{2,6},{3,7},{4,0},{5,1},{6,2},{7,3},{8,12},{9,13},{10,... | collective-permute-start | bytes 393224 | tf_op jit(solution)/shard_map/ppermute | solution.py:25
  4.7 13.4 %collective-permute-start.3 = (bf16[64,1024]{1,0:T(8,128)(2,1)}, bf16[64,1024]{1,0:T(8,128)(2,1)S(1)}, u32[]{:S(2)}, u32[]{:S(2)}) collective-permute-start(bf16[64,1024]{1,0:T(8,128)(2,1)} %refs_2_.1), channel_id=1, source_target_pairs={{0,2},{1,3},{2,0},{3,1},{4,6},{5,7},{6,4},{7,5},{8,10},{9,11},{10,... | collective-permute-start | bytes 393224 | tf_op jit(solution)/shard_map/ppermute | solution.py:25
  6.3 11.8 %collective-permute-start.5 = (bf16[64,1024]{1,0:T(8,128)(2,1)}, bf16[64,1024]{1,0:T(8,128)(2,1)S(1)}, u32[]{:S(2)}, u32[]{:S(2)}) collective-permute-start(bf16[64,1024]{1,0:T(8,128)(2,1)} %refs_2_.1), channel_id=1, source_target_pairs={{0,6},{1,7},{2,4},{3,5},{4,2},{5,3},{6,0},{7,1},{8,14},{9,15},{10,... | collective-permute-start | bytes 393224 | tf_op jit(solution)/shard_map/ppermute | solution.py:25
  7.6 10.6 %all-to-all-start = ((s32[8,1,8]{2,1,0:T(1,128)}), s32[8,1,8]{2,1,0:T(1,128)S(1)}, u32[]{:S(2)}, u32[]{:S(2)}) async-start(s32[8,1,8]{2,1,0:T(1,128)} %broadcast_in_dim.12), calls=%async_computation | async-start | bytes 8192 | tf_op jit(solution)/shard_map/all_to_all | solution.py:29
  12.7 0.8 %copy-start.2 = (bf16[64,512]{1,0:T(8,128)(2,1)S(1)}, bf16[64,512]{1,0:T(8,128)(2,1)}, u32[]{:S(2)}) copy-start(bf16[64,512]{1,0:T(8,128)(2,1)} %refs_1_.1) | copy-start | bytes 196612
  13.6 4.5 %copy-start = (bf16[128,3072]{1,0:T(8,128)(2,1)S(1)}, bf16[128,3072]{1,0:T(8,128)(2,1)}, u32[]{:S(2)}) copy-start(bf16[128,3072]{1,0:T(8,128)(2,1)} %refs_0_.1) | copy-start | bytes 2359300
  13.6 4.6 %copy-start.1 = (bf16[64,1024]{1,0:T(8,128)(2,1)S(1)}, bf16[64,1024]{1,0:T(8,128)(2,1)}, u32[]{:S(2)}) copy-start(bf16[64,1024]{1,0:T(8,128)(2,1)} %refs_2_.1) | copy-start | bytes 393220
  14.1 6.4 %collective-permute-start.1 = (bf16[64,256]{1,0:T(8,128)(2,1)S(1)}, bf16[64,256]{1,0:T(8,128)(2,1)S(1)}, u32[]{:S(2)}, u32[]{:S(2)}) collective-permute-start(bf16[64,256]{1,0:T(8,128)(2,1)S(1)} %get-tuple-element.19), channel_id=1, source_target_pairs={{0,6},{1,7},{2,4},{3,5},{4,2},{5,3},{6,0},{7,1},{8,14},{9,15},{10,... | collective-permute-start | bytes 98312 | tf_op jit(solution)/shard_map/ppermute | solution.py:25
  18.0 3.9 %collective-permute-start = (bf16[64,256]{1,0:T(8,128)(2,1)S(1)}, bf16[64,256]{1,0:T(8,128)(2,1)S(1)}, u32[]{:S(2)}, u32[]{:S(2)}) collective-permute-start(bf16[64,256]{1,0:T(8,128)(2,1)S(1)} %get-tuple-element.19), channel_id=1, source_target_pairs={{0,2},{1,3},{2,0},{3,1},{4,6},{5,7},{6,4},{7,5},{8,10},{9,11},{10,... | collective-permute-start | bytes 98312 | tf_op jit(solution)/shard_map/ppermute | solution.py:25
  18.0 2.4 %collective-permute-start.2 = (bf16[128,3072]{1,0:T(8,128)(2,1)S(1)}, bf16[128,3072]{1,0:T(8,128)(2,1)S(1)}, u32[]{:S(2)}, u32[]{:S(2)}) collective-permute-start(bf16[128,3072]{1,0:T(8,128)(2,1)S(1)} %copy-done), channel_id=1, source_target_pairs={{0,1},{1,0},{2,3},{3,2},{4,5},{5,4},{6,7},{7,6},{8,9},{9,8},{10,11... | collective-permute-start | bytes 2359304 | tf_op jit(solution)/shard_map/ppermute | solution.py:25
  18.2 3.7 %collective-permute-start.6 = (bf16[256,1024]{1,0:T(8,128)(2,1)S(1)}, bf16[256,1024]{1,0:T(8,128)(2,1)S(1)}, u32[]{:S(2)}, u32[]{:S(2)}) collective-permute-start(bf16[256,1024]{1,0:T(8,128)(2,1)S(1)} %shard_map.69.refs_5_.refs_2_), channel_id=1, source_target_pairs={{0,1},{1,0},{2,3},{3,2},{4,5},{5,4},{6,7},{7,6},{8,9},{9,8},{10,11... | collective-permute-start | bytes 1572872 | tf_op jit(solution)/shard_map/ppermute | solution.py:25
  20.5 3.1 %copy-start.3 = (bf16[768,1024]{1,0:T(8,128)(2,1)}, bf16[768,1024]{1,0:T(8,128)(2,1)S(1)}, u32[]{:S(2)}) copy-start(bf16[768,1024]{1,0:T(8,128)(2,1)S(1)} %shard_map.68.refs_4_.refs_3_.refs_2_) | copy-start | bytes 4718596
  23.6 9.9 %collective-permute-start.7 = (bf16[320,256]{1,0:T(8,128)(2,1)S(1)}, bf16[320,256]{1,0:T(8,128)(2,1)S(1)}, u32[]{:S(2)}, u32[]{:S(2)}) collective-permute-start(bf16[320,256]{1,0:T(8,128)(2,1)S(1)} %get-tuple-element.21.refs_0_), channel_id=1, source_target_pairs={{0,4},{1,5},{2,6},{3,7},{4,0},{5,1},{6,2},{7,3},{8,12},{9,13},{10,... | collective-permute-start | bytes 491528 | tf_op jit(solution)/shard_map/ppermute | solution.py:25
  23.7 21.3 %collective-permute-start.14 = (bf16[256,1024]{1,0:T(8,128)(2,1)S(1)}, bf16[256,1024]{1,0:T(8,128)(2,1)S(1)}, u32[]{:S(2)}, u32[]{:S(2)}) collective-permute-start(bf16[256,1024]{1,0:T(8,128)(2,1)S(1)} %shard_map.69.refs_5_.refs_2_), channel_id=1, source_target_pairs={{0,24},{8,16},{16,8},{24,0},{1,25},{9,17},{17,9},{25,1},{2,26},{10... | collective-permute-start | bytes 1572872 | tf_op jit(solution)/shard_map/ppermute | solution.py:25
  26.2 24.2 %collective-permute-start.13 = (bf16[256,1024]{1,0:T(8,128)(2,1)S(1)}, bf16[256,1024]{1,0:T(8,128)(2,1)S(1)}, u32[]{:S(2)}, u32[]{:S(2)}) collective-permute-start(bf16[256,1024]{1,0:T(8,128)(2,1)S(1)} %shard_map.69.refs_5_.refs_2_), channel_id=1, source_target_pairs={{0,16},{8,24},{16,0},{24,8},{1,17},{9,25},{17,1},{25,9},{2,18},{10... | collective-permute-start | bytes 1572872 | tf_op jit(solution)/shard_map/ppermute | solution.py:25
  26.7 24.1 %collective-permute-start.12 = (bf16[256,1024]{1,0:T(8,128)(2,1)S(1)}, bf16[256,1024]{1,0:T(8,128)(2,1)S(1)}, u32[]{:S(2)}, u32[]{:S(2)}) collective-permute-start(bf16[256,1024]{1,0:T(8,128)(2,1)S(1)} %shard_map.69.refs_5_.refs_2_), channel_id=1, source_target_pairs={{0,8},{8,0},{16,24},{24,16},{1,9},{9,1},{17,25},{25,17},{2,10},{10... | collective-permute-start | bytes 1572872 | tf_op jit(solution)/shard_map/ppermute | solution.py:25
  34.2 1.8 %copy-start.10 = (bf16[64,256]{1,0:T(8,128)(2,1)}, bf16[64,256]{1,0:T(8,128)(2,1)S(1)}, u32[]{:S(2)}) copy-start(bf16[64,256]{1,0:T(8,128)(2,1)S(1)} %get-tuple-element.26.refs_2_) | copy-start | bytes 98308
  34.2 1.8 %copy-start.4 = (bf16[768,1024]{1,0:T(8,128)(2,1)S(1)}, bf16[768,1024]{1,0:T(8,128)(2,1)}, u32[]{:S(2)}) copy-start(bf16[768,1024]{1,0:T(8,128)(2,1)} %copy-done.3) | copy-start | bytes 4718596
  34.2 1.8 %collective-permute-start.8 = (bf16[256,256]{1,0:T(8,128)(2,1)S(1)}, bf16[256,256]{1,0:T(8,128)(2,1)S(1)}, u32[]{:S(2)}, u32[]{:S(2)}) collective-permute-start(bf16[256,256]{1,0:T(8,128)(2,1)S(1)} %get-tuple-element.23.refs_1_), channel_id=1, source_target_pairs={{0,1},{1,0},{2,3},{3,2},{4,5},{5,4},{6,7},{7,6},{8,9},{9,8},{10,11... | collective-permute-start | bytes 393224 | tf_op jit(solution)/shard_map/ppermute | solution.py:25
  37.8 0.6 %copy-start.8 = (bf16[64,768]{1,0:T(8,128)(2,1)}, bf16[64,768]{1,0:T(8,128)(2,1)S(1)}, u32[]{:S(2)}) copy-start(bf16[64,768]{1,0:T(8,128)(2,1)S(1)} %get-tuple-element.25.refs_1_) | copy-start | bytes 294916
  38.4 17.3 %collective-permute-start.10 = (bf16[64,1024]{1,0:T(8,128)(2,1)}, bf16[64,1024]{1,0:T(8,128)(2,1)}, u32[]{:S(2)}, u32[]{:S(2)}) collective-permute-start(bf16[64,1024]{1,0:T(8,128)(2,1)} %get-tuple-element.28), channel_id=1, source_target_pairs={{0,4},{1,5},{2,6},{3,7},{4,0},{5,1},{6,2},{7,3},{8,12},{9,13},{10,... | collective-permute-start | bytes 393224 | tf_op jit(solution)/shard_map/ppermute | solution.py:25
  38.4 17.3 %collective-permute-start.11 = (bf16[64,1024]{1,0:T(8,128)(2,1)}, bf16[64,1024]{1,0:T(8,128)(2,1)}, u32[]{:S(2)}, u32[]{:S(2)}) collective-permute-start(bf16[64,1024]{1,0:T(8,128)(2,1)} %get-tuple-element.29), channel_id=1, source_target_pairs={{0,6},{1,7},{2,4},{3,5},{4,2},{5,3},{6,0},{7,1},{8,14},{9,15},{10,... | collective-permute-start | bytes 393224 | tf_op jit(solution)/shard_map/ppermute | solution.py:25
  41.3 13.9 %all-to-all-start.1 = ((bf16[4,528,128]{2,1,0:T(8,128)(2,1)}), bf16[4,528,128]{2,1,0:T(8,128)(2,1)S(1)}, u32[]{:S(2)}, u32[]{:S(2)}) async-start(bf16[4,528,128]{2,1,0:T(8,128)(2,1)} %shard_map.73.refs_0_), calls=%async_computation.1 | async-start | bytes 1081344 | tf_op jit(solution)/shard_map/all_to_all | solution.py:29
  45.0 10.7 %collective-permute-start.9 = (bf16[80,1024]{1,0:T(8,128)(2,1)S(1)}, bf16[80,1024]{1,0:T(8,128)(2,1)S(1)}, u32[]{:S(2)}, u32[]{:S(2)}) collective-permute-start(bf16[80,1024]{1,0:T(8,128)(2,1)S(1)} %get-tuple-element.27), channel_id=1, source_target_pairs={{0,2},{1,3},{2,0},{3,1},{4,6},{5,7},{6,4},{7,5},{8,10},{9,11},{10,... | collective-permute-start | bytes 491528 | tf_op jit(solution)/shard_map/ppermute | solution.py:25
  47.0 1.4 %copy-start.5 = (bf16[768,1024]{1,0:T(8,128)(2,1)S(1)}, bf16[768,1024]{1,0:T(8,128)(2,1)}, u32[]{:S(2)}) copy-start(bf16[768,1024]{1,0:T(8,128)(2,1)} %copy-done.3) | copy-start | bytes 4718596
  48.4 0.9 %copy-start.9 = (bf16[64,768]{1,0:T(8,128)(2,1)S(1)}, bf16[64,768]{1,0:T(8,128)(2,1)}, u32[]{:S(2)}) copy-start(bf16[64,768]{1,0:T(8,128)(2,1)} %copy-done.8) | copy-start | bytes 294916
  49.7 0.7 %copy-start.6 = (f32[64,1024]{1,0:T(8,128)}, f32[64,1024]{1,0:T(8,128)S(1)}, u32[]{:S(2)}) copy-start(f32[64,1024]{1,0:T(8,128)S(1)} %shard_map.75.refs_1_) | copy-start | bytes 786436
  50.4 5.3 %copy-start.11 = (bf16[64,256]{1,0:T(8,128)(2,1)S(1)}, bf16[64,256]{1,0:T(8,128)(2,1)}, u32[]{:S(2)}) copy-start(bf16[64,256]{1,0:T(8,128)(2,1)} %copy-done.10) | copy-start | bytes 98308
  55.2 1.0 %copy-start.7 = (f32[64,1024]{1,0:T(8,128)S(1)}, f32[64,1024]{1,0:T(8,128)}, u32[]{:S(2)}) copy-start(f32[64,1024]{1,0:T(8,128)} %copy-done.6) | copy-start | bytes 786436
  55.2 2.7 %collective-permute-start.15 = (bf16[256,1024]{1,0:T(8,128)(2,1)S(1)}, bf16[256,1024]{1,0:T(8,128)(2,1)S(1)}, u32[]{:S(2)}, u32[]{:S(2)}) collective-permute-start(bf16[256,1024]{1,0:T(8,128)(2,1)S(1)} %get-tuple-element.32.refs_4_), channel_id=1, source_target_pairs={{0,1},{1,0},{2,3},{3,2},{4,5},{5,4},{6,7},{7,6},{8,9},{9,8},{10,11... | collective-permute-start | bytes 1572872 | tf_op jit(solution)/shard_map/ppermute | solution.py:25
  55.2 2.7 %collective-permute-start.16 = (bf16[256,1024]{1,0:T(8,128)(2,1)S(1)}, bf16[256,1024]{1,0:T(8,128)(2,1)S(1)}, u32[]{:S(2)}, u32[]{:S(2)}) collective-permute-start(bf16[256,1024]{1,0:T(8,128)(2,1)S(1)} %get-tuple-element.33.refs_6_), channel_id=1, source_target_pairs={{0,1},{1,0},{2,3},{3,2},{4,5},{5,4},{6,7},{7,6},{8,9},{9,8},{10,11... | collective-permute-start | bytes 1572872 | tf_op jit(solution)/shard_map/ppermute | solution.py:25
  55.7 2.9 %collective-permute-start.17 = (bf16[256,1024]{1,0:T(8,128)(2,1)S(1)}, bf16[256,1024]{1,0:T(8,128)(2,1)S(1)}, u32[]{:S(2)}, u32[]{:S(2)}) collective-permute-start(bf16[256,1024]{1,0:T(8,128)(2,1)S(1)} %get-tuple-element.34.refs_8_), channel_id=1, source_target_pairs={{0,1},{1,0},{2,3},{3,2},{4,5},{5,4},{6,7},{7,6},{8,9},{9,8},{10,11... | collective-permute-start | bytes 1572872 | tf_op jit(solution)/shard_map/ppermute | solution.py:25

commit v4 on v3

--- a/solution.py
+++ b/solution.py
@@ -53,9 +53,9 @@
     return pltpu.roll(jnp.where(row >= 4, first, second), 4, 0)
 
 
-def pick(me_ref, grad_ref, *outs):
+def pick(grad_ref, *outs):
     half = outs[0].shape[1] // 2
-    q = lax.rem(me_ref[0], grad_ref.shape[1] // half)
+    q = lax.rem(lax.axis_index("fsdp"), grad_ref.shape[1] // half)
     for pair, out in enumerate(outs):
         for part in range(2):
             start = pl.multiple_of((q ^ (2 * pair + part)) * half, half)
@@ -71,23 +71,29 @@
 
 
 def place(source, seg_count, chips, me):
-    apart = (source // seg_count) ^ me
-    return ((apart & 1) * chips + (apart >> 1)) * seg_count + lax.rem(source, seg_count)
-
-
-def follows(chips, me_ref, table_ref, follow_ref):
+    bits = seg_count.bit_length() - 1
+    apart = lax.shift_right_logical(source, jnp.int32(bits)) ^ me
+    slot = (apart & 1) * chips + lax.shift_right_logical(apart, jnp.int32(1))
+    return slot * seg_count + (source & (seg_count - 1))
+
+
+def follows(chips, table_ref, follow_ref, row_ref):
     peers, seg_count = table_ref.shape
-    me = me_ref[0]
-    for i in range(peers * seg_count):
-        follow_ref[i] = peers * seg_count
+    me = lax.axis_index("fsdp")
+    count = peers * seg_count
+    for i in range(count):
+        follow_ref[i] = count
     for peer in range(peers):
-        slot = place(peer * seg_count, seg_count, chips, me)
+        slot = place(jnp.int32(peer * seg_count), seg_count, chips, me)
         for position in range(seg_count):
             source = table_ref[peer, position]
-
-            @pl.when(source >= 0)
-            def _():
-                follow_ref[place(source, seg_count, chips, me)] = slot + position
+            found = place(jnp.maximum(source, 0), seg_count, chips, me)
+            follow_ref[jnp.where(source >= 0, found, count)] = slot + position
+    lane = lax.broadcasted_iota(jnp.int32, row_ref.shape, 1)
+    value = jnp.zeros(row_ref.shape, jnp.int32)
+    for segment in range(count):
+        value = jnp.where(lane == segment, follow_ref[segment], value)
+    row_ref[...] = value.astype(F32).astype(BF16)
 
 
 def stack(*refs):
@@ -97,10 +103,10 @@
         out_ref[slot * count : (slot + 1) * count, :] = block[...]
 
 
-def forward(me_ref, table_ref, weight_ref, own_ref, other_ref, grad_ref, act_ref, sent_ref, rows_ref, early_ref):
+def forward(table_ref, weight_ref, own_ref, other_ref, grad_ref, act_ref, sent_ref, rows_ref, early_ref):
     own_class = own_ref.shape[0]
     peers, seg_count = table_ref.shape
-    me = me_ref[0]
+    me = lax.axis_index("fsdp")
     rows_ref[:own_class, :] = own_ref[...]
     rows_ref[own_class:, :] = other_ref[...]
     total = 2 * own_class
@@ -113,7 +119,7 @@
     act_ref[...] = lax.dot_general(
         rows_ref[:own_class, :], weight_ref[2 * wide :, :], nt, preferred_element_type=F32
     )
-    is_filter = me_ref[0] < me_ref[1]
+    is_filter = lax.axis_index("fsdp") < lax.axis_size("fsdp") // 2
     for segment in range(own_class // SEG):
         at = segment * SEG
         source = table_ref[me ^ (2 * (segment // seg_count)), segment % seg_count]
@@ -130,10 +136,10 @@
     sent_ref[own_class:, :] = grad_ref[...]
 
 
-def gate(me_ref, act_ref, other_ref, *refs):
+def gate(act_ref, other_ref, *refs):
     grads, outs, pre_ref = list(refs[:-3]), refs[-3:-1], refs[-1]
     count = outs[0].shape[0]
-    is_filter = me_ref[0] < me_ref[1]
+    is_filter = lax.axis_index("fsdp") < lax.axis_size("fsdp") // 2
     slots = len(grads) + 1
     grads.insert(slots // 2, other_ref.at[slots * count :, :])
     for slot, grad in enumerate(grads):
@@ -177,18 +183,13 @@
         out[:count, :] = part[slot * count : (slot + 1) * count, :].astype(BF16)
 
 
-def spread(follow_ref, own_ref, other_ref, copies_ref):
+def spread(own_ref, other_ref, row_ref, copies_ref):
     total, wide = own_ref.shape
     width = wide // 2
-    lane = lax.broadcasted_iota(jnp.int32, (16, width), 1)
-    value = jnp.zeros((16, width), jnp.int32)
-    for segment in range(follow_ref.shape[0]):
-        value = jnp.where(lane == segment, follow_ref[segment], value)
-    value = value.astype(F32).astype(BF16)
     for copy in range(copies_ref.shape[0]):
         copies_ref[copy, :total, :] = own_ref[:, :width]
         copies_ref[copy, total : 2 * total, :] = other_ref[:, width:]
-        copies_ref[copy, 2 * total :, :] = value
+        copies_ref[copy, 2 * total :, :] = row_ref[...]
 
 
 def local(here_ref, weight_ref, out_ref):
@@ -215,20 +216,22 @@
     )(*values, *after)
 
 
-def weight_grad(scale, group_ref, pre_ref, *refs):
-    blocks = refs[:-7]
-    out_ref, early_ref, routed_ref, rows_ref, wide_ref, follow_ref, sem = refs[-7:]
+def weight_grad(scale, pre_ref, *refs):
+    blocks = refs[:-8]
+    out_ref, early_ref, routed_ref, rows_ref, wide_ref, follow_ref, sem, sems = refs[-8:]
     groups, total, width = early_ref.shape
     total -= SEG
     for i in range(groups):
-        wide_ref[i] = pre_ref[group_ref[0] ^ i, total:, :].astype(F32).astype(jnp.int32)
+        wide_ref[i] = pre_ref[lax.axis_index("dp") ^ i, total:, :].astype(F32).astype(jnp.int32)
     load = pltpu.make_async_copy(wide_ref, follow_ref, sem)
     load.start()
+    loads = []
     for i, block in enumerate(blocks):
-        count = block.shape[0]
-        rows_ref[i * count : (i + 1) * count, :] = block[...]
+        rows = pl.ds(i * block.shape[0], block.shape[0])
+        loads.append(pltpu.make_async_copy(block, rows_ref.at[rows, :], sems.at[i]))
+        loads[-1].start()
     for i in range(groups):
-        early_ref[i, :total, :] = pre_ref[group_ref[0] ^ i, :total, :].astype(F32)
+        early_ref[i, :total, :] = pre_ref[lax.axis_index("dp") ^ i, :total, :].astype(F32)
         early_ref[i, total:, :] = jnp.zeros((SEG, width), F32)
     load.wait()
     for i in range(groups):
@@ -241,14 +244,15 @@
             routed_ref[at : at + SEG, :width] = carried
             routed_ref[at : at + SEG, width : 2 * width] = roll_half(local, carried)
             routed_ref[at : at + SEG, 2 * width :] = local
-    product = lax.dot_general(
-        routed_ref[...].astype(BF16), rows_ref[...], (((0,), (0,)), ((), ())), preferred_element_type=F32
-    )
+    routed = routed_ref[...].astype(BF16)
+    for one in loads:
+        one.wait()
+    product = lax.dot_general(routed, rows_ref[...], (((0,), (0,)), ((), ())), preferred_element_type=F32)
     for tap in range(3):
         out_ref[:, tap * C : (tap + 1) * C] = product[tap * width : (tap + 1) * width, :] * scale
 
 
-def finish(me_ref, kept_ref, gated_ref, *refs):
+def finish(kept_ref, gated_ref, *refs):
     parts, (grad_ref, out_ref) = refs[:-2], refs[-2:]
     count = grad_ref.shape[0]
     total = kept_ref[...]
@@ -259,7 +263,7 @@
     width = wide // 2
     fold = C // wide
     short = count // fold
-    q = lax.rem(me_ref[0], out_ref.shape[1] // width)
+    q = lax.rem(lax.axis_index("fsdp"), out_ref.shape[1] // width)
     for part in range(2):
         here = slice(part * width, (part + 1) * width)
         out_ref[:, pl.ds(pl.multiple_of((q ^ part) * width, width), width)] = gated_ref[:, here]
@@ -277,14 +281,11 @@
     own_class, all_rows = chips * rows, peers * rows
     wide = 2 * width
     half_chips = chips // 2
-    me = lax.axis_index("fsdp").astype(jnp.int32)
-    group = lax.axis_index("dp").astype(jnp.int32)
-    who = jnp.stack([me, jnp.int32(peers // 2)])
 
     fold = C // wide
     own_rows = [signal] + [swap(signal, "fsdp", 2 * k) for k in range(1, chips)]
     picked = call(
-        pick, [shaped((rows, wide), BF16)] * half_chips, [who, grad_gated], [SMEM, VMEM]
+        pick, [shaped((rows, wide), BF16)] * half_chips, [grad_gated], [VMEM]
     )
     other_weight = swap(conv_weight, "fsdp", 1)
     weight = call(
@@ -299,27 +300,27 @@
     act, sent = call(
         forward,
         [shaped((own_class, wide), F32), shaped((own_class + rows, wide), BF16)],
-        [who, table, weight, own_stack, other_stack, picked[0]],
-        [SMEM, SMEM] + [VMEM] * 4,
+        [table, weight, own_stack, other_stack, picked[0]],
+        [SMEM] + [VMEM] * 4,
         [pltpu.VMEM((all_rows, C), BF16), pltpu.VMEM((all_rows + SEG, 2 * wide), F32)],
         after=grads[1:],
     )
     partner = swap(sent, "fsdp", peers // 2)
     far_own = [swap(own_stack, "dp", d) for d in (1, 2, 3)]
-    follow = call(
+    follow, follow_row = call(
         functools.partial(follows, chips),
-        [shaped((peers * seg_count,), jnp.int32)],
-        [who, table],
-        [SMEM, SMEM],
-        out_specs=[SMEM],
+        [shaped((peers * seg_count + 1,), jnp.int32), shaped((16, width), BF16)],
+        [table],
+        [SMEM],
+        out_specs=[SMEM, VMEM],
         after=[sent],
-    )[0]
+    )
 
     *gated, pre = call(
         gate,
         [shaped((rows, wide), BF16)] * half_chips + [shaped((own_class, wide), BF16)],
-        [who, act, partner, *grads],
-        [SMEM] + [VMEM] * (2 + len(grads)),
+        [act, partner, *grads],
+        [VMEM] * (2 + len(grads)),
     )
     other_pre = swap(pre, "fsdp", 1)
     *sends, here = call(
@@ -335,27 +336,27 @@
     sent_pre = call(
         spread,
         [shaped((groups, all_rows + 16, width), BF16)],
-        [follow, pre, other_pre],
-        [SMEM, VMEM, VMEM],
+        [pre, other_pre, follow_row],
+        [VMEM] * 3,
     )[0]
     all_pre = exchange(sent_pre, "dp")
     kept = call(
-        local, [shaped((rows, C), F32)], [here, weight], [VMEM] * 2, after=[sent_pre]
+        local, [shaped((rows, C), F32)], [here, weight], [VMEM] * 2, after=[sent_pre, *far_own]
     )[0]
     grad_in, gated_out = call(
         finish,
         [shaped((rows, C), BF16), shaped((rows, H), BF16)],
-        [who, kept, gated[0], *parts],
-        [SMEM] + [VMEM] * (chips + 1),
-    )
-    far_own = held(far_own, [all_pre])
+        [kept, gated[0], *parts],
+        [VMEM] * (chips + 1),
+    )
+    far_own = held(far_own, [kept])
     far_other = [swap(block, "fsdp", 1) for block in far_own]
     blocks = [own_stack, other_stack] + [block for pair in zip(far_own, far_other) for block in pair]
     grad_weight = call(
         functools.partial(weight_grad, 1.0 / math.sqrt(all_rows * groups)),
         [shaped((width, 3 * C), F32)],
-        [group[None], all_pre, *blocks],
-        [SMEM] + [VMEM] * (1 + len(blocks)),
+        [all_pre, *blocks],
+        [VMEM] + [ANY] * len(blocks),
         [
             pltpu.VMEM((groups, all_rows + SEG, width), F32),
             pltpu.VMEM((groups * all_rows, 3 * width), F32),
@@ -363,6 +364,7 @@
             pltpu.VMEM((groups, 16, width), jnp.int32),
             pltpu.SMEM((groups, 16, width), jnp.int32),
             pltpu.SemaphoreType.DMA,
+            pltpu.SemaphoreType.DMA((len(blocks),)),
         ],
         room=24,
     )[0]
@@ -479,6 +481,7 @@
         and groups * peers * rows <= 2048
         and rows % 64 == 0
         and peers * seg_count <= 128
+        and seg_count & (seg_count - 1) == 0
     )
     plan = by_channels if fits else by_rows
     return plan(signal, grad_gated, conv_weight, source_seg)

time: 63 us -> 61 us (0.968)
  local copies, waits for them, and re-layouts: 6.16 us -> 3.59 us
  waiting for transfers between devices: 14.9 us -> 16.8 us
  Pallas kernels: 14 us -> 12.7 us
    ppermute x18, waiting for transfers between devices: 10.6 us -> 15.6 us  [swap(): return lax.ppermute(value, axis, [(i, i ^ distance) for i in range(count)])]
    all_to_all x2, waiting for transfers between devices: 4.32 us -> 1.13 us  [exchange(): return lax.all_to_all(copies, axis, split_axis=0, concat_axis=0, tiled=True)]
    unnamed x24 -> x14, local copies, waits for them, and re-layouts: 4.91 us -> 2.34 us
    pallas_call x11, Pallas kernels: 14 us -> 12.7 us  [call(): pl.pallas_call(run, out_shape=out_shapes, in_specs=[ANY] * len(after) + l...]
  transfers between devices with their start and end apart: 20 -> 20, of which waited for: 6 -> 7; matrix products, arithmetic and copies ran while one was open for 2% -> 2% of each run, Pallas kernels for 13% -> 11%
where the time goes in v4:
time: 61 us; the launch traced here: 60.6 us
  starting transfers between devices  26.7 us (44%)
  waiting for transfers between devices  16.8 us (28%)
  Pallas kernels  12.7 us (21%)
  local copies, waits for them, and re-layouts  3.59 us (6%)
  between operations  0.8 us (1%)
    ppermute x18, starting transfers between devices, swap(): return lax.ppermute(value, axis, [(i, i ^ distance) for i in range(count)])  17.9 us
    ppermute x18, waiting for transfers between devices, swap(): return lax.ppermute(value, axis, [(i, i ^ distance) for i in range(count)])  15.6 us
    pallas_call x11, Pallas kernels, call(): pl.pallas_call(run, out_shape=out_shapes, in_specs=[ANY] * len(after) + l...  12.7 us
    all_to_all x2, starting transfers between devices, exchange(): return lax.all_to_all(copies, axis, split_axis=0, concat_axis=0, tiled=True)  8.81 us
    unnamed x14, local copies, waits for them, and re-layouts  2.34 us
    broadcast_in_dim x1, local copies, waits for them, and re-layouts, by_channels(): jnp.broadcast_to(source_seg[None], (peers, 1, seg_count))  1.25 us
  transfers between devices with their start and end apart: 20, of which 7 were waited for; matrix products, arithmetic and copies ran while one was open for 2% of the time, Pallas kernels for 11%

profile of v4, /device:TPU:0, one launch (start us, length us, event | category | flops | bytes accessed | tf_op | source)
XLA Modules:
  0.0 60.6 jit_solution(11731621096126406839)
XLA Ops:
  0.6 4.1 %collective-permute-start.4 = (bf16[64,1024]{1,0:T(8,128)(2,1)}, bf16[64,1024]{1,0:T(8,128)(2,1)S(1)}, u32[]{:S(2)}, u32[]{:S(2)}) collective-permute-start(bf16[64,1024]{1,0:T(8,128)(2,1)} %refs_2_.1), channel_id=1, source_target_pairs={{0,4},{1,5},{2,6},{3,7},{4,0},{5,1},{6,2},{7,3},{8,12},{9,13},{10,... | collective-permute-start | bytes 393224 | tf_op jit(solution)/shard_map/ppermute | solution.py:25
  4.7 1.6 %collective-permute-start.3 = (bf16[64,1024]{1,0:T(8,128)(2,1)}, bf16[64,1024]{1,0:T(8,128)(2,1)S(1)}, u32[]{:S(2)}, u32[]{:S(2)}) collective-permute-start(bf16[64,1024]{1,0:T(8,128)(2,1)} %refs_2_.1), channel_id=1, source_target_pairs={{0,2},{1,3},{2,0},{3,1},{4,6},{5,7},{6,4},{7,5},{8,10},{9,11},{10,... | collective-permute-start | bytes 393224 | tf_op jit(solution)/shard_map/ppermute | solution.py:25
  6.3 0.0 collective-permute-start.5
  6.3 1.2 %broadcast_in_dim.9 = s32[8,1,8]{2,1,0:T(1,128)} broadcast(s32[8]{0:T(128)} %bitcast.5), dimensions={2} | broadcast | bytes 288 | tf_op jit(solution)/shard_map/broadcast_in_dim | solution.py:294
  7.6 5.1 %all-to-all-start = ((s32[8,1,8]{2,1,0:T(1,128)}), s32[8,1,8]{2,1,0:T(1,128)S(1)}, u32[]{:S(2)}, u32[]{:S(2)}) async-start(s32[8,1,8]{2,1,0:T(1,128)} %broadcast_in_dim.9), calls=%async_computation | async-start | bytes 8192 | tf_op jit(solution)/shard_map/all_to_all | solution.py:29
  12.7 0.0 copy-start.2
  12.7 0.8 %copy-done.2 = bf16[64,512]{1,0:T(8,128)(2,1)S(1)} copy-done((bf16[64,512]{1,0:T(8,128)(2,1)S(1)}, bf16[64,512]{1,0:T(8,128)(2,1)}, u32[]{:S(2)}) %copy-start.2) | copy-done | bytes 65560
  13.5 0.0 copy-start
  13.5 0.0 copy-start.1
  13.5 3.9 %collective-permute-start.1 = (bf16[64,256]{1,0:T(8,128)(2,1)S(1)}, bf16[64,256]{1,0:T(8,128)(2,1)S(1)}, u32[]{:S(2)}, u32[]{:S(2)}) collective-permute-start(bf16[64,256]{1,0:T(8,128)(2,1)S(1)} %get-tuple-element.21), channel_id=1, source_target_pairs={{0,6},{1,7},{2,4},{3,5},{4,2},{5,3},{6,0},{7,1},{8,14},{9,15},{10,... | collective-permute-start | bytes 98312 | tf_op jit(solution)/shard_map/ppermute | solution.py:25
  17.4 0.0 collective-permute-start
  17.4 0.0 collective-permute-done.4.refs_4_
  17.4 0.0 copy-done
  17.4 0.1 collective-permute-start.2
  17.5 0.6 %all-to-all-done = s32[8,1,8]{2,1,0:T(1,128)S(1)} async-done(((s32[8,1,8]{2,1,0:T(1,128)}), s32[8,1,8]{2,1,0:T(1,128)S(1)}, u32[]{:S(2)}, u32[]{:S(2)}) %all-to-all-start) | async-done | bytes 288 | tf_op jit(solution)/shard_map/all_to_all | solution.py:29
  18.1 0.0 collective-permute-done.3.refs_3_
  18.1 0.0 collective-permute-done.5.refs_5_
  18.1 0.0 copy-done.1
  18.2 0.1 collective-permute-start.6
  18.3 1.5 %collective-permute-done.2.refs_1_ = bf16[128,3072]{1,0:T(8,128)(2,1)S(1)} collective-permute-done((bf16[128,3072]{1,0:T(8,128)(2,1)S(1)}, bf16[128,3072]{1,0:T(8,128)(2,1)S(1)}, u32[]{:S(2)}, u32[]{:S(2)}) %collective-permute-start.2) | collective-permute-done | bytes 786464 | tf_op jit(solution)/shard_map/ppermute | solution.py:25
  19.8 0.1 shard_map.68.refs_3_.refs_5_
  19.9 0.0 copy-start.3
  19.9 0.0 collective-permute-done.1.refs_1_.refs_4_
  19.9 1.4 %collective-permute-done.refs_0_.refs_3_ = bf16[64,256]{1,0:T(8,128)(2,1)S(1)} collective-permute-done((bf16[64,256]{1,0:T(8,128)(2,1)S(1)}, bf16[64,256]{1,0:T(8,128)(2,1)S(1)}, u32[]{:S(2)}, u32[]{:S(2)}) %collective-permute-start) | collective-permute-done | bytes 32800 | tf_op jit(solution)/shard_map/ppermute | solution.py:25
  21.3 0.0 collective-permute-done.6.refs_5_.refs_2_
  21.3 1.6 %shard_map.70 = (f32[256,256]{1,0:T(8,128)S(1)}, bf16[320,256]{1,0:T(8,128)(2,1)S(1)}) custom-call(bf16[64,256]{1,0:T(8,128)(2,1)S(1)} %collective-permute-done.refs_0_.refs_3_, bf16[64,256]{1,0:T(8,128)(2,1)S(1)} %collective-permute-done.1.refs_1_.refs_4_, s32[8,8]{1,0:T(8,128)S(1)} %bitcast.3, bf16[768,1024]{1,0:T(8,128)(2,1)S(1)} %shard_map.68.refs_3_.refs_5_, ...), custom_call_target="tpu_custom_call" | custom-call | flops 10000000000 | tf_op jit(solution)/shard_map/pallas_call | solution.py:36
  23.0 0.5 collective-permute-start.7
  23.5 2.5 %collective-permute-start.11 = (bf16[256,1024]{1,0:T(8,128)(2,1)S(1)}, bf16[256,1024]{1,0:T(8,128)(2,1)S(1)}, u32[]{:S(2)}, u32[]{:S(2)}) collective-permute-start(bf16[256,1024]{1,0:T(8,128)(2,1)S(1)} %shard_map.69.refs_4_.refs_1_), channel_id=1, source_target_pairs={{0,24},{8,16},{16,8},{24,0},{1,25},{9,17},{17,9},{25,1},{2,26},{10... | collective-permute-start | bytes 1572872 | tf_op jit(solution)/shard_map/ppermute | solution.py:25
  25.9 0.5 collective-permute-start.10
  26.4 0.5 collective-permute-start.9
  26.9 5.9 %collective-permute-done.7.refs_1_ = bf16[320,256]{1,0:T(8,128)(2,1)S(1)} collective-permute-done((bf16[320,256]{1,0:T(8,128)(2,1)S(1)}, bf16[320,256]{1,0:T(8,128)(2,1)S(1)}, u32[]{:S(2)}, u32[]{:S(2)}) %collective-permute-start.7) | collective-permute-done | bytes 163872 | tf_op jit(solution)/shard_map/ppermute | solution.py:25
  32.9 0.1 shard_map.71
  33.0 0.0 copy-start.5
  33.0 0.1 collective-permute-start.8
  33.1 1.6 %shard_map.72 = (s32[65]{0:T(128)S(1)}, bf16[16,128]{1,0:T(8,128)(2,1)S(1)}) custom-call(bf16[320,256]{1,0:T(8,128)(2,1)S(1)} %get-tuple-element.24.refs_0_, s32[8,8]{1,0:T(8,128)S(1)} %bitcast.4), custom_call_target="tpu_custom_call" | custom-call | flops 10000000000 | tf_op jit(solution)/shard_map/pallas_call | solution.py:36
  34.6 0.0 copy-done.5
  34.7 0.0 collective-permute-done.8.refs_1_.refs_2_
  34.7 0.0 copy-done.3
  34.7 1.7 %shard_map.74 = (bf16[80,1024]{1,0:T(8,128)(2,1)S(1)}, bf16[64,1024]{1,0:T(8,128)(2,1)}, bf16[64,1024]{1,0:T(8,128)(2,1)}, bf16[64,768]{1,0:T(8,128)(2,1)S(1)}) custom-call(s32[65]{0:T(128)S(1)} %get-tuple-element.27.refs_0_, bf16[256,256]{1,0:T(8,128)(2,1)S(1)} %get-tuple-element.25.refs_0_.refs_1_, ...), custom_call_target="tpu_custom_call" | custom-call | flops 10000000000 | tf_op jit(solution)/shard_map/pallas_call | solution.py:36
  36.4 0.0 collective-permute-start.13
  36.4 2.1 %collective-permute-start.14 = (bf16[64,1024]{1,0:T(8,128)(2,1)}, bf16[64,1024]{1,0:T(8,128)(2,1)}, u32[]{:S(2)}, u32[]{:S(2)}) collective-permute-start(bf16[64,1024]{1,0:T(8,128)(2,1)} %get-tuple-element.33), channel_id=1, source_target_pairs={{0,6},{1,7},{2,4},{3,5},{4,2},{5,3},{6,0},{7,1},{8,14},{9,15},{10,... | collective-permute-start | bytes 393224 | tf_op jit(solution)/shard_map/ppermute | solution.py:25
  38.5 0.9 %shard_map.73.refs_0_ = bf16[4,528,128]{2,1,0:T(8,128)(2,1)} custom-call(bf16[256,256]{1,0:T(8,128)(2,1)S(1)} %get-tuple-element.25.refs_0_.refs_1_, bf16[256,256]{1,0:T(8,128)(2,1)S(1)} %collective-permute-done.8.refs_1_.refs_2_, bf16[16,128]{1,0:T(8,128)(2,1)S(1)} %get-tuple-element.26.refs_2_), custom_call_target="tpu_custom_call" | custom-call | flops 10000000000 | tf_op jit(solution)/shard_map/pallas_call | solution.py:36
  39.4 3.7 %all-to-all-start.1 = ((bf16[4,528,128]{2,1,0:T(8,128)(2,1)}), bf16[4,528,128]{2,1,0:T(8,128)(2,1)S(1)}, u32[]{:S(2)}, u32[]{:S(2)}) async-start(bf16[4,528,128]{2,1,0:T(8,128)(2,1)} %shard_map.73.refs_0_), calls=%async_computation.1 | async-start | bytes 1081344 | tf_op jit(solution)/shard_map/all_to_all | solution.py:29
  43.1 0.0 collective-permute-done.11.refs_3_.refs_2_
  43.1 1.4 %collective-permute-start.12 = (bf16[80,1024]{1,0:T(8,128)(2,1)S(1)}, bf16[80,1024]{1,0:T(8,128)(2,1)S(1)}, u32[]{:S(2)}, u32[]{:S(2)}) collective-permute-start(bf16[80,1024]{1,0:T(8,128)(2,1)S(1)} %get-tuple-element.31), channel_id=1, source_target_pairs={{0,2},{1,3},{2,0},{3,1},{4,6},{5,7},{6,4},{7,5},{8,10},{9,11},{10,... | collective-permute-start | bytes 491528 | tf_op jit(solution)/shard_map/ppermute | solution.py:25
  44.5 6.0 %collective-permute-done.10.refs_2_.refs_1_ = bf16[256,1024]{1,0:T(8,128)(2,1)S(1)} collective-permute-done((bf16[256,1024]{1,0:T(8,128)(2,1)S(1)}, bf16[256,1024]{1,0:T(8,128)(2,1)S(1)}, u32[]{:S(2)}, u32[]{:S(2)}) %collective-permute-start.10) | collective-permute-done | bytes 524320 | tf_op jit(solution)/shard_map/ppermute | solution.py:25
  50.5 0.0 collective-permute-done.9.refs_1_.refs_0_
  50.5 0.0 copy-start.4
  50.5 1.4 %copy-done.4 = bf16[768,1024]{1,0:T(8,128)(2,1)S(1)} copy-done((bf16[768,1024]{1,0:T(8,128)(2,1)S(1)}, bf16[768,1024]{1,0:T(8,128)(2,1)}, u32[]{:S(2)}) %copy-start.4) | copy-done | bytes 1572888
  51.9 0.4 shard_map.75.refs_0_.refs_3_
  52.3 0.0 copy-start.6
  52.3 0.1 collective-permute-start.15
  52.4 0.5 collective-permute-start.16
  52.9 0.0 collective-permute-done.13.refs_3_
  52.9 0.1 collective-permute-start.17
  53.0 0.0 collective-permute-done.14.refs_4_
  53.0 0.0 collective-permute-done.12.refs_2_
  53.0 0.1 copy-done.6
  53.1 1.6 %shard_map.76 = (bf16[64,1024]{1,0:T(8,128)(2,1)}, bf16[64,512]{1,0:T(8,128)(2,1)}) custom-call(f32[64,1024]{1,0:T(8,128)S(1)} %shard_map.75.refs_0_.refs_3_, bf16[64,256]{1,0:T(8,128)(2,1)S(1)} %copy-done.6, bf16[80,1024]{1,0:T(8,128)(2,1)S(1)} %collective-permute-done.12.refs_2_, bf16[64,1024]{1,0:T(8,128)(2,1)S(1)} %collective-permute-done.13.refs_3_, ...), custom_call_target="tpu_custom_call" | custom-call | flops 10000000000 | tf_op jit(solution)/shard_map/pallas_call | solution.py:36
  54.7 0.5 all-to-all-done.1.refs_0_
  55.2 0.0 collective-permute-done.15.refs_4_
  55.2 0.0 collective-permute-done.16.refs_6_
  55.2 0.7 %collective-permute-done.17.refs_8_ = bf16[256,1024]{1,0:T(8,128)(2,1)} collective-permute-done((bf16[256,1024]{1,0:T(8,128)(2,1)S(1)}, bf16[256,1024]{1,0:T(8,128)(2,1)}, u32[]{:S(2)}, u32[]{:S(2)}) %collective-permute-start.17) | collective-permute-done | bytes 524320 | tf_op jit(solution)/shard_map/ppermute | solution.py:25
  55.9 4.6 %shard_map.78 = f32[128,3072]{1,0:T(8,128)} custom-call(bf16[4,528,128]{2,1,0:T(8,128)(2,1)S(1)} %all-to-all-done.1.refs_0_, bf16[256,1024]{1,0:T(8,128)(2,1)S(1)} %shard_map.69.refs_4_.refs_1_, bf16[256,1024]{1,0:T(8,128)(2,1)S(1)} %collective-permute-done.6.refs_5_.refs_2_, bf16[256,1024]{1,0:T(8,128)(2,1)S(1)} %get-tuple-element.36.refs_3_, ...), custom_call_target="tpu_custom_call" | custom-call | flops 10000000000 | tf_op jit(solution)/shard_map/pallas_call | solution.py:36
  (3 shorter events, 0.1 us)
Async XLA Ops:
  0.6 16.8 %collective-permute-start.4 = (bf16[64,1024]{1,0:T(8,128)(2,1)}, bf16[64,1024]{1,0:T(8,128)(2,1)S(1)}, u32[]{:S(2)}, u32[]{:S(2)}) collective-permute-start(bf16[64,1024]{1,0:T(8,128)(2,1)} %refs_2_.1), channel_id=1, source_target_pairs={{0,4},{1,5},{2,6},{3,7},{4,0},{5,1},{6,2},{7,3},{8,12},{9,13},{10,... | collective-permute-start | bytes 393224 | tf_op jit(solution)/shard_map/ppermute | solution.py:25
  4.7 13.4 %collective-permute-start.3 = (bf16[64,1024]{1,0:T(8,128)(2,1)}, bf16[64,1024]{1,0:T(8,128)(2,1)S(1)}, u32[]{:S(2)}, u32[]{:S(2)}) collective-permute-start(bf16[64,1024]{1,0:T(8,128)(2,1)} %refs_2_.1), channel_id=1, source_target_pairs={{0,2},{1,3},{2,0},{3,1},{4,6},{5,7},{6,4},{7,5},{8,10},{9,11},{10,... | collective-permute-start | bytes 393224 | tf_op jit(solution)/shard_map/ppermute | solution.py:25
  6.3 11.8 %collective-permute-start.5 = (bf16[64,1024]{1,0:T(8,128)(2,1)}, bf16[64,1024]{1,0:T(8,128)(2,1)S(1)}, u32[]{:S(2)}, u32[]{:S(2)}) collective-permute-start(bf16[64,1024]{1,0:T(8,128)(2,1)} %refs_2_.1), channel_id=1, source_target_pairs={{0,6},{1,7},{2,4},{3,5},{4,2},{5,3},{6,0},{7,1},{8,14},{9,15},{10,... | collective-permute-start | bytes 393224 | tf_op jit(solution)/shard_map/ppermute | solution.py:25
  7.6 10.6 %all-to-all-start = ((s32[8,1,8]{2,1,0:T(1,128)}), s32[8,1,8]{2,1,0:T(1,128)S(1)}, u32[]{:S(2)}, u32[]{:S(2)}) async-start(s32[8,1,8]{2,1,0:T(1,128)} %broadcast_in_dim.9), calls=%async_computation | async-start | bytes 8192 | tf_op jit(solution)/shard_map/all_to_all | solution.py:29
  12.7 0.8 %copy-start.2 = (bf16[64,512]{1,0:T(8,128)(2,1)S(1)}, bf16[64,512]{1,0:T(8,128)(2,1)}, u32[]{:S(2)}) copy-start(bf16[64,512]{1,0:T(8,128)(2,1)} %refs_0_.2) | copy-start | bytes 196612
  13.5 3.9 %copy-start = (bf16[128,3072]{1,0:T(8,128)(2,1)S(1)}, bf16[128,3072]{1,0:T(8,128)(2,1)}, u32[]{:S(2)}) copy-start(bf16[128,3072]{1,0:T(8,128)(2,1)} %refs_0_.3) | copy-start | bytes 2359300
  13.5 4.7 %copy-start.1 = (bf16[64,1024]{1,0:T(8,128)(2,1)S(1)}, bf16[64,1024]{1,0:T(8,128)(2,1)}, u32[]{:S(2)}) copy-start(bf16[64,1024]{1,0:T(8,128)(2,1)} %refs_2_.1) | copy-start | bytes 393220
  13.5 6.4 %collective-permute-start.1 = (bf16[64,256]{1,0:T(8,128)(2,1)S(1)}, bf16[64,256]{1,0:T(8,128)(2,1)S(1)}, u32[]{:S(2)}, u32[]{:S(2)}) collective-permute-start(bf16[64,256]{1,0:T(8,128)(2,1)S(1)} %get-tuple-element.21), channel_id=1, source_target_pairs={{0,6},{1,7},{2,4},{3,5},{4,2},{5,3},{6,0},{7,1},{8,14},{9,15},{10,... | collective-permute-start | bytes 98312 | tf_op jit(solution)/shard_map/ppermute | solution.py:25
  17.4 3.9 %collective-permute-start = (bf16[64,256]{1,0:T(8,128)(2,1)S(1)}, bf16[64,256]{1,0:T(8,128)(2,1)S(1)}, u32[]{:S(2)}, u32[]{:S(2)}) collective-permute-start(bf16[64,256]{1,0:T(8,128)(2,1)S(1)} %get-tuple-element.21), channel_id=1, source_target_pairs={{0,2},{1,3},{2,0},{3,1},{4,6},{5,7},{6,4},{7,5},{8,10},{9,11},{10,... | collective-permute-start | bytes 98312 | tf_op jit(solution)/shard_map/ppermute | solution.py:25
  17.4 2.4 %collective-permute-start.2 = (bf16[128,3072]{1,0:T(8,128)(2,1)S(1)}, bf16[128,3072]{1,0:T(8,128)(2,1)S(1)}, u32[]{:S(2)}, u32[]{:S(2)}) collective-permute-start(bf16[128,3072]{1,0:T(8,128)(2,1)S(1)} %copy-done), channel_id=1, source_target_pairs={{0,1},{1,0},{2,3},{3,2},{4,5},{5,4},{6,7},{7,6},{8,9},{9,8},{10,11... | collective-permute-start | bytes 2359304 | tf_op jit(solution)/shard_map/ppermute | solution.py:25
  18.2 3.1 %collective-permute-start.6 = (bf16[256,1024]{1,0:T(8,128)(2,1)S(1)}, bf16[256,1024]{1,0:T(8,128)(2,1)S(1)}, u32[]{:S(2)}, u32[]{:S(2)}) collective-permute-start(bf16[256,1024]{1,0:T(8,128)(2,1)S(1)} %shard_map.69.refs_4_.refs_1_), channel_id=1, source_target_pairs={{0,1},{1,0},{2,3},{3,2},{4,5},{5,4},{6,7},{7,6},{8,9},{9,8},{10,11... | collective-permute-start | bytes 1572872 | tf_op jit(solution)/shard_map/ppermute | solution.py:25
  19.9 14.8 %copy-start.3 = (bf16[768,1024]{1,0:T(8,128)(2,1)}, bf16[768,1024]{1,0:T(8,128)(2,1)S(1)}, u32[]{:S(2)}) copy-start(bf16[768,1024]{1,0:T(8,128)(2,1)S(1)} %shard_map.68.refs_3_.refs_5_) | copy-start | bytes 4718596
  23.0 9.9 %collective-permute-start.7 = (bf16[320,256]{1,0:T(8,128)(2,1)S(1)}, bf16[320,256]{1,0:T(8,128)(2,1)S(1)}, u32[]{:S(2)}, u32[]{:S(2)}) collective-permute-start(bf16[320,256]{1,0:T(8,128)(2,1)S(1)} %get-tuple-element.24.refs_0_), channel_id=1, source_target_pairs={{0,4},{1,5},{2,6},{3,7},{4,0},{5,1},{6,2},{7,3},{8,12},{9,13},{10,... | collective-permute-start | bytes 491528 | tf_op jit(solution)/shard_map/ppermute | solution.py:25
  23.5 19.6 %collective-permute-start.11 = (bf16[256,1024]{1,0:T(8,128)(2,1)S(1)}, bf16[256,1024]{1,0:T(8,128)(2,1)S(1)}, u32[]{:S(2)}, u32[]{:S(2)}) collective-permute-start(bf16[256,1024]{1,0:T(8,128)(2,1)S(1)} %shard_map.69.refs_4_.refs_1_), channel_id=1, source_target_pairs={{0,24},{8,16},{16,8},{24,0},{1,25},{9,17},{17,9},{25,1},{2,26},{10... | collective-permute-start | bytes 1572872 | tf_op jit(solution)/shard_map/ppermute | solution.py:25
  25.9 24.6 %collective-permute-start.10 = (bf16[256,1024]{1,0:T(8,128)(2,1)S(1)}, bf16[256,1024]{1,0:T(8,128)(2,1)S(1)}, u32[]{:S(2)}, u32[]{:S(2)}) collective-permute-start(bf16[256,1024]{1,0:T(8,128)(2,1)S(1)} %shard_map.69.refs_4_.refs_1_), channel_id=1, source_target_pairs={{0,16},{8,24},{16,0},{24,8},{1,17},{9,25},{17,1},{25,9},{2,18},{10... | collective-permute-start | bytes 1572872 | tf_op jit(solution)/shard_map/ppermute | solution.py:25
  26.4 24.1 %collective-permute-start.9 = (bf16[256,1024]{1,0:T(8,128)(2,1)S(1)}, bf16[256,1024]{1,0:T(8,128)(2,1)S(1)}, u32[]{:S(2)}, u32[]{:S(2)}) collective-permute-start(bf16[256,1024]{1,0:T(8,128)(2,1)S(1)} %shard_map.69.refs_4_.refs_1_), channel_id=1, source_target_pairs={{0,8},{8,0},{16,24},{24,16},{1,9},{9,1},{17,25},{25,17},{2,10},{10... | collective-permute-start | bytes 1572872 | tf_op jit(solution)/shard_map/ppermute | solution.py:25
  33.0 1.7 %copy-start.5 = (bf16[64,256]{1,0:T(8,128)(2,1)}, bf16[64,256]{1,0:T(8,128)(2,1)S(1)}, u32[]{:S(2)}) copy-start(bf16[64,256]{1,0:T(8,128)(2,1)S(1)} %get-tuple-element.30.refs_1_) | copy-start | bytes 98308
  33.0 1.7 %collective-permute-start.8 = (bf16[256,256]{1,0:T(8,128)(2,1)S(1)}, bf16[256,256]{1,0:T(8,128)(2,1)S(1)}, u32[]{:S(2)}, u32[]{:S(2)}) collective-permute-start(bf16[256,256]{1,0:T(8,128)(2,1)S(1)} %get-tuple-element.25.refs_0_.refs_1_), channel_id=1, source_target_pairs={{0,1},{1,0},{2,3},{3,2},{4,5},{5,4},{6,7},{7,6},{8,9},{9,8},{10,11... | collective-permute-start | bytes 393224 | tf_op jit(solution)/shard_map/ppermute | solution.py:25
  36.4 16.5 %collective-permute-start.13 = (bf16[64,1024]{1,0:T(8,128)(2,1)}, bf16[64,1024]{1,0:T(8,128)(2,1)S(1)}, u32[]{:S(2)}, u32[]{:S(2)}) collective-permute-start(bf16[64,1024]{1,0:T(8,128)(2,1)} %get-tuple-element.32), channel_id=1, source_target_pairs={{0,4},{1,5},{2,6},{3,7},{4,0},{5,1},{6,2},{7,3},{8,12},{9,13},{10,... | collective-permute-start | bytes 393224 | tf_op jit(solution)/shard_map/ppermute | solution.py:25
  36.4 16.6 %collective-permute-start.14 = (bf16[64,1024]{1,0:T(8,128)(2,1)}, bf16[64,1024]{1,0:T(8,128)(2,1)}, u32[]{:S(2)}, u32[]{:S(2)}) collective-permute-start(bf16[64,1024]{1,0:T(8,128)(2,1)} %get-tuple-element.33), channel_id=1, source_target_pairs={{0,6},{1,7},{2,4},{3,5},{4,2},{5,3},{6,0},{7,1},{8,14},{9,15},{10,... | collective-permute-start | bytes 393224 | tf_op jit(solution)/shard_map/ppermute | solution.py:25
  39.4 15.8 %all-to-all-start.1 = ((bf16[4,528,128]{2,1,0:T(8,128)(2,1)}), bf16[4,528,128]{2,1,0:T(8,128)(2,1)S(1)}, u32[]{:S(2)}, u32[]{:S(2)}) async-start(bf16[4,528,128]{2,1,0:T(8,128)(2,1)} %shard_map.73.refs_0_), calls=%async_computation.1 | async-start | bytes 1081344 | tf_op jit(solution)/shard_map/all_to_all | solution.py:29
  43.1 9.9 %collective-permute-start.12 = (bf16[80,1024]{1,0:T(8,128)(2,1)S(1)}, bf16[80,1024]{1,0:T(8,128)(2,1)S(1)}, u32[]{:S(2)}, u32[]{:S(2)}) collective-permute-start(bf16[80,1024]{1,0:T(8,128)(2,1)S(1)} %get-tuple-element.31), channel_id=1, source_target_pairs={{0,2},{1,3},{2,0},{3,1},{4,6},{5,7},{6,4},{7,5},{8,10},{9,11},{10,... | collective-permute-start | bytes 491528 | tf_op jit(solution)/shard_map/ppermute | solution.py:25
  50.5 1.4 %copy-start.4 = (bf16[768,1024]{1,0:T(8,128)(2,1)S(1)}, bf16[768,1024]{1,0:T(8,128)(2,1)}, u32[]{:S(2)}) copy-start(bf16[768,1024]{1,0:T(8,128)(2,1)} %copy-done.3) | copy-start | bytes 4718596
  52.3 0.8 %copy-start.6 = (bf16[64,256]{1,0:T(8,128)(2,1)S(1)}, bf16[64,256]{1,0:T(8,128)(2,1)}, u32[]{:S(2)}) copy-start(bf16[64,256]{1,0:T(8,128)(2,1)} %copy-done.5) | copy-start | bytes 98308
  52.3 2.8 %collective-permute-start.15 = (bf16[256,1024]{1,0:T(8,128)(2,1)S(1)}, bf16[256,1024]{1,0:T(8,128)(2,1)}, u32[]{:S(2)}, u32[]{:S(2)}) collective-permute-start(bf16[256,1024]{1,0:T(8,128)(2,1)S(1)} %get-tuple-element.36.refs_3_), channel_id=1, source_target_pairs={{0,1},{1,0},{2,3},{3,2},{4,5},{5,4},{6,7},{7,6},{8,9},{9,8},{10,11... | collective-permute-start | bytes 1572872 | tf_op jit(solution)/shard_map/ppermute | solution.py:25
  52.4 2.8 %collective-permute-start.16 = (bf16[256,1024]{1,0:T(8,128)(2,1)S(1)}, bf16[256,1024]{1,0:T(8,128)(2,1)}, u32[]{:S(2)}, u32[]{:S(2)}) collective-permute-start(bf16[256,1024]{1,0:T(8,128)(2,1)S(1)} %get-tuple-element.37.refs_5_), channel_id=1, source_target_pairs={{0,1},{1,0},{2,3},{3,2},{4,5},{5,4},{6,7},{7,6},{8,9},{9,8},{10,11... | collective-permute-start | bytes 1572872 | tf_op jit(solution)/shard_map/ppermute | solution.py:25
  52.9 3.0 %collective-permute-start.17 = (bf16[256,1024]{1,0:T(8,128)(2,1)S(1)}, bf16[256,1024]{1,0:T(8,128)(2,1)}, u32[]{:S(2)}, u32[]{:S(2)}) collective-permute-start(bf16[256,1024]{1,0:T(8,128)(2,1)S(1)} %get-tuple-element.38.refs_7_), channel_id=1, source_target_pairs={{0,1},{1,0},{2,3},{3,2},{4,5},{5,4},{6,7},{7,6},{8,9},{9,8},{10,11... | collective-permute-start | bytes 1572872 | tf_op jit(solution)/shard_map/ppermute | solution.py:25

commit v5 on v4

--- a/solution.py
+++ b/solution.py
@@ -12,6 +12,7 @@
 H = 512
 DILATION_SIZE = 4
 SEG = 8
+LOADED = (0, 3, 5, 7)
 BF16 = jnp.bfloat16
 F32 = jnp.float32
 VMEM = pl.BlockSpec(memory_space=pltpu.VMEM)
@@ -226,10 +227,14 @@
     load = pltpu.make_async_copy(wide_ref, follow_ref, sem)
     load.start()
     loads = []
+    count = blocks[0].shape[0]
+    for i in LOADED:
+        rows = pl.ds(i * count, count)
+        loads.append(pltpu.make_async_copy(blocks[i], rows_ref.at[rows, :], sems.at[i]))
+        loads[-1].start()
     for i, block in enumerate(blocks):
-        rows = pl.ds(i * block.shape[0], block.shape[0])
-        loads.append(pltpu.make_async_copy(block, rows_ref.at[rows, :], sems.at[i]))
-        loads[-1].start()
+        if i not in LOADED:
+            rows_ref[i * count : (i + 1) * count, :] = block[...]
     for i in range(groups):
         early_ref[i, :total, :] = pre_ref[lax.axis_index("dp") ^ i, :total, :].astype(F32)
         early_ref[i, total:, :] = jnp.zeros((SEG, width), F32)
@@ -341,22 +346,24 @@
     )[0]
     all_pre = exchange(sent_pre, "dp")
     kept = call(
-        local, [shaped((rows, C), F32)], [here, weight], [VMEM] * 2, after=[sent_pre, *far_own]
+        local, [shaped((rows, C), F32)], [here, weight], [VMEM] * 2, after=[sent_pre]
     )[0]
+    arrived = call(mark, [shaped((8, 128), F32)], [], [], after=[kept, *far_own])[0]
     grad_in, gated_out = call(
         finish,
         [shaped((rows, C), BF16), shaped((rows, H), BF16)],
         [kept, gated[0], *parts],
         [VMEM] * (chips + 1),
-    )
-    far_own = held(far_own, [kept])
+        after=[arrived],
+    )
+    far_own = held(far_own, [arrived])
     far_other = [swap(block, "fsdp", 1) for block in far_own]
     blocks = [own_stack, other_stack] + [block for pair in zip(far_own, far_other) for block in pair]
     grad_weight = call(
         functools.partial(weight_grad, 1.0 / math.sqrt(all_rows * groups)),
         [shaped((width, 3 * C), F32)],
         [all_pre, *blocks],
-        [VMEM] + [ANY] * len(blocks),
+        [VMEM] + [ANY if i in LOADED else VMEM for i in range(len(blocks))],
         [
             pltpu.VMEM((groups, all_rows + SEG, width), F32),
             pltpu.VMEM((groups * all_rows, 3 * width), F32),

time: 61 us -> 60.2 us (0.987)
  waiting for transfers between devices: 16.8 us -> 16 us
    ppermute x18, waiting for transfers between devices: 15.6 us -> 13.8 us  [swap(): return lax.ppermute(value, axis, [(i, i ^ distance) for i in range(count)])]
    all_to_all x2, waiting for transfers between devices: 1.13 us -> 2.19 us  [exchange(): return lax.all_to_all(copies, axis, split_axis=0, concat_axis=0, tiled=True)]
    pallas_call x11 -> x12, Pallas kernels: 12.7 us -> 12.7 us  [call(): pl.pallas_call(run, out_shape=out_shapes, in_specs=[ANY] * len(after) + l...]
where the time goes in v5:
time: 60.2 us; the launch traced here: 59.8 us
  starting transfers between devices  26.8 us (45%)
  waiting for transfers between devices  16 us (27%)
  Pallas kernels  12.7 us (21%)
  local copies, waits for them, and re-layouts  3.52 us (6%)
  between operations  0.8 us (1%)
    ppermute x18, starting transfers between devices, swap(): return lax.ppermute(value, axis, [(i, i ^ distance) for i in range(count)])  18 us
    ppermute x18, waiting for transfers between devices, swap(): return lax.ppermute(value, axis, [(i, i ^ distance) for i in range(count)])  13.8 us
    pallas_call x12, Pallas kernels, call(): pl.pallas_call(run, out_shape=out_shapes, in_specs=[ANY] * len(after) + l...  12.7 us
    all_to_all x2, starting transfers between devices, exchange(): return lax.all_to_all(copies, axis, split_axis=0, concat_axis=0, tiled=True)  8.81 us
    unnamed x14, local copies, waits for them, and re-layouts  2.27 us
    all_to_all x2, waiting for transfers between devices, exchange(): return lax.all_to_all(copies, axis, split_axis=0, concat_axis=0, tiled=True)  2.19 us
    broadcast_in_dim x1, local copies, waits for them, and re-layouts, by_channels(): jnp.broadcast_to(source_seg[None], (peers, 1, seg_count))  1.25 us
  transfers between devices with their start and end apart: 20, of which 7 were waited for; matrix products, arithmetic and copies ran while one was open for 2% of the time, Pallas kernels for 11%

profile of v5, /device:TPU:0, one launch (start us, length us, event | category | flops | bytes accessed | tf_op | source)
XLA Modules:
  0.0 59.8 jit_solution(12483194610421062461)
XLA Ops:
  0.6 4.1 %collective-permute-start.4 = (bf16[64,1024]{1,0:T(8,128)(2,1)}, bf16[64,1024]{1,0:T(8,128)(2,1)S(1)}, u32[]{:S(2)}, u32[]{:S(2)}) collective-permute-start(bf16[64,1024]{1,0:T(8,128)(2,1)} %refs_2_.1), channel_id=1, source_target_pairs={{0,4},{1,5},{2,6},{3,7},{4,0},{5,1},{6,2},{7,3},{8,12},{9,13},{10,... | collective-permute-start | bytes 393224 | tf_op jit(solution)/shard_map/ppermute | solution.py:26
  4.7 1.6 %collective-permute-start.3 = (bf16[64,1024]{1,0:T(8,128)(2,1)}, bf16[64,1024]{1,0:T(8,128)(2,1)S(1)}, u32[]{:S(2)}, u32[]{:S(2)}) collective-permute-start(bf16[64,1024]{1,0:T(8,128)(2,1)} %refs_2_.1), channel_id=1, source_target_pairs={{0,2},{1,3},{2,0},{3,1},{4,6},{5,7},{6,4},{7,5},{8,10},{9,11},{10,... | collective-permute-start | bytes 393224 | tf_op jit(solution)/shard_map/ppermute | solution.py:26
  6.3 0.0 collective-permute-start.5
  6.3 1.2 %broadcast_in_dim.9 = s32[8,1,8]{2,1,0:T(1,128)} broadcast(s32[8]{0:T(128)} %bitcast.5), dimensions={2} | broadcast | bytes 288 | tf_op jit(solution)/shard_map/broadcast_in_dim | solution.py:299
  7.6 5.1 %all-to-all-start = ((s32[8,1,8]{2,1,0:T(1,128)}), s32[8,1,8]{2,1,0:T(1,128)S(1)}, u32[]{:S(2)}, u32[]{:S(2)}) async-start(s32[8,1,8]{2,1,0:T(1,128)} %broadcast_in_dim.9), calls=%async_computation | async-start | bytes 8192 | tf_op jit(solution)/shard_map/all_to_all | solution.py:30
  12.7 0.0 copy-start.2
  12.7 0.8 %copy-done.2 = bf16[64,512]{1,0:T(8,128)(2,1)S(1)} copy-done((bf16[64,512]{1,0:T(8,128)(2,1)S(1)}, bf16[64,512]{1,0:T(8,128)(2,1)}, u32[]{:S(2)}) %copy-start.2) | copy-done | bytes 65560
  13.5 0.0 copy-start
  13.5 0.0 copy-start.1
  13.5 3.9 %collective-permute-start.1 = (bf16[64,256]{1,0:T(8,128)(2,1)S(1)}, bf16[64,256]{1,0:T(8,128)(2,1)S(1)}, u32[]{:S(2)}, u32[]{:S(2)}) collective-permute-start(bf16[64,256]{1,0:T(8,128)(2,1)S(1)} %get-tuple-element.21), channel_id=1, source_target_pairs={{0,6},{1,7},{2,4},{3,5},{4,2},{5,3},{6,0},{7,1},{8,14},{9,15},{10,... | collective-permute-start | bytes 98312 | tf_op jit(solution)/shard_map/ppermute | solution.py:26
  17.4 0.0 collective-permute-start
  17.4 0.0 collective-permute-done.4.refs_4_
  17.4 0.0 copy-done
  17.4 0.1 collective-permute-start.2
  17.5 0.6 %all-to-all-done = s32[8,1,8]{2,1,0:T(1,128)S(1)} async-done(((s32[8,1,8]{2,1,0:T(1,128)}), s32[8,1,8]{2,1,0:T(1,128)S(1)}, u32[]{:S(2)}, u32[]{:S(2)}) %all-to-all-start) | async-done | bytes 288 | tf_op jit(solution)/shard_map/all_to_all | solution.py:30
  18.1 0.0 collective-permute-done.3.refs_3_
  18.1 0.0 collective-permute-done.5.refs_5_
  18.1 0.0 copy-done.1
  18.2 0.1 collective-permute-start.6
  18.3 1.5 %collective-permute-done.2.refs_1_ = bf16[128,3072]{1,0:T(8,128)(2,1)S(1)} collective-permute-done((bf16[128,3072]{1,0:T(8,128)(2,1)S(1)}, bf16[128,3072]{1,0:T(8,128)(2,1)S(1)}, u32[]{:S(2)}, u32[]{:S(2)}) %collective-permute-start.2) | collective-permute-done | bytes 786464 | tf_op jit(solution)/shard_map/ppermute | solution.py:26
  19.8 0.1 shard_map.68.refs_3_.refs_2_
  19.9 0.0 copy-start.3
  19.9 0.0 collective-permute-done.1.refs_1_.refs_4_
  19.9 1.4 %collective-permute-done.refs_0_.refs_3_ = bf16[64,256]{1,0:T(8,128)(2,1)S(1)} collective-permute-done((bf16[64,256]{1,0:T(8,128)(2,1)S(1)}, bf16[64,256]{1,0:T(8,128)(2,1)S(1)}, u32[]{:S(2)}, u32[]{:S(2)}) %collective-permute-start) | collective-permute-done | bytes 32800 | tf_op jit(solution)/shard_map/ppermute | solution.py:26
  21.3 0.0 collective-permute-done.6.refs_5_.refs_2_
  21.3 1.6 %shard_map.70 = (f32[256,256]{1,0:T(8,128)S(1)}, bf16[320,256]{1,0:T(8,128)(2,1)S(1)}) custom-call(bf16[64,256]{1,0:T(8,128)(2,1)S(1)} %collective-permute-done.refs_0_.refs_3_, bf16[64,256]{1,0:T(8,128)(2,1)S(1)} %collective-permute-done.1.refs_1_.refs_4_, s32[8,8]{1,0:T(8,128)S(1)} %bitcast.3, bf16[768,1024]{1,0:T(8,128)(2,1)S(1)} %shard_map.68.refs_3_.refs_2_, ...), custom_call_target="tpu_custom_call" | custom-call | flops 10000000000 | tf_op jit(solution)/shard_map/pallas_call | solution.py:37
  23.0 0.5 collective-permute-start.7
  23.5 2.5 %collective-permute-start.11 = (bf16[256,1024]{1,0:T(8,128)(2,1)S(1)}, bf16[256,1024]{1,0:T(8,128)(2,1)S(1)}, u32[]{:S(2)}, u32[]{:S(2)}) collective-permute-start(bf16[256,1024]{1,0:T(8,128)(2,1)S(1)} %shard_map.69.refs_4_.refs_1_), channel_id=1, source_target_pairs={{0,24},{8,16},{16,8},{24,0},{1,25},{9,17},{17,9},{25,1},{2,26},{10... | collective-permute-start | bytes 1572872 | tf_op jit(solution)/shard_map/ppermute | solution.py:26
  25.9 0.5 collective-permute-start.10
  26.4 0.5 collective-permute-start.9
  26.9 5.9 %collective-permute-done.7.refs_1_ = bf16[320,256]{1,0:T(8,128)(2,1)S(1)} collective-permute-done((bf16[320,256]{1,0:T(8,128)(2,1)S(1)}, bf16[320,256]{1,0:T(8,128)(2,1)S(1)}, u32[]{:S(2)}, u32[]{:S(2)}) %collective-permute-start.7) | collective-permute-done | bytes 163872 | tf_op jit(solution)/shard_map/ppermute | solution.py:26
  32.9 0.1 shard_map.71
  33.0 0.0 copy-start.5
  33.0 0.1 collective-permute-start.8
  33.1 1.6 %shard_map.72 = (s32[65]{0:T(128)S(1)}, bf16[16,128]{1,0:T(8,128)(2,1)S(1)}) custom-call(bf16[320,256]{1,0:T(8,128)(2,1)S(1)} %get-tuple-element.24.refs_0_, s32[8,8]{1,0:T(8,128)S(1)} %bitcast.4), custom_call_target="tpu_custom_call" | custom-call | flops 10000000000 | tf_op jit(solution)/shard_map/pallas_call | solution.py:37
  34.6 0.0 copy-done.5
  34.7 0.0 collective-permute-done.8.refs_1_.refs_2_
  34.7 0.0 copy-done.3
  34.7 1.7 %shard_map.74 = (bf16[80,1024]{1,0:T(8,128)(2,1)S(1)}, bf16[64,1024]{1,0:T(8,128)(2,1)}, bf16[64,1024]{1,0:T(8,128)(2,1)}, bf16[64,768]{1,0:T(8,128)(2,1)S(1)}) custom-call(s32[65]{0:T(128)S(1)} %get-tuple-element.27.refs_0_, bf16[256,256]{1,0:T(8,128)(2,1)S(1)} %get-tuple-element.25.refs_0_.refs_1_, ...), custom_call_target="tpu_custom_call" | custom-call | flops 10000000000 | tf_op jit(solution)/shard_map/pallas_call | solution.py:37
  36.4 0.0 collective-permute-start.13
  36.4 2.1 %collective-permute-start.14 = (bf16[64,1024]{1,0:T(8,128)(2,1)}, bf16[64,1024]{1,0:T(8,128)(2,1)}, u32[]{:S(2)}, u32[]{:S(2)}) collective-permute-start(bf16[64,1024]{1,0:T(8,128)(2,1)} %get-tuple-element.33), channel_id=1, source_target_pairs={{0,6},{1,7},{2,4},{3,5},{4,2},{5,3},{6,0},{7,1},{8,14},{9,15},{10,... | collective-permute-start | bytes 393224 | tf_op jit(solution)/shard_map/ppermute | solution.py:26
  38.5 0.9 %shard_map.73.refs_0_ = bf16[4,528,128]{2,1,0:T(8,128)(2,1)} custom-call(bf16[256,256]{1,0:T(8,128)(2,1)S(1)} %get-tuple-element.25.refs_0_.refs_1_, bf16[256,256]{1,0:T(8,128)(2,1)S(1)} %collective-permute-done.8.refs_1_.refs_2_, bf16[16,128]{1,0:T(8,128)(2,1)S(1)} %get-tuple-element.26.refs_2_), custom_call_target="tpu_custom_call" | custom-call | flops 10000000000 | tf_op jit(solution)/shard_map/pallas_call | solution.py:37
  39.4 3.7 %all-to-all-start.1 = ((bf16[4,528,128]{2,1,0:T(8,128)(2,1)}), bf16[4,528,128]{2,1,0:T(8,128)(2,1)S(1)}, u32[]{:S(2)}, u32[]{:S(2)}) async-start(bf16[4,528,128]{2,1,0:T(8,128)(2,1)} %shard_map.73.refs_0_), calls=%async_computation.1 | async-start | bytes 1081344 | tf_op jit(solution)/shard_map/all_to_all | solution.py:30
  43.1 0.0 copy-start.4
  43.1 1.4 %copy-done.4 = bf16[768,1024]{1,0:T(8,128)(2,1)S(1)} copy-done((bf16[768,1024]{1,0:T(8,128)(2,1)S(1)}, bf16[768,1024]{1,0:T(8,128)(2,1)}, u32[]{:S(2)}) %copy-start.4) | copy-done | bytes 1572888
  44.5 0.4 shard_map.75.refs_0_.refs_1_
  44.9 0.0 collective-permute-done.11.refs_3_.refs_2_
  44.9 1.5 %collective-permute-start.12 = (bf16[80,1024]{1,0:T(8,128)(2,1)S(1)}, bf16[80,1024]{1,0:T(8,128)(2,1)S(1)}, u32[]{:S(2)}, u32[]{:S(2)}) collective-permute-start(bf16[80,1024]{1,0:T(8,128)(2,1)S(1)} %get-tuple-element.31), channel_id=1, source_target_pairs={{0,2},{1,3},{2,0},{3,1},{4,6},{5,7},{6,4},{7,5},{8,10},{9,11},{10,... | collective-permute-start | bytes 491528 | tf_op jit(solution)/shard_map/ppermute | solution.py:26
  46.4 4.1 %collective-permute-done.10.refs_2_.refs_1_ = bf16[256,1024]{1,0:T(8,128)(2,1)S(1)} collective-permute-done((bf16[256,1024]{1,0:T(8,128)(2,1)S(1)}, bf16[256,1024]{1,0:T(8,128)(2,1)S(1)}, u32[]{:S(2)}, u32[]{:S(2)}) %collective-permute-start.10) | collective-permute-done | bytes 524320 | tf_op jit(solution)/shard_map/ppermute | solution.py:26
  50.5 0.0 collective-permute-done.9.refs_1_.refs_0_
  50.5 0.0 copy-start.6
  50.5 0.1 collective-permute-start.15
  50.6 0.5 collective-permute-start.16
  51.1 0.0 collective-permute-done.13.refs_4_
  51.1 0.1 collective-permute-start.17
  51.2 0.0 collective-permute-done.14.refs_5_
  51.2 0.8 %collective-permute-done.12.refs_3_ = bf16[80,1024]{1,0:T(8,128)(2,1)S(1)} collective-permute-done((bf16[80,1024]{1,0:T(8,128)(2,1)S(1)}, bf16[80,1024]{1,0:T(8,128)(2,1)S(1)}, u32[]{:S(2)}, u32[]{:S(2)}) %collective-permute-start.12) | collective-permute-done | bytes 163872 | tf_op jit(solution)/shard_map/ppermute | solution.py:26
  52.0 0.0 copy-done.6
  52.0 1.6 %shard_map.77 = (bf16[64,1024]{1,0:T(8,128)(2,1)}, bf16[64,512]{1,0:T(8,128)(2,1)}) custom-call(f32[8,128]{1,0:T(8,128)S(1)} %shard_map.76.refs_0_.refs_3_, f32[64,1024]{1,0:T(8,128)S(1)} %shard_map.75.refs_0_.refs_1_, bf16[64,256]{1,0:T(8,128)(2,1)S(1)} %copy-done.6, bf16[80,1024]{1,0:T(8,128)(2,1)S(1)} %collective-permute-done.12.refs_3_, ...), custom_call_target="tpu_custom_call" | custom-call | flops 10000000000 | tf_op jit(solution)/shard_map/pallas_call | solution.py:37
  53.6 1.5 %all-to-all-done.1.refs_0_ = bf16[4,528,128]{2,1,0:T(8,128)(2,1)S(1)} async-done(((bf16[4,528,128]{2,1,0:T(8,128)(2,1)}), bf16[4,528,128]{2,1,0:T(8,128)(2,1)S(1)}, u32[]{:S(2)}, u32[]{:S(2)}) %all-to-all-start.1) | async-done | bytes 540704 | tf_op jit(solution)/shard_map/all_to_all | solution.py:30
  55.2 0.0 collective-permute-done.15.refs_4_
  55.2 0.0 collective-permute-done.16.refs_6_
  55.2 0.0 collective-permute-done.17.refs_8_
  55.2 4.7 %shard_map.79 = f32[128,3072]{1,0:T(8,128)} custom-call(bf16[4,528,128]{2,1,0:T(8,128)(2,1)S(1)} %all-to-all-done.1.refs_0_, bf16[256,1024]{1,0:T(8,128)(2,1)S(1)} %shard_map.69.refs_4_.refs_1_, bf16[256,1024]{1,0:T(8,128)(2,1)S(1)} %collective-permute-done.6.refs_5_.refs_2_, bf16[256,1024]{1,0:T(8,128)(2,1)S(1)} %get-tuple-element.36.refs_3_, ...), custom_call_target="tpu_custom_call" | custom-call | flops 10000000000 | tf_op jit(solution)/shard_map/pallas_call | solution.py:37
  (4 shorter events, 0.1 us)
Async XLA Ops:
  0.6 16.8 %collective-permute-start.4 = (bf16[64,1024]{1,0:T(8,128)(2,1)}, bf16[64,1024]{1,0:T(8,128)(2,1)S(1)}, u32[]{:S(2)}, u32[]{:S(2)}) collective-permute-start(bf16[64,1024]{1,0:T(8,128)(2,1)} %refs_2_.1), channel_id=1, source_target_pairs={{0,4},{1,5},{2,6},{3,7},{4,0},{5,1},{6,2},{7,3},{8,12},{9,13},{10,... | collective-permute-start | bytes 393224 | tf_op jit(solution)/shard_map/ppermute | solution.py:26
  4.7 13.4 %collective-permute-start.3 = (bf16[64,1024]{1,0:T(8,128)(2,1)}, bf16[64,1024]{1,0:T(8,128)(2,1)S(1)}, u32[]{:S(2)}, u32[]{:S(2)}) collective-permute-start(bf16[64,1024]{1,0:T(8,128)(2,1)} %refs_2_.1), channel_id=1, source_target_pairs={{0,2},{1,3},{2,0},{3,1},{4,6},{5,7},{6,4},{7,5},{8,10},{9,11},{10,... | collective-permute-start | bytes 393224 | tf_op jit(solution)/shard_map/ppermute | solution.py:26
  6.3 11.8 %collective-permute-start.5 = (bf16[64,1024]{1,0:T(8,128)(2,1)}, bf16[64,1024]{1,0:T(8,128)(2,1)S(1)}, u32[]{:S(2)}, u32[]{:S(2)}) collective-permute-start(bf16[64,1024]{1,0:T(8,128)(2,1)} %refs_2_.1), channel_id=1, source_target_pairs={{0,6},{1,7},{2,4},{3,5},{4,2},{5,3},{6,0},{7,1},{8,14},{9,15},{10,... | collective-permute-start | bytes 393224 | tf_op jit(solution)/shard_map/ppermute | solution.py:26
  7.6 10.6 %all-to-all-start = ((s32[8,1,8]{2,1,0:T(1,128)}), s32[8,1,8]{2,1,0:T(1,128)S(1)}, u32[]{:S(2)}, u32[]{:S(2)}) async-start(s32[8,1,8]{2,1,0:T(1,128)} %broadcast_in_dim.9), calls=%async_computation | async-start | bytes 8192 | tf_op jit(solution)/shard_map/all_to_all | solution.py:30
  12.7 0.8 %copy-start.2 = (bf16[64,512]{1,0:T(8,128)(2,1)S(1)}, bf16[64,512]{1,0:T(8,128)(2,1)}, u32[]{:S(2)}) copy-start(bf16[64,512]{1,0:T(8,128)(2,1)} %refs_0_.2) | copy-start | bytes 196612
  13.5 3.9 %copy-start = (bf16[128,3072]{1,0:T(8,128)(2,1)S(1)}, bf16[128,3072]{1,0:T(8,128)(2,1)}, u32[]{:S(2)}) copy-start(bf16[128,3072]{1,0:T(8,128)(2,1)} %refs_0_.3) | copy-start | bytes 2359300
  13.5 4.7 %copy-start.1 = (bf16[64,1024]{1,0:T(8,128)(2,1)S(1)}, bf16[64,1024]{1,0:T(8,128)(2,1)}, u32[]{:S(2)}) copy-start(bf16[64,1024]{1,0:T(8,128)(2,1)} %refs_2_.1) | copy-start | bytes 393220
  13.5 6.4 %collective-permute-start.1 = (bf16[64,256]{1,0:T(8,128)(2,1)S(1)}, bf16[64,256]{1,0:T(8,128)(2,1)S(1)}, u32[]{:S(2)}, u32[]{:S(2)}) collective-permute-start(bf16[64,256]{1,0:T(8,128)(2,1)S(1)} %get-tuple-element.21), channel_id=1, source_target_pairs={{0,6},{1,7},{2,4},{3,5},{4,2},{5,3},{6,0},{7,1},{8,14},{9,15},{10,... | collective-permute-start | bytes 98312 | tf_op jit(solution)/shard_map/ppermute | solution.py:26
  17.4 3.9 %collective-permute-start = (bf16[64,256]{1,0:T(8,128)(2,1)S(1)}, bf16[64,256]{1,0:T(8,128)(2,1)S(1)}, u32[]{:S(2)}, u32[]{:S(2)}) collective-permute-start(bf16[64,256]{1,0:T(8,128)(2,1)S(1)} %get-tuple-element.21), channel_id=1, source_target_pairs={{0,2},{1,3},{2,0},{3,1},{4,6},{5,7},{6,4},{7,5},{8,10},{9,11},{10,... | collective-permute-start | bytes 98312 | tf_op jit(solution)/shard_map/ppermute | solution.py:26
  17.4 2.4 %collective-permute-start.2 = (bf16[128,3072]{1,0:T(8,128)(2,1)S(1)}, bf16[128,3072]{1,0:T(8,128)(2,1)S(1)}, u32[]{:S(2)}, u32[]{:S(2)}) collective-permute-start(bf16[128,3072]{1,0:T(8,128)(2,1)S(1)} %copy-done), channel_id=1, source_target_pairs={{0,1},{1,0},{2,3},{3,2},{4,5},{5,4},{6,7},{7,6},{8,9},{9,8},{10,11... | collective-permute-start | bytes 2359304 | tf_op jit(solution)/shard_map/ppermute | solution.py:26
  18.2 3.1 %collective-permute-start.6 = (bf16[256,1024]{1,0:T(8,128)(2,1)S(1)}, bf16[256,1024]{1,0:T(8,128)(2,1)S(1)}, u32[]{:S(2)}, u32[]{:S(2)}) collective-permute-start(bf16[256,1024]{1,0:T(8,128)(2,1)S(1)} %shard_map.69.refs_4_.refs_1_), channel_id=1, source_target_pairs={{0,1},{1,0},{2,3},{3,2},{4,5},{5,4},{6,7},{7,6},{8,9},{9,8},{10,11... | collective-permute-start | bytes 1572872 | tf_op jit(solution)/shard_map/ppermute | solution.py:26
  19.9 14.8 %copy-start.3 = (bf16[768,1024]{1,0:T(8,128)(2,1)}, bf16[768,1024]{1,0:T(8,128)(2,1)S(1)}, u32[]{:S(2)}) copy-start(bf16[768,1024]{1,0:T(8,128)(2,1)S(1)} %shard_map.68.refs_3_.refs_2_) | copy-start | bytes 4718596
  23.0 9.9 %collective-permute-start.7 = (bf16[320,256]{1,0:T(8,128)(2,1)S(1)}, bf16[320,256]{1,0:T(8,128)(2,1)S(1)}, u32[]{:S(2)}, u32[]{:S(2)}) collective-permute-start(bf16[320,256]{1,0:T(8,128)(2,1)S(1)} %get-tuple-element.24.refs_0_), channel_id=1, source_target_pairs={{0,4},{1,5},{2,6},{3,7},{4,0},{5,1},{6,2},{7,3},{8,12},{9,13},{10,... | collective-permute-start | bytes 491528 | tf_op jit(solution)/shard_map/ppermute | solution.py:26
  23.5 21.4 %collective-permute-start.11 = (bf16[256,1024]{1,0:T(8,128)(2,1)S(1)}, bf16[256,1024]{1,0:T(8,128)(2,1)S(1)}, u32[]{:S(2)}, u32[]{:S(2)}) collective-permute-start(bf16[256,1024]{1,0:T(8,128)(2,1)S(1)} %shard_map.69.refs_4_.refs_1_), channel_id=1, source_target_pairs={{0,24},{8,16},{16,8},{24,0},{1,25},{9,17},{17,9},{25,1},{2,26},{10... | collective-permute-start | bytes 1572872 | tf_op jit(solution)/shard_map/ppermute | solution.py:26
  25.9 24.6 %collective-permute-start.10 = (bf16[256,1024]{1,0:T(8,128)(2,1)S(1)}, bf16[256,1024]{1,0:T(8,128)(2,1)S(1)}, u32[]{:S(2)}, u32[]{:S(2)}) collective-permute-start(bf16[256,1024]{1,0:T(8,128)(2,1)S(1)} %shard_map.69.refs_4_.refs_1_), channel_id=1, source_target_pairs={{0,16},{8,24},{16,0},{24,8},{1,17},{9,25},{17,1},{25,9},{2,18},{10... | collective-permute-start | bytes 1572872 | tf_op jit(solution)/shard_map/ppermute | solution.py:26
  26.4 24.1 %collective-permute-start.9 = (bf16[256,1024]{1,0:T(8,128)(2,1)S(1)}, bf16[256,1024]{1,0:T(8,128)(2,1)S(1)}, u32[]{:S(2)}, u32[]{:S(2)}) collective-permute-start(bf16[256,1024]{1,0:T(8,128)(2,1)S(1)} %shard_map.69.refs_4_.refs_1_), channel_id=1, source_target_pairs={{0,8},{8,0},{16,24},{24,16},{1,9},{9,1},{17,25},{25,17},{2,10},{10... | collective-permute-start | bytes 1572872 | tf_op jit(solution)/shard_map/ppermute | solution.py:26
  33.0 1.7 %copy-start.5 = (bf16[64,256]{1,0:T(8,128)(2,1)}, bf16[64,256]{1,0:T(8,128)(2,1)S(1)}, u32[]{:S(2)}) copy-start(bf16[64,256]{1,0:T(8,128)(2,1)S(1)} %get-tuple-element.30.refs_2_) | copy-start | bytes 98308
  33.0 1.7 %collective-permute-start.8 = (bf16[256,256]{1,0:T(8,128)(2,1)S(1)}, bf16[256,256]{1,0:T(8,128)(2,1)S(1)}, u32[]{:S(2)}, u32[]{:S(2)}) collective-permute-start(bf16[256,256]{1,0:T(8,128)(2,1)S(1)} %get-tuple-element.25.refs_0_.refs_1_), channel_id=1, source_target_pairs={{0,1},{1,0},{2,3},{3,2},{4,5},{5,4},{6,7},{7,6},{8,9},{9,8},{10,11... | collective-permute-start | bytes 393224 | tf_op jit(solution)/shard_map/ppermute | solution.py:26
  36.4 14.7 %collective-permute-start.13 = (bf16[64,1024]{1,0:T(8,128)(2,1)}, bf16[64,1024]{1,0:T(8,128)(2,1)S(1)}, u32[]{:S(2)}, u32[]{:S(2)}) collective-permute-start(bf16[64,1024]{1,0:T(8,128)(2,1)} %get-tuple-element.32), channel_id=1, source_target_pairs={{0,4},{1,5},{2,6},{3,7},{4,0},{5,1},{6,2},{7,3},{8,12},{9,13},{10,... | collective-permute-start | bytes 393224 | tf_op jit(solution)/shard_map/ppermute | solution.py:26
  36.4 14.7 %collective-permute-start.14 = (bf16[64,1024]{1,0:T(8,128)(2,1)}, bf16[64,1024]{1,0:T(8,128)(2,1)}, u32[]{:S(2)}, u32[]{:S(2)}) collective-permute-start(bf16[64,1024]{1,0:T(8,128)(2,1)} %get-tuple-element.33), channel_id=1, source_target_pairs={{0,6},{1,7},{2,4},{3,5},{4,2},{5,3},{6,0},{7,1},{8,14},{9,15},{10,... | collective-permute-start | bytes 393224 | tf_op jit(solution)/shard_map/ppermute | solution.py:26
  39.4 15.8 %all-to-all-start.1 = ((bf16[4,528,128]{2,1,0:T(8,128)(2,1)}), bf16[4,528,128]{2,1,0:T(8,128)(2,1)S(1)}, u32[]{:S(2)}, u32[]{:S(2)}) async-start(bf16[4,528,128]{2,1,0:T(8,128)(2,1)} %shard_map.73.refs_0_), calls=%async_computation.1 | async-start | bytes 1081344 | tf_op jit(solution)/shard_map/all_to_all | solution.py:30
  43.1 1.4 %copy-start.4 = (bf16[768,1024]{1,0:T(8,128)(2,1)S(1)}, bf16[768,1024]{1,0:T(8,128)(2,1)}, u32[]{:S(2)}) copy-start(bf16[768,1024]{1,0:T(8,128)(2,1)} %copy-done.3) | copy-start | bytes 4718596
  44.9 7.1 %collective-permute-start.12 = (bf16[80,1024]{1,0:T(8,128)(2,1)S(1)}, bf16[80,1024]{1,0:T(8,128)(2,1)S(1)}, u32[]{:S(2)}, u32[]{:S(2)}) collective-permute-start(bf16[80,1024]{1,0:T(8,128)(2,1)S(1)} %get-tuple-element.31), channel_id=1, source_target_pairs={{0,2},{1,3},{2,0},{3,1},{4,6},{5,7},{6,4},{7,5},{8,10},{9,11},{10,... | collective-permute-start | bytes 491528 | tf_op jit(solution)/shard_map/ppermute | solution.py:26
  50.5 1.5 %copy-start.6 = (bf16[64,256]{1,0:T(8,128)(2,1)S(1)}, bf16[64,256]{1,0:T(8,128)(2,1)}, u32[]{:S(2)}) copy-start(bf16[64,256]{1,0:T(8,128)(2,1)} %copy-done.5) | copy-start | bytes 98308
  50.5 4.7 %collective-permute-start.15 = (bf16[256,1024]{1,0:T(8,128)(2,1)S(1)}, bf16[256,1024]{1,0:T(8,128)(2,1)}, u32[]{:S(2)}, u32[]{:S(2)}) collective-permute-start(bf16[256,1024]{1,0:T(8,128)(2,1)S(1)} %get-tuple-element.36.refs_3_), channel_id=1, source_target_pairs={{0,1},{1,0},{2,3},{3,2},{4,5},{5,4},{6,7},{7,6},{8,9},{9,8},{10,11... | collective-permute-start | bytes 1572872 | tf_op jit(solution)/shard_map/ppermute | solution.py:26
  50.6 4.6 %collective-permute-start.16 = (bf16[256,1024]{1,0:T(8,128)(2,1)S(1)}, bf16[256,1024]{1,0:T(8,128)(2,1)}, u32[]{:S(2)}, u32[]{:S(2)}) collective-permute-start(bf16[256,1024]{1,0:T(8,128)(2,1)S(1)} %get-tuple-element.37.refs_5_), channel_id=1, source_target_pairs={{0,1},{1,0},{2,3},{3,2},{4,5},{5,4},{6,7},{7,6},{8,9},{9,8},{10,11... | collective-permute-start | bytes 1572872 | tf_op jit(solution)/shard_map/ppermute | solution.py:26
  51.1 4.1 %collective-permute-start.17 = (bf16[256,1024]{1,0:T(8,128)(2,1)S(1)}, bf16[256,1024]{1,0:T(8,128)(2,1)}, u32[]{:S(2)}, u32[]{:S(2)}) collective-permute-start(bf16[256,1024]{1,0:T(8,128)(2,1)S(1)} %get-tuple-element.38.refs_7_), channel_id=1, source_target_pairs={{0,1},{1,0},{2,3},{3,2},{4,5},{5,4},{6,7},{7,6},{8,9},{9,8},{10,11... | collective-permute-start | bytes 1572872 | tf_op jit(solution)/shard_map/ppermute | solution.py:26

commit v6 on v5

--- a/solution.py
+++ b/solution.py
@@ -218,8 +218,8 @@
 
 
 def weight_grad(scale, pre_ref, *refs):
-    blocks = refs[:-8]
-    out_ref, early_ref, routed_ref, rows_ref, wide_ref, follow_ref, sem, sems = refs[-8:]
+    blocks = refs[:-10]
+    out_ref, total_ref, early_ref, routed_ref, rows_ref, wide_ref, follow_ref, sem, sems, out_sems = refs[-10:]
     groups, total, width = early_ref.shape
     total -= SEG
     for i in range(groups):
@@ -252,9 +252,23 @@
     routed = routed_ref[...].astype(BF16)
     for one in loads:
         one.wait()
-    product = lax.dot_general(routed, rows_ref[...], (((0,), (0,)), ((), ())), preferred_element_type=F32)
-    for tap in range(3):
-        out_ref[:, tap * C : (tap + 1) * C] = product[tap * width : (tap + 1) * width, :] * scale
+    half = C // 2
+    stores = []
+    for part in range(2):
+        product = lax.dot_general(
+            routed,
+            rows_ref[:, part * half : (part + 1) * half],
+            (((0,), (0,)), ((), ())),
+            preferred_element_type=F32,
+        )
+        for tap in range(3):
+            start = tap * C + part * half
+            here = pl.ds(start, half)
+            total_ref[:, start : start + half] = product[tap * width : (tap + 1) * width, :] * scale
+            stores.append(pltpu.make_async_copy(total_ref.at[:, here], out_ref.at[:, here], out_sems.at[len(stores)]))
+            stores[-1].start()
+    for one in stores:
+        one.wait()
 
 
 def finish(kept_ref, gated_ref, *refs):
@@ -365,6 +379,7 @@
         [all_pre, *blocks],
         [VMEM] + [ANY if i in LOADED else VMEM for i in range(len(blocks))],
         [
+            pltpu.VMEM((width, 3 * C), F32),
             pltpu.VMEM((groups, all_rows + SEG, width), F32),
             pltpu.VMEM((groups * all_rows, 3 * width), F32),
             pltpu.VMEM((groups * all_rows, C), BF16),
@@ -372,7 +387,9 @@
             pltpu.SMEM((groups, 16, width), jnp.int32),
             pltpu.SemaphoreType.DMA,
             pltpu.SemaphoreType.DMA((len(blocks),)),
+            pltpu.SemaphoreType.DMA((6,)),
         ],
+        out_specs=[ANY],
         room=24,
     )[0]
     return gated_out, grad_in, grad_weight

time: 60.2 us -> 59.9 us (level)
  no operation moved by 1% of the time
where the time goes in v6:
time: 59.9 us; the launch traced here: 59.5 us
  starting transfers between devices  26.8 us (45%)
  waiting for transfers between devices  16 us (27%)
  Pallas kernels  12.4 us (21%)
  local copies, waits for them, and re-layouts  3.52 us (6%)
  between operations  0.8 us (1%)
    ppermute x18, starting transfers between devices, swap(): return lax.ppermute(value, axis, [(i, i ^ distance) for i in range(count)])  18 us
    ppermute x18, waiting for transfers between devices, swap(): return lax.ppermute(value, axis, [(i, i ^ distance) for i in range(count)])  13.8 us
    pallas_call x12, Pallas kernels, call(): pl.pallas_call(run, out_shape=out_shapes, in_specs=[ANY] * len(after) + l...  12.4 us
    all_to_all x2, starting transfers between devices, exchange(): return lax.all_to_all(copies, axis, split_axis=0, concat_axis=0, tiled=True)  8.81 us
    unnamed x14, local copies, waits for them, and re-layouts  2.27 us
    all_to_all x2, waiting for transfers between devices, exchange(): return lax.all_to_all(copies, axis, split_axis=0, concat_axis=0, tiled=True)  2.18 us
    broadcast_in_dim x1, local copies, waits for them, and re-layouts, by_channels(): jnp.broadcast_to(source_seg[None], (peers, 1, seg_count))  1.25 us
  transfers between devices with their start and end apart: 20, of which 7 were waited for; matrix products, arithmetic and copies ran while one was open for 2% of the time, Pallas kernels for 11%

profile of v6, /device:TPU:0, one launch (start us, length us, event | category | flops | bytes accessed | tf_op | source)
XLA Modules:
  0.0 59.5 jit_solution(17048386770145699108)
XLA Ops:
  0.6 4.1 %collective-permute-start.4 = (bf16[64,1024]{1,0:T(8,128)(2,1)}, bf16[64,1024]{1,0:T(8,128)(2,1)S(1)}, u32[]{:S(2)}, u32[]{:S(2)}) collective-permute-start(bf16[64,1024]{1,0:T(8,128)(2,1)} %refs_2_.1), channel_id=1, source_target_pairs={{0,4},{1,5},{2,6},{3,7},{4,0},{5,1},{6,2},{7,3},{8,12},{9,13},{10,... | collective-permute-start | bytes 393224 | tf_op jit(solution)/shard_map/ppermute | solution.py:26
  4.7 1.6 %collective-permute-start.3 = (bf16[64,1024]{1,0:T(8,128)(2,1)}, bf16[64,1024]{1,0:T(8,128)(2,1)S(1)}, u32[]{:S(2)}, u32[]{:S(2)}) collective-permute-start(bf16[64,1024]{1,0:T(8,128)(2,1)} %refs_2_.1), channel_id=1, source_target_pairs={{0,2},{1,3},{2,0},{3,1},{4,6},{5,7},{6,4},{7,5},{8,10},{9,11},{10,... | collective-permute-start | bytes 393224 | tf_op jit(solution)/shard_map/ppermute | solution.py:26
  6.3 0.0 collective-permute-start.5
  6.3 1.2 %broadcast_in_dim.9 = s32[8,1,8]{2,1,0:T(1,128)} broadcast(s32[8]{0:T(128)} %bitcast.5), dimensions={2} | broadcast | bytes 288 | tf_op jit(solution)/shard_map/broadcast_in_dim | solution.py:313
  7.6 5.1 %all-to-all-start = ((s32[8,1,8]{2,1,0:T(1,128)}), s32[8,1,8]{2,1,0:T(1,128)S(1)}, u32[]{:S(2)}, u32[]{:S(2)}) async-start(s32[8,1,8]{2,1,0:T(1,128)} %broadcast_in_dim.9), calls=%async_computation | async-start | bytes 8192 | tf_op jit(solution)/shard_map/all_to_all | solution.py:30
  12.7 0.0 copy-start.2
  12.7 0.8 %copy-done.2 = bf16[64,512]{1,0:T(8,128)(2,1)S(1)} copy-done((bf16[64,512]{1,0:T(8,128)(2,1)S(1)}, bf16[64,512]{1,0:T(8,128)(2,1)}, u32[]{:S(2)}) %copy-start.2) | copy-done | bytes 65560
  13.5 0.0 copy-start
  13.5 0.0 copy-start.1
  13.5 3.9 %collective-permute-start.1 = (bf16[64,256]{1,0:T(8,128)(2,1)S(1)}, bf16[64,256]{1,0:T(8,128)(2,1)S(1)}, u32[]{:S(2)}, u32[]{:S(2)}) collective-permute-start(bf16[64,256]{1,0:T(8,128)(2,1)S(1)} %get-tuple-element.21), channel_id=1, source_target_pairs={{0,6},{1,7},{2,4},{3,5},{4,2},{5,3},{6,0},{7,1},{8,14},{9,15},{10,... | collective-permute-start | bytes 98312 | tf_op jit(solution)/shard_map/ppermute | solution.py:26
  17.4 0.0 collective-permute-start
  17.4 0.0 collective-permute-done.4.refs_4_
  17.4 0.0 copy-done
  17.4 0.1 collective-permute-start.2
  17.5 0.6 %all-to-all-done = s32[8,1,8]{2,1,0:T(1,128)S(1)} async-done(((s32[8,1,8]{2,1,0:T(1,128)}), s32[8,1,8]{2,1,0:T(1,128)S(1)}, u32[]{:S(2)}, u32[]{:S(2)}) %all-to-all-start) | async-done | bytes 288 | tf_op jit(solution)/shard_map/all_to_all | solution.py:30
  18.1 0.0 collective-permute-done.3.refs_3_
  18.1 0.0 collective-permute-done.5.refs_5_
  18.1 0.0 copy-done.1
  18.2 0.1 collective-permute-start.6
  18.3 1.5 %collective-permute-done.2.refs_1_ = bf16[128,3072]{1,0:T(8,128)(2,1)S(1)} collective-permute-done((bf16[128,3072]{1,0:T(8,128)(2,1)S(1)}, bf16[128,3072]{1,0:T(8,128)(2,1)S(1)}, u32[]{:S(2)}, u32[]{:S(2)}) %collective-permute-start.2) | collective-permute-done | bytes 786464 | tf_op jit(solution)/shard_map/ppermute | solution.py:26
  19.8 0.1 shard_map.68.refs_3_.refs_2_
  19.9 0.0 copy-start.3
  19.9 0.0 collective-permute-done.1.refs_1_.refs_4_
  19.9 1.4 %collective-permute-done.refs_0_.refs_3_ = bf16[64,256]{1,0:T(8,128)(2,1)S(1)} collective-permute-done((bf16[64,256]{1,0:T(8,128)(2,1)S(1)}, bf16[64,256]{1,0:T(8,128)(2,1)S(1)}, u32[]{:S(2)}, u32[]{:S(2)}) %collective-permute-start) | collective-permute-done | bytes 32800 | tf_op jit(solution)/shard_map/ppermute | solution.py:26
  21.3 0.0 collective-permute-done.6.refs_5_.refs_2_
  21.3 1.6 %shard_map.70 = (f32[256,256]{1,0:T(8,128)S(1)}, bf16[320,256]{1,0:T(8,128)(2,1)S(1)}) custom-call(bf16[64,256]{1,0:T(8,128)(2,1)S(1)} %collective-permute-done.refs_0_.refs_3_, bf16[64,256]{1,0:T(8,128)(2,1)S(1)} %collective-permute-done.1.refs_1_.refs_4_, s32[8,8]{1,0:T(8,128)S(1)} %bitcast.3, bf16[768,1024]{1,0:T(8,128)(2,1)S(1)} %shard_map.68.refs_3_.refs_2_, ...), custom_call_target="tpu_custom_call" | custom-call | flops 10000000000 | tf_op jit(solution)/shard_map/pallas_call | solution.py:37
  23.0 0.5 collective-permute-start.7
  23.5 2.5 %collective-permute-start.11 = (bf16[256,1024]{1,0:T(8,128)(2,1)S(1)}, bf16[256,1024]{1,0:T(8,128)(2,1)S(1)}, u32[]{:S(2)}, u32[]{:S(2)}) collective-permute-start(bf16[256,1024]{1,0:T(8,128)(2,1)S(1)} %shard_map.69.refs_4_.refs_1_), channel_id=1, source_target_pairs={{0,24},{8,16},{16,8},{24,0},{1,25},{9,17},{17,9},{25,1},{2,26},{10... | collective-permute-start | bytes 1572872 | tf_op jit(solution)/shard_map/ppermute | solution.py:26
  25.9 0.5 collective-permute-start.10
  26.4 0.5 collective-permute-start.9
  26.9 5.9 %collective-permute-done.7.refs_1_ = bf16[320,256]{1,0:T(8,128)(2,1)S(1)} collective-permute-done((bf16[320,256]{1,0:T(8,128)(2,1)S(1)}, bf16[320,256]{1,0:T(8,128)(2,1)S(1)}, u32[]{:S(2)}, u32[]{:S(2)}) %collective-permute-start.7) | collective-permute-done | bytes 163872 | tf_op jit(solution)/shard_map/ppermute | solution.py:26
  32.9 0.1 shard_map.71
  33.0 0.0 copy-start.5
  33.0 0.1 collective-permute-start.8
  33.1 1.6 %shard_map.72 = (s32[65]{0:T(128)S(1)}, bf16[16,128]{1,0:T(8,128)(2,1)S(1)}) custom-call(bf16[320,256]{1,0:T(8,128)(2,1)S(1)} %get-tuple-element.24.refs_0_, s32[8,8]{1,0:T(8,128)S(1)} %bitcast.4), custom_call_target="tpu_custom_call" | custom-call | flops 10000000000 | tf_op jit(solution)/shard_map/pallas_call | solution.py:37
  34.6 0.0 copy-done.5
  34.7 0.0 collective-permute-done.8.refs_1_.refs_2_
  34.7 0.0 copy-done.3
  34.7 1.7 %shard_map.74 = (bf16[80,1024]{1,0:T(8,128)(2,1)S(1)}, bf16[64,1024]{1,0:T(8,128)(2,1)}, bf16[64,1024]{1,0:T(8,128)(2,1)}, bf16[64,768]{1,0:T(8,128)(2,1)S(1)}) custom-call(s32[65]{0:T(128)S(1)} %get-tuple-element.27.refs_0_, bf16[256,256]{1,0:T(8,128)(2,1)S(1)} %get-tuple-element.25.refs_0_.refs_1_, ...), custom_call_target="tpu_custom_call" | custom-call | flops 10000000000 | tf_op jit(solution)/shard_map/pallas_call | solution.py:37
  36.4 0.0 collective-permute-start.13
  36.4 2.1 %collective-permute-start.14 = (bf16[64,1024]{1,0:T(8,128)(2,1)}, bf16[64,1024]{1,0:T(8,128)(2,1)}, u32[]{:S(2)}, u32[]{:S(2)}) collective-permute-start(bf16[64,1024]{1,0:T(8,128)(2,1)} %get-tuple-element.33), channel_id=1, source_target_pairs={{0,6},{1,7},{2,4},{3,5},{4,2},{5,3},{6,0},{7,1},{8,14},{9,15},{10,... | collective-permute-start | bytes 393224 | tf_op jit(solution)/shard_map/ppermute | solution.py:26
  38.5 0.9 %shard_map.73.refs_0_ = bf16[4,528,128]{2,1,0:T(8,128)(2,1)} custom-call(bf16[256,256]{1,0:T(8,128)(2,1)S(1)} %get-tuple-element.25.refs_0_.refs_1_, bf16[256,256]{1,0:T(8,128)(2,1)S(1)} %collective-permute-done.8.refs_1_.refs_2_, bf16[16,128]{1,0:T(8,128)(2,1)S(1)} %get-tuple-element.26.refs_2_), custom_call_target="tpu_custom_call" | custom-call | flops 10000000000 | tf_op jit(solution)/shard_map/pallas_call | solution.py:37
  39.4 3.7 %all-to-all-start.1 = ((bf16[4,528,128]{2,1,0:T(8,128)(2,1)}), bf16[4,528,128]{2,1,0:T(8,128)(2,1)S(1)}, u32[]{:S(2)}, u32[]{:S(2)}) async-start(bf16[4,528,128]{2,1,0:T(8,128)(2,1)} %shard_map.73.refs_0_), calls=%async_computation.1 | async-start | bytes 1081344 | tf_op jit(solution)/shard_map/all_to_all | solution.py:30
  43.1 0.0 copy-start.4
  43.1 1.4 %copy-done.4 = bf16[768,1024]{1,0:T(8,128)(2,1)S(1)} copy-done((bf16[768,1024]{1,0:T(8,128)(2,1)S(1)}, bf16[768,1024]{1,0:T(8,128)(2,1)}, u32[]{:S(2)}) %copy-start.4) | copy-done | bytes 1572888
  44.5 0.4 shard_map.75.refs_0_.refs_1_
  44.9 0.0 collective-permute-done.11.refs_3_.refs_2_
  44.9 1.5 %collective-permute-start.12 = (bf16[80,1024]{1,0:T(8,128)(2,1)S(1)}, bf16[80,1024]{1,0:T(8,128)(2,1)S(1)}, u32[]{:S(2)}, u32[]{:S(2)}) collective-permute-start(bf16[80,1024]{1,0:T(8,128)(2,1)S(1)} %get-tuple-element.31), channel_id=1, source_target_pairs={{0,2},{1,3},{2,0},{3,1},{4,6},{5,7},{6,4},{7,5},{8,10},{9,11},{10,... | collective-permute-start | bytes 491528 | tf_op jit(solution)/shard_map/ppermute | solution.py:26
  46.4 4.1 %collective-permute-done.10.refs_2_.refs_1_ = bf16[256,1024]{1,0:T(8,128)(2,1)S(1)} collective-permute-done((bf16[256,1024]{1,0:T(8,128)(2,1)S(1)}, bf16[256,1024]{1,0:T(8,128)(2,1)S(1)}, u32[]{:S(2)}, u32[]{:S(2)}) %collective-permute-start.10) | collective-permute-done | bytes 524320 | tf_op jit(solution)/shard_map/ppermute | solution.py:26
  50.5 0.0 collective-permute-done.9.refs_1_.refs_0_
  50.5 0.0 copy-start.6
  50.5 0.1 collective-permute-start.15
  50.6 0.5 collective-permute-start.16
  51.1 0.0 collective-permute-done.13.refs_4_
  51.1 0.1 collective-permute-start.17
  51.2 0.0 collective-permute-done.14.refs_5_
  51.2 0.8 %collective-permute-done.12.refs_3_ = bf16[80,1024]{1,0:T(8,128)(2,1)S(1)} collective-permute-done((bf16[80,1024]{1,0:T(8,128)(2,1)S(1)}, bf16[80,1024]{1,0:T(8,128)(2,1)S(1)}, u32[]{:S(2)}, u32[]{:S(2)}) %collective-permute-start.12) | collective-permute-done | bytes 163872 | tf_op jit(solution)/shard_map/ppermute | solution.py:26
  52.0 0.0 copy-done.6
  52.0 1.6 %shard_map.77 = (bf16[64,1024]{1,0:T(8,128)(2,1)}, bf16[64,512]{1,0:T(8,128)(2,1)}) custom-call(f32[8,128]{1,0:T(8,128)S(1)} %shard_map.76.refs_0_.refs_3_, f32[64,1024]{1,0:T(8,128)S(1)} %shard_map.75.refs_0_.refs_1_, bf16[64,256]{1,0:T(8,128)(2,1)S(1)} %copy-done.6, bf16[80,1024]{1,0:T(8,128)(2,1)S(1)} %collective-permute-done.12.refs_3_, ...), custom_call_target="tpu_custom_call" | custom-call | flops 10000000000 | tf_op jit(solution)/shard_map/pallas_call | solution.py:37
  53.6 1.5 %all-to-all-done.1.refs_0_ = bf16[4,528,128]{2,1,0:T(8,128)(2,1)S(1)} async-done(((bf16[4,528,128]{2,1,0:T(8,128)(2,1)}), bf16[4,528,128]{2,1,0:T(8,128)(2,1)S(1)}, u32[]{:S(2)}, u32[]{:S(2)}) %all-to-all-start.1) | async-done | bytes 540704 | tf_op jit(solution)/shard_map/all_to_all | solution.py:30
  55.2 0.0 collective-permute-done.15.refs_4_
  55.2 0.0 collective-permute-done.16.refs_6_
  55.2 0.0 collective-permute-done.17.refs_8_
  55.2 4.3 %shard_map.79 = f32[128,3072]{1,0:T(8,128)} custom-call(bf16[4,528,128]{2,1,0:T(8,128)(2,1)S(1)} %all-to-all-done.1.refs_0_, bf16[256,1024]{1,0:T(8,128)(2,1)S(1)} %shard_map.69.refs_4_.refs_1_, bf16[256,1024]{1,0:T(8,128)(2,1)S(1)} %collective-permute-done.6.refs_5_.refs_2_, bf16[256,1024]{1,0:T(8,128)(2,1)S(1)} %get-tuple-element.36.refs_3_, ...), custom_call_target="tpu_custom_call" | custom-call | flops 10000000000 | tf_op jit(solution)/shard_map/pallas_call | solution.py:37
  (4 shorter events, 0.1 us)
Async XLA Ops:
  0.6 16.8 %collective-permute-start.4 = (bf16[64,1024]{1,0:T(8,128)(2,1)}, bf16[64,1024]{1,0:T(8,128)(2,1)S(1)}, u32[]{:S(2)}, u32[]{:S(2)}) collective-permute-start(bf16[64,1024]{1,0:T(8,128)(2,1)} %refs_2_.1), channel_id=1, source_target_pairs={{0,4},{1,5},{2,6},{3,7},{4,0},{5,1},{6,2},{7,3},{8,12},{9,13},{10,... | collective-permute-start | bytes 393224 | tf_op jit(solution)/shard_map/ppermute | solution.py:26
  4.7 13.4 %collective-permute-start.3 = (bf16[64,1024]{1,0:T(8,128)(2,1)}, bf16[64,1024]{1,0:T(8,128)(2,1)S(1)}, u32[]{:S(2)}, u32[]{:S(2)}) collective-permute-start(bf16[64,1024]{1,0:T(8,128)(2,1)} %refs_2_.1), channel_id=1, source_target_pairs={{0,2},{1,3},{2,0},{3,1},{4,6},{5,7},{6,4},{7,5},{8,10},{9,11},{10,... | collective-permute-start | bytes 393224 | tf_op jit(solution)/shard_map/ppermute | solution.py:26
  6.3 11.8 %collective-permute-start.5 = (bf16[64,1024]{1,0:T(8,128)(2,1)}, bf16[64,1024]{1,0:T(8,128)(2,1)S(1)}, u32[]{:S(2)}, u32[]{:S(2)}) collective-permute-start(bf16[64,1024]{1,0:T(8,128)(2,1)} %refs_2_.1), channel_id=1, source_target_pairs={{0,6},{1,7},{2,4},{3,5},{4,2},{5,3},{6,0},{7,1},{8,14},{9,15},{10,... | collective-permute-start | bytes 393224 | tf_op jit(solution)/shard_map/ppermute | solution.py:26
  7.6 10.6 %all-to-all-start = ((s32[8,1,8]{2,1,0:T(1,128)}), s32[8,1,8]{2,1,0:T(1,128)S(1)}, u32[]{:S(2)}, u32[]{:S(2)}) async-start(s32[8,1,8]{2,1,0:T(1,128)} %broadcast_in_dim.9), calls=%async_computation | async-start | bytes 8192 | tf_op jit(solution)/shard_map/all_to_all | solution.py:30
  12.7 0.8 %copy-start.2 = (bf16[64,512]{1,0:T(8,128)(2,1)S(1)}, bf16[64,512]{1,0:T(8,128)(2,1)}, u32[]{:S(2)}) copy-start(bf16[64,512]{1,0:T(8,128)(2,1)} %refs_0_.2) | copy-start | bytes 196612
  13.5 3.9 %copy-start = (bf16[128,3072]{1,0:T(8,128)(2,1)S(1)}, bf16[128,3072]{1,0:T(8,128)(2,1)}, u32[]{:S(2)}) copy-start(bf16[128,3072]{1,0:T(8,128)(2,1)} %refs_0_.3) | copy-start | bytes 2359300
  13.5 4.7 %copy-start.1 = (bf16[64,1024]{1,0:T(8,128)(2,1)S(1)}, bf16[64,1024]{1,0:T(8,128)(2,1)}, u32[]{:S(2)}) copy-start(bf16[64,1024]{1,0:T(8,128)(2,1)} %refs_2_.1) | copy-start | bytes 393220
  13.5 6.4 %collective-permute-start.1 = (bf16[64,256]{1,0:T(8,128)(2,1)S(1)}, bf16[64,256]{1,0:T(8,128)(2,1)S(1)}, u32[]{:S(2)}, u32[]{:S(2)}) collective-permute-start(bf16[64,256]{1,0:T(8,128)(2,1)S(1)} %get-tuple-element.21), channel_id=1, source_target_pairs={{0,6},{1,7},{2,4},{3,5},{4,2},{5,3},{6,0},{7,1},{8,14},{9,15},{10,... | collective-permute-start | bytes 98312 | tf_op jit(solution)/shard_map/ppermute | solution.py:26
  17.4 3.9 %collective-permute-start = (bf16[64,256]{1,0:T(8,128)(2,1)S(1)}, bf16[64,256]{1,0:T(8,128)(2,1)S(1)}, u32[]{:S(2)}, u32[]{:S(2)}) collective-permute-start(bf16[64,256]{1,0:T(8,128)(2,1)S(1)} %get-tuple-element.21), channel_id=1, source_target_pairs={{0,2},{1,3},{2,0},{3,1},{4,6},{5,7},{6,4},{7,5},{8,10},{9,11},{10,... | collective-permute-start | bytes 98312 | tf_op jit(solution)/shard_map/ppermute | solution.py:26
  17.4 2.4 %collective-permute-start.2 = (bf16[128,3072]{1,0:T(8,128)(2,1)S(1)}, bf16[128,3072]{1,0:T(8,128)(2,1)S(1)}, u32[]{:S(2)}, u32[]{:S(2)}) collective-permute-start(bf16[128,3072]{1,0:T(8,128)(2,1)S(1)} %copy-done), channel_id=1, source_target_pairs={{0,1},{1,0},{2,3},{3,2},{4,5},{5,4},{6,7},{7,6},{8,9},{9,8},{10,11... | collective-permute-start | bytes 2359304 | tf_op jit(solution)/shard_map/ppermute | solution.py:26
  18.2 3.1 %collective-permute-start.6 = (bf16[256,1024]{1,0:T(8,128)(2,1)S(1)}, bf16[256,1024]{1,0:T(8,128)(2,1)S(1)}, u32[]{:S(2)}, u32[]{:S(2)}) collective-permute-start(bf16[256,1024]{1,0:T(8,128)(2,1)S(1)} %shard_map.69.refs_4_.refs_1_), channel_id=1, source_target_pairs={{0,1},{1,0},{2,3},{3,2},{4,5},{5,4},{6,7},{7,6},{8,9},{9,8},{10,11... | collective-permute-start | bytes 1572872 | tf_op jit(solution)/shard_map/ppermute | solution.py:26
  19.9 14.8 %copy-start.3 = (bf16[768,1024]{1,0:T(8,128)(2,1)}, bf16[768,1024]{1,0:T(8,128)(2,1)S(1)}, u32[]{:S(2)}) copy-start(bf16[768,1024]{1,0:T(8,128)(2,1)S(1)} %shard_map.68.refs_3_.refs_2_) | copy-start | bytes 4718596
  23.0 9.9 %collective-permute-start.7 = (bf16[320,256]{1,0:T(8,128)(2,1)S(1)}, bf16[320,256]{1,0:T(8,128)(2,1)S(1)}, u32[]{:S(2)}, u32[]{:S(2)}) collective-permute-start(bf16[320,256]{1,0:T(8,128)(2,1)S(1)} %get-tuple-element.24.refs_0_), channel_id=1, source_target_pairs={{0,4},{1,5},{2,6},{3,7},{4,0},{5,1},{6,2},{7,3},{8,12},{9,13},{10,... | collective-permute-start | bytes 491528 | tf_op jit(solution)/shard_map/ppermute | solution.py:26
  23.5 21.4 %collective-permute-start.11 = (bf16[256,1024]{1,0:T(8,128)(2,1)S(1)}, bf16[256,1024]{1,0:T(8,128)(2,1)S(1)}, u32[]{:S(2)}, u32[]{:S(2)}) collective-permute-start(bf16[256,1024]{1,0:T(8,128)(2,1)S(1)} %shard_map.69.refs_4_.refs_1_), channel_id=1, source_target_pairs={{0,24},{8,16},{16,8},{24,0},{1,25},{9,17},{17,9},{25,1},{2,26},{10... | collective-permute-start | bytes 1572872 | tf_op jit(solution)/shard_map/ppermute | solution.py:26
  25.9 24.6 %collective-permute-start.10 = (bf16[256,1024]{1,0:T(8,128)(2,1)S(1)}, bf16[256,1024]{1,0:T(8,128)(2,1)S(1)}, u32[]{:S(2)}, u32[]{:S(2)}) collective-permute-start(bf16[256,1024]{1,0:T(8,128)(2,1)S(1)} %shard_map.69.refs_4_.refs_1_), channel_id=1, source_target_pairs={{0,16},{8,24},{16,0},{24,8},{1,17},{9,25},{17,1},{25,9},{2,18},{10... | collective-permute-start | bytes 1572872 | tf_op jit(solution)/shard_map/ppermute | solution.py:26
  26.4 24.1 %collective-permute-start.9 = (bf16[256,1024]{1,0:T(8,128)(2,1)S(1)}, bf16[256,1024]{1,0:T(8,128)(2,1)S(1)}, u32[]{:S(2)}, u32[]{:S(2)}) collective-permute-start(bf16[256,1024]{1,0:T(8,128)(2,1)S(1)} %shard_map.69.refs_4_.refs_1_), channel_id=1, source_target_pairs={{0,8},{8,0},{16,24},{24,16},{1,9},{9,1},{17,25},{25,17},{2,10},{10... | collective-permute-start | bytes 1572872 | tf_op jit(solution)/shard_map/ppermute | solution.py:26
  33.0 1.7 %copy-start.5 = (bf16[64,256]{1,0:T(8,128)(2,1)}, bf16[64,256]{1,0:T(8,128)(2,1)S(1)}, u32[]{:S(2)}) copy-start(bf16[64,256]{1,0:T(8,128)(2,1)S(1)} %get-tuple-element.30.refs_2_) | copy-start | bytes 98308
  33.0 1.7 %collective-permute-start.8 = (bf16[256,256]{1,0:T(8,128)(2,1)S(1)}, bf16[256,256]{1,0:T(8,128)(2,1)S(1)}, u32[]{:S(2)}, u32[]{:S(2)}) collective-permute-start(bf16[256,256]{1,0:T(8,128)(2,1)S(1)} %get-tuple-element.25.refs_0_.refs_1_), channel_id=1, source_target_pairs={{0,1},{1,0},{2,3},{3,2},{4,5},{5,4},{6,7},{7,6},{8,9},{9,8},{10,11... | collective-permute-start | bytes 393224 | tf_op jit(solution)/shard_map/ppermute | solution.py:26
  36.4 14.7 %collective-permute-start.13 = (bf16[64,1024]{1,0:T(8,128)(2,1)}, bf16[64,1024]{1,0:T(8,128)(2,1)S(1)}, u32[]{:S(2)}, u32[]{:S(2)}) collective-permute-start(bf16[64,1024]{1,0:T(8,128)(2,1)} %get-tuple-element.32), channel_id=1, source_target_pairs={{0,4},{1,5},{2,6},{3,7},{4,0},{5,1},{6,2},{7,3},{8,12},{9,13},{10,... | collective-permute-start | bytes 393224 | tf_op jit(solution)/shard_map/ppermute | solution.py:26
  36.4 14.7 %collective-permute-start.14 = (bf16[64,1024]{1,0:T(8,128)(2,1)}, bf16[64,1024]{1,0:T(8,128)(2,1)}, u32[]{:S(2)}, u32[]{:S(2)}) collective-permute-start(bf16[64,1024]{1,0:T(8,128)(2,1)} %get-tuple-element.33), channel_id=1, source_target_pairs={{0,6},{1,7},{2,4},{3,5},{4,2},{5,3},{6,0},{7,1},{8,14},{9,15},{10,... | collective-permute-start | bytes 393224 | tf_op jit(solution)/shard_map/ppermute | solution.py:26
  39.4 15.8 %all-to-all-start.1 = ((bf16[4,528,128]{2,1,0:T(8,128)(2,1)}), bf16[4,528,128]{2,1,0:T(8,128)(2,1)S(1)}, u32[]{:S(2)}, u32[]{:S(2)}) async-start(bf16[4,528,128]{2,1,0:T(8,128)(2,1)} %shard_map.73.refs_0_), calls=%async_computation.1 | async-start | bytes 1081344 | tf_op jit(solution)/shard_map/all_to_all | solution.py:30
  43.1 1.4 %copy-start.4 = (bf16[768,1024]{1,0:T(8,128)(2,1)S(1)}, bf16[768,1024]{1,0:T(8,128)(2,1)}, u32[]{:S(2)}) copy-start(bf16[768,1024]{1,0:T(8,128)(2,1)} %copy-done.3) | copy-start | bytes 4718596
  44.9 7.1 %collective-permute-start.12 = (bf16[80,1024]{1,0:T(8,128)(2,1)S(1)}, bf16[80,1024]{1,0:T(8,128)(2,1)S(1)}, u32[]{:S(2)}, u32[]{:S(2)}) collective-permute-start(bf16[80,1024]{1,0:T(8,128)(2,1)S(1)} %get-tuple-element.31), channel_id=1, source_target_pairs={{0,2},{1,3},{2,0},{3,1},{4,6},{5,7},{6,4},{7,5},{8,10},{9,11},{10,... | collective-permute-start | bytes 491528 | tf_op jit(solution)/shard_map/ppermute | solution.py:26
  50.5 1.5 %copy-start.6 = (bf16[64,256]{1,0:T(8,128)(2,1)S(1)}, bf16[64,256]{1,0:T(8,128)(2,1)}, u32[]{:S(2)}) copy-start(bf16[64,256]{1,0:T(8,128)(2,1)} %copy-done.5) | copy-start | bytes 98308
  50.5 4.7 %collective-permute-start.15 = (bf16[256,1024]{1,0:T(8,128)(2,1)S(1)}, bf16[256,1024]{1,0:T(8,128)(2,1)}, u32[]{:S(2)}, u32[]{:S(2)}) collective-permute-start(bf16[256,1024]{1,0:T(8,128)(2,1)S(1)} %get-tuple-element.36.refs_3_), channel_id=1, source_target_pairs={{0,1},{1,0},{2,3},{3,2},{4,5},{5,4},{6,7},{7,6},{8,9},{9,8},{10,11... | collective-permute-start | bytes 1572872 | tf_op jit(solution)/shard_map/ppermute | solution.py:26
  50.6 4.6 %collective-permute-start.16 = (bf16[256,1024]{1,0:T(8,128)(2,1)S(1)}, bf16[256,1024]{1,0:T(8,128)(2,1)}, u32[]{:S(2)}, u32[]{:S(2)}) collective-permute-start(bf16[256,1024]{1,0:T(8,128)(2,1)S(1)} %get-tuple-element.37.refs_5_), channel_id=1, source_target_pairs={{0,1},{1,0},{2,3},{3,2},{4,5},{5,4},{6,7},{7,6},{8,9},{9,8},{10,11... | collective-permute-start | bytes 1572872 | tf_op jit(solution)/shard_map/ppermute | solution.py:26
  51.1 4.1 %collective-permute-start.17 = (bf16[256,1024]{1,0:T(8,128)(2,1)S(1)}, bf16[256,1024]{1,0:T(8,128)(2,1)}, u32[]{:S(2)}, u32[]{:S(2)}) collective-permute-start(bf16[256,1024]{1,0:T(8,128)(2,1)S(1)} %get-tuple-element.38.refs_7_), channel_id=1, source_target_pairs={{0,1},{1,0},{2,3},{3,2},{4,5},{5,4},{6,7},{7,6},{8,9},{9,8},{10,11... | collective-permute-start | bytes 1572872 | tf_op jit(solution)/shard_map/ppermute | solution.py:26
